TPU v7x, 256 devices: a whole 4x4x8 slice. The times are simulated.
256 devices in a mesh: row: 4 (over y), col: 16 (over z, core), layer: 4 (over x).
Axes of the slice: x: 4, y: 4, z: 8, core: 2. Of those that a mesh axis runs over, the one named last changes fastest.
Arguments:
- matrix: bfloat16 [8192, 8192], P('row', 'col'), may hold values from -1.1953125 to 1.1953125
- pattern: int32 [256, 256], P('row', 'col'), may hold values from 0 to 1, as said below
- keep: int32 [256, 256], P('row', ('col', 'layer')), may hold values 0 or 1
Outputs:
- square: bfloat16 [8192, 8192], P('row', ('col', 'layer'))
Inputs may be any that keep to these rules, and one draw needn't show every extreme that they name: `pattern`: every diagonal atom block is stored; blocks near the diagonal are stored more often than far ones.
All inputs are finite; a program needn't handle non-finite values. No bound on the sum of `keep` on one device may be relied on, other than what follows from the above.
Results may differ from a plain program's by a relative error of at most 0.012.
Values may be sent and summed in bfloat16 or wider, within the bound.
No kernel may reach another device: no remote copies, remote signals or barrier semaphores. Data moves between devices by JAX's collectives and lax.ppermute only.
A program may use at most 128 MiB of HBM per device.

v0:
```python
import jax
import jax.numpy as jnp
from jax import lax
from jax.sharding import PartitionSpec as P

BLOCK = 32


def blockwise(values, mask):
    rows, cols = mask.shape
    shaped = values.reshape(rows, BLOCK, cols, BLOCK)
    kept = jnp.where(mask[:, None, :, None] > 0, shaped, jnp.zeros((), values.dtype))
    return kept.reshape(rows * BLOCK, cols * BLOCK)


def on_device(matrix, pattern, keep):
    rows_here, cols_here = matrix.shape
    n_row = lax.axis_size("row")
    n_col = lax.axis_size("col")
    n_layer = lax.axis_size("layer")
    layer = lax.axis_index("layer")
    sparse = blockwise(matrix, pattern)
    width = cols_here // n_layer
    piece = rows_here // (n_col * n_layer)
    left_local = lax.dynamic_slice_in_dim(
        sparse.reshape(rows_here, n_row, n_layer, piece), layer, 1, 2
    )
    left_local = left_local.reshape(rows_here, n_row * piece)
    right_local = lax.dynamic_slice_in_dim(
        sparse.reshape(n_col, n_layer, piece, cols_here), layer, 1, 1
    )
    right_local = right_local.reshape(n_col * piece, cols_here)
    right_panel = lax.all_gather(right_local, "row", axis=0, tiled=True)
    partial_sum = jnp.dot(
        lax.all_gather(left_local, "col", axis=1, tiled=True),
        right_panel,
        preferred_element_type=jnp.float32,
    )
    rounded_part = partial_sum.astype(jnp.bfloat16)
    totals = lax.psum(rounded_part, "layer").astype(jnp.float32)
    summed = lax.dynamic_slice_in_dim(totals, layer * width, width, 1)
    return blockwise(summed, keep).astype(jnp.bfloat16)


def solution(mesh):
    in_specs = (P("row", "col"), P("row", "col"), P("row", ("col", "layer")))
    out_specs = P("row", ("col", "layer"))
    return jax.shard_map(
        on_device, mesh=mesh, in_specs=in_specs, out_specs=out_specs, check_vma=False
    )
```

profile of v0, /device:TPU:1, one launch (start us, length us, event | category | flops | bytes accessed | tf_op | source)
XLA Modules:
  0.0 185.9 jit_solution(15587477300967587054)
XLA Ops:
  6.5 0.7 broadcast_compare_fusion
  7.2 0.1 copy.8
  7.3 0.2 broadcast_in_dim.46
  7.6 0.3 broadcast_in_dim.47
  7.8 0.1 constant_dynamic-slice_fusion
  7.9 1.9 %dynamic-slice_select_fusion = bf16[16,1,32,512]{3,2,1,0:T(8,128)(2,1)} fusion(bf16[16,4,32,512]{3,2,1,0:T(8,128)(2,1)} %bitcast.12, s32[]{:T(128)S(6)} %select_n.21, pred[16,1,512]{2,1,0:T(4,128)(4,1)S(1)} %constant_dynamic-slice_fusion), kind=kLoop, calls=%fused_computation.2 | loop fusion | flops 262144 | bytes 1056772 | tf_op jit(solution)/shard_map/jit(_where)/select_n | solution.py:12
  9.8 0.0 all-gather.5.cloned.1.call-update
  9.8 0.0 all-gather.3.cloned.1.call-start
  9.9 2.9 %copy.7 = bf16[2048,512]{0,1:T(8,128)(2,1)S(1)} copy(bf16[2048,512]{1,0:T(8,128)(2,1)} %param.3) | data formatting | bytes 4194304 | tf_op args[0]
  12.8 0.2 broadcast_in_dim.42
  13.0 0.3 broadcast_in_dim.43
  13.3 0.1 constant_dynamic-slice_fusion.1
  13.4 0.9 dynamic-slice_select_fusion.1
  14.2 0.0 all-gather.3.cloned.1.call-update
  14.3 0.0 all-reduce.2.cloned.1.call-start
  14.3 32.9 %all-gather.5.cloned.1.call-done = bf16[2048,512]{1,0:T(8,128)(2,1)} async-done(((bf16[512,512]{1,0:T(8,128)(2,1)}), bf16[2048,512]{1,0:T(8,128)(2,1)}) %all-gather.5.cloned.1.call-update) | async-done | bytes 2097168 | tf_op jit(solution)/shard_map/all_gather | solution.py:33
  47.2 58.2 %all-gather.3.cloned.1.call-done = bf16[2048,2048]{0,1:T(8,128)(2,1)} async-done(((bf16[2048,128]{0,1:T(8,128)(2,1)}), bf16[2048,2048]{0,1:T(8,128)(2,1)}) %all-gather.3.cloned.1.call-update) | async-done | bytes 8388624 | tf_op jit(solution)/shard_map/all_gather | solution.py:35
  105.4 9.9 %convolution_convert_fusion = bf16[2048,512]{1,0:T(8,128)(2,1)} fusion(bf16[2048,2048]{0,1:T(8,128)(2,1)} %all-gather.3.cloned.1.call-done, bf16[2048,512]{1,0:T(8,128)(2,1)} %all-gather.5.cloned.1.call-done), kind=kOutput, calls=%fused_computation | convolution fusion | flops 4296015872 | bytes 12582912 | tf_op jit(solution)/shard_map/dot_general | solution.py:34
  115.3 0.7 copy-done
  116.0 0.3 broadcast_in_dim.40
  116.3 2.4 %broadcast_in_dim.41 = pred[2048,128]{0,1:T(8,128)(4,1)S(1)} reshape(pred[64,32,4,32]{1,0,3,2:T(8,128)(4,1)S(1)} %broadcast_in_dim.40) | data formatting | bytes 524288 | tf_op jit(solution)/shard_map/jit(_where)/broadcast_in_dim | solution.py:12
  118.8 0.4 copy.9
  119.2 58.2 %all-reduce.2.cloned.1.call-done = bf16[2048,512]{1,0:T(8,128)(2,1)} async-done(((bf16[2048,512]{1,0:T(8,128)(2,1)}), bf16[2048,512]{1,0:T(8,128)(2,1)}) %all-reduce.2.cloned.1.call-update) | async-done | bytes 2097168 | tf_op jit(solution)/shard_map/psum | solution.py:40
  177.4 2.0 %select_convert_fusion = bf16[2048,128]{1,0:T(8,128)(2,1)} fusion(pred[2048,128]{1,0:T(8,128)(4,1)S(1)} %copy.9, bf16[2048,512]{1,0:T(8,128)(2,1)} %all-reduce.2.cloned.1.call-done, s32[]{:T(128)S(6)} %select_n.23), kind=kLoop, calls=%fused_computation.1 | loop fusion | flops 786432 | bytes 1310724 | tf_op jit(solution)/shard_map/convert_element_type | solution.py:42
  (4 shorter events, 0.0 us)
Async XLA Ops:
  6.5 40.7 %all-gather.5.cloned.1.call-start = ((), (), s32[]{:S(2)}) async-start(), calls=%async_computation.1 | async-start | bytes 2621440 | tf_op jit(solution)/shard_map/all_gather | solution.py:33
  9.8 95.6 %all-gather.3.cloned.1.call-start = ((), (), s32[]{:S(2)}) async-start(), calls=%async_computation | async-start | bytes 8912896 | tf_op jit(solution)/shard_map/all_gather | solution.py:35
  14.3 163.1 %all-reduce.2.cloned.1.call-start = ((), (), s32[]{:S(2)}) async-start(), calls=%async_computation.2 | async-start | bytes 4194304 | tf_op jit(solution)/shard_map/psum | solution.py:40
  115.3 0.7 copy-start
Sparse Core Ops, SparseCore 0:
  10.0 37.2 all-gather.4
  49.0 56.3 all-gather.2
  115.4 61.9 all-reduce.1
where the time goes:
time: 186 us
  waiting for transfers between devices  149 us (80%)
  between operations  13.2 us (7%)
  matrix products  9.87 us (5%)
  local copies, waits for them, and re-layouts  7.95 us (4%)
  other arithmetic  5.51 us (3%)
    all_gather x1, waiting for transfers between devices, on_device(): lax.all_gather(left_local, 'col', axis=1, tiled=True)  58.2 us
    psum x1, waiting for transfers between devices, on_device(): totals = lax.psum(rounded_part, 'layer').astype(jnp.float32)  58.2 us
    all_gather x1, waiting for transfers between devices, on_device(): right_panel = lax.all_gather(right_local, 'row', axis=0, tiled=True)  32.9 us
    dot_general x1, matrix products, on_device(): jnp.dot(lax.all_gather(left_local, 'col', axis=1, tiled=True), right_pane...  9.87 us
    broadcast_in_dim x7, local copies, waits for them, and re-layouts, blockwise(): jnp.where(mask[:, None, :, None] > 0, shaped, jnp.zeros((), values.dtype))  4.15 us
  transfers between devices with their start and end apart: 3, of which 3 were waited for; matrix products, arithmetic and copies ran while one was open for 4% of the time, Pallas kernels for 0%

commit v1 on v0

v1 whole, which is shorter than its diff:
```python
import functools

import jax
import jax.numpy as jnp
from jax import lax
from jax.experimental import pallas as pl
from jax.experimental.pallas import tpu as pltpu
from jax.sharding import PartitionSpec as P

BLOCK = 32
F32 = jnp.float32
BF16 = jnp.bfloat16
HBM = pl.BlockSpec(memory_space=pl.ANY)
VM = pl.BlockSpec(memory_space=pltpu.VMEM)
PARAMS = pltpu.CompilerParams(vmem_limit_bytes=48 * 1024 * 1024)


def place():
    layer = lax.axis_index("layer")
    return layer // 2, layer % 2


def widen(mask, width):
    k = mask.shape[1]
    rep = lax.broadcasted_iota(jnp.int32, (k, width), 1) // (width // k)
    one = lax.broadcasted_iota(jnp.int32, (k, width), 0)
    spread = jnp.where(rep == one, 1.0, 0.0).astype(F32)
    flag = jnp.where(mask > 0, 1.0, 0.0).astype(F32)
    return jnp.dot(flag, spread, preferred_element_type=F32)


def tall(flags):
    n, width = flags.shape
    return jnp.broadcast_to(flags.reshape(n, 1, width), (n, BLOCK, width)).reshape(
        n * BLOCK, width
    )


def left_kernel(x_ref, pat_ref, s_ref, t_ref, wide, buf, sem):
    a, b = place()
    rows, cols = buf.shape
    copy = pltpu.make_async_copy(
        x_ref.at[pl.ds(pl.multiple_of(a * rows, rows), rows),
                 pl.ds(pl.multiple_of(b * cols, cols), cols)],
        buf, sem)
    copy.start()
    wide[...] = widen(pat_ref[...], wide.shape[1])
    copy.wait()
    atoms = rows // BLOCK
    half = rows // 2
    flags = wide[pl.ds(pl.multiple_of(a * atoms, atoms), atoms),
                 pl.ds(pl.multiple_of(b * cols, cols), cols)]
    s_ref[...] = buf[:half, :] * tall(flags[: atoms // 2]).astype(BF16)
    t_ref[...] = buf[half:, :] * tall(flags[atoms // 2:]).astype(BF16)


def left_blocks(matrix, pattern):
    rows, cols = matrix.shape
    out = jax.ShapeDtypeStruct((rows // 4, cols // 2), BF16)
    return pl.pallas_call(
        left_kernel,
        out_shape=(out, out),
        in_specs=[HBM, VM],
        out_specs=(VM, VM),
        scratch_shapes=[
            pltpu.VMEM((rows // BLOCK, cols), F32),
            pltpu.VMEM((rows // 2, cols // 2), BF16),
            pltpu.SemaphoreType.DMA,
        ],
        compiler_params=PARAMS,
        name="left_blocks",
    )(matrix, pattern)


def right_kernel(x_ref, pat_ref, own_ref, send_ref, wide, buf, sems):
    _, b = place()
    h = lax.axis_index("col") % 2
    cols = wide.shape[1]
    slab = cols // 2
    atoms = slab // BLOCK
    copies = []
    for c in range(4):
        copies.append(pltpu.make_async_copy(
            x_ref.at[pl.ds(pl.multiple_of(c * cols + b * slab, slab), slab), :],
            buf.at[c], sems.at[c]))
        copies[-1].start()
    wide[...] = widen(pat_ref[...], cols)
    for c in range(4):
        copies[c].wait()
        start = pl.multiple_of(c * 2 * atoms + b * atoms, atoms)
        buf[c] = buf[c] * tall(wide[pl.ds(start, atoms), :]).astype(BF16)
    for i in range(2):
        own_ref[i * slab:(i + 1) * slab, :] = buf[2 * i + h]
        send_ref[i * slab:(i + 1) * slab, :] = buf[2 * i + 1 - h]


def right_blocks(matrix, pattern):
    rows, cols = matrix.shape
    out = jax.ShapeDtypeStruct((cols, cols), BF16)
    return pl.pallas_call(
        right_kernel,
        out_shape=(out, out),
        in_specs=[HBM, VM],
        out_specs=(VM, VM),
        scratch_shapes=[
            pltpu.VMEM((rows // BLOCK, cols), F32),
            pltpu.VMEM((4, cols // 2, cols), BF16),
            pltpu.SemaphoreType.DMA((4,)),
        ],
        compiler_params=PARAMS,
        name="right_blocks",
    )(matrix, pattern)


def product_kernel(slot, left_from, right_from, *refs):
    n_left = len(left_from)
    lefts = refs[:n_left]
    rights = refs[n_left:n_left + len(right_from)]
    out_ref, left, right, lsem, rsem = refs[n_left + len(right_from):]
    z = lax.axis_index("col") // 2
    r = lax.axis_index("row")
    half, width = lefts[0].shape
    copies = []
    for i, (step, part) in enumerate(right_from):
        source = lax.rem(r - step + 8, 4)
        depth = rights[i].shape[-2]
        src = rights[i] if part is None else rights[i].at[part]
        copies.append(pltpu.make_async_copy(
            src, right.at[pl.ds(pl.multiple_of(source * depth, depth), depth), :], rsem.at[i]))
    for i, (step, part) in enumerate(left_from):
        source = lax.rem(z - step + 16, 8)
        copies.append(pltpu.make_async_copy(
            lefts[i],
            left.at[pl.ds(part * half, half), pl.ds(pl.multiple_of(source * width, width), width)],
            lsem.at[i]))
    for copy in copies:
        copy.start()
    for copy in copies:
        copy.wait()
    for part in range(2):
        out_ref[part * half:(part + 1) * half, :] = jnp.dot(
            left[part * half:(part + 1) * half, :], right[...], preferred_element_type=F32
        ).astype(out_ref.dtype)


def product(slot, lefts, rights, dtype):
    half, width = lefts[0][0].shape
    depth, cols = rights[0][0].shape[-2:]
    return pl.pallas_call(
        functools.partial(product_kernel, slot, [x[1:] for x in lefts], [x[1:] for x in rights]),
        out_shape=jax.ShapeDtypeStruct((2 * half, cols), dtype),
        in_specs=[HBM] * (len(lefts) + len(rights)),
        out_specs=VM,
        scratch_shapes=[
            pltpu.VMEM((2 * half, 8 * width), BF16),
            pltpu.VMEM((4 * depth, cols), BF16),
            pltpu.SemaphoreType.DMA((len(lefts),)),
            pltpu.SemaphoreType.DMA((len(rights),)),
        ],
        compiler_params=PARAMS,
        name="product%d" % slot,
    )(*[x[0] for x in lefts], *[x[0] for x in rights])


def pieces_kernel(own_ref, other_ref, *outs):
    layer = lax.axis_index("layer")
    width = outs[0].shape[1]
    for d, out in enumerate(outs):
        cols = pl.ds(pl.multiple_of(lax.rem(layer + d, 4) * width, width), width)
        out[...] = (own_ref[:, cols] + other_ref[:, cols].astype(F32)).astype(out.dtype)


def pieces(own, other):
    rows, cols = own.shape
    return pl.pallas_call(
        pieces_kernel,
        out_shape=(jax.ShapeDtypeStruct((rows, cols // 4), BF16),) * 4,
        in_specs=[VM, VM],
        out_specs=(VM,) * 4,
        compiler_params=PARAMS,
        name="pieces",
    )(own, other)


def total_kernel(p0, p1, p2, p3, keep_ref, out_ref, parts, sems):
    layer = lax.axis_index("layer")
    copies = []
    for d, ref in enumerate((p0, p1, p2, p3)):
        copies.append(pltpu.make_async_copy(ref, parts.at[lax.rem(layer - d + 4, 4)], sems.at[d]))
        copies[-1].start()
    flags = widen(keep_ref[...], out_ref.shape[1])
    for copy in copies:
        copy.wait()
    rows = parts.shape[1]
    for a in range(2):
        both = parts[2 * a].astype(F32) + parts[2 * a + 1].astype(F32)
        kept = tall(flags[a * (rows // BLOCK):(a + 1) * (rows // BLOCK)]) > 0.5
        out_ref[a * rows:(a + 1) * rows, :] = jnp.where(kept, both, 0.0).astype(BF16)


def total(parts, keep):
    rows, width = parts[0].shape
    return pl.pallas_call(
        total_kernel,
        out_shape=jax.ShapeDtypeStruct((2 * rows, width), BF16),
        in_specs=[HBM] * 4 + [VM],
        out_specs=VM,
        scratch_shapes=[pltpu.VMEM((4, rows, width), BF16), pltpu.SemaphoreType.DMA((4,))],
        compiler_params=PARAMS,
        name="total",
    )(*parts, keep)


def along_z(x, d):
    return lax.ppermute(x, "col", [(c, (c // 2 + d) % 8 * 2 + c % 2) for c in range(16)])


def along(x, axis, d):
    return lax.ppermute(x, axis, [(i, (i + d) % 4) for i in range(4)])


def swap(x):
    return lax.ppermute(x, "col", [(c, c ^ 1) for c in range(16)])


def on_device(matrix, pattern, keep):
    s, t = left_blocks(matrix, pattern)
    lefts = [(s, 0, 0), (t, 0, 1)]
    s_up = s_down = s
    t_up = t_down = t
    for step in range(1, 5):
        s_up = along_z(s_up, 1)
        lefts.append((s_up, step, 0))
        t_down = along_z(t_down, -1)
        lefts.append((t_down, -step, 1))
        if step < 4:
            t_up = along_z(t_up, 1)
            lefts.append((t_up, step, 1))
            s_down = along_z(s_down, -1)
            lefts.append((s_down, -step, 0))

    mine, theirs = right_blocks(matrix, pattern)
    both = jnp.stack([mine, swap(theirs)])
    below = along(both, "row", 1)
    above = along(both, "row", -1)
    far = [along(below[0], "row", 1), along(above[1], "row", -1)]

    def rights(slot):
        return [(both, 0, slot), (below, 1, slot), (above, -1, slot), (far[slot], 2, None)]

    other = swap(product(1, lefts, rights(1), BF16))
    own = product(0, lefts, rights(0), F32)
    parts = list(pieces(own, other))
    for d in range(1, 4):
        parts[d] = along(parts[d], "layer", d)
    return total(parts, keep)


def solution(mesh):
    in_specs = (P("row", "col"), P("row", "col"), P("row", ("col", "layer")))
    out_specs = P("row", ("col", "layer"))
    return jax.shard_map(
        on_device, mesh=mesh, in_specs=in_specs, out_specs=out_specs, check_vma=False
    )
```

time: 186 us -> 104 us (0.56)
  waiting for transfers between devices: 149 us -> 52.8 us
  starting transfers between devices: 0.09 us -> 31.7 us
  between operations: 13.2 us -> 0.31 us
  Pallas kernels: 0 us -> 11.3 us
  matrix products: 9.87 us -> 0 us
  other arithmetic: 5.51 us -> 0.1 us
    all_gather x2 -> x0, waiting for transfers between devices: 91.1 us -> none  [the longest x1 58.2 us: on_device(): lax.all_gather(left_local, 'col', axis=1, tiled=True)]
    psum x1 -> x0, waiting for transfers between devices: 58.2 us -> none  [on_device(): totals = lax.psum(rounded_part, 'layer').astype(jnp.float32)]
    ppermute x0 -> x23, waiting for transfers between devices: none -> 52.8 us  [the longest x14 26.6 us: along_z(): lax.ppermute(x, 'col', [(c, (c // 2 + d) % 8 * 2 + c % 2) for c in range(...]
    ppermute x0 -> x23, starting transfers between devices: none -> 31.7 us  [the longest x14 18.3 us: along_z(): lax.ppermute(x, 'col', [(c, (c // 2 + d) % 8 * 2 + c % 2) for c in range(...]
    pallas_call x0 -> x6, Pallas kernels: none -> 11.3 us  [the longest x2 9.01 us: product(): pl.pallas_call(functools.partial(product_kernel, slot, [x[1:] for x in le...]
    dot_general x1 -> x0, matrix products: 9.87 us -> none  [on_device(): jnp.dot(lax.all_gather(left_local, 'col', axis=1, tiled=True), right_pane...]
    broadcast_in_dim x7 -> x0, local copies, waits for them, and re-layouts: 4.15 us -> none  [blockwise(): jnp.where(mask[:, None, :, None] > 0, shaped, jnp.zeros((), values.dtype))]
    select_n x2 -> x0, other arithmetic: 2.8 us -> none  [blockwise(): jnp.where(mask[:, None, :, None] > 0, shaped, jnp.zeros((), values.dtype))]
  transfers between devices with their start and end apart: 3 -> 23, of which waited for: 3 -> 12; matrix products, arithmetic and copies ran while one was open for 4% -> 1% of each run, Pallas kernels for 0% -> 5%
where the time goes in v1:
time: 104 us
  waiting for transfers between devices  52.8 us (51%)
  starting transfers between devices  31.7 us (30%)
  Pallas kernels  11.3 us (11%)
  local copies, waits for them, and re-layouts  7.36 us (7%)
    ppermute x14, waiting for transfers between devices, along_z(): lax.ppermute(x, 'col', [(c, (c // 2 + d) % 8 * 2 + c % 2) for c in range(...  26.6 us
    ppermute x7, waiting for transfers between devices, along(): return lax.ppermute(x, axis, [(i, (i + d) % 4) for i in range(4)])  24.7 us
    ppermute x14, starting transfers between devices, along_z(): lax.ppermute(x, 'col', [(c, (c // 2 + d) % 8 * 2 + c % 2) for c in range(...  18.3 us
    pallas_call x2, Pallas kernels, product(): pl.pallas_call(functools.partial(product_kernel, slot, [x[1:] for x in le...  9.01 us
    ppermute x2, starting transfers between devices, swap(): return lax.ppermute(x, 'col', [(c, c ^ 1) for c in range(16)])  6.81 us
    ppermute x7, starting transfers between devices, along(): return lax.ppermute(x, axis, [(i, (i + d) % 4) for i in range(4)])  6.61 us
    unnamed x16, local copies, waits for them, and re-layouts  6.25 us
  transfers between devices with their start and end apart: 23, of which 12 were waited for; matrix products, arithmetic and copies ran while one was open for 1% of the time, Pallas kernels for 5%

profile of v1, /device:TPU:1, one launch (start us, length us, event | category | flops | bytes accessed | tf_op | source)
XLA Modules:
  0.0 103.6 jit_solution(6749064077649151860)
XLA Ops:
  0.8 1.6 %copy-done.3 = bf16[2048,512]{1,0:T(8,128)(2,1)S(1)} copy-done((bf16[2048,512]{1,0:T(8,128)(2,1)S(1)}, bf16[2048,512]{1,0:T(8,128)(2,1)}, u32[]{:S(2)}) %copy-start.3) | copy-done | bytes 2097176
  2.8 3.3 %collective-permute-start.14 = (bf16[512,512]{1,0:T(8,128)(2,1)S(1)}, bf16[512,512]{1,0:T(8,128)(2,1)S(1)}, u32[]{:S(2)}, u32[]{:S(2)}) collective-permute-start(bf16[512,512]{1,0:T(8,128)(2,1)S(1)} %get-tuple-element.16), channel_id=1, source_target_pairs={{0,4},{4,0},{8,12},{12,8},{16,20},{20,16},{24,28},{28,24},{32,36},... | collective-permute-start | bytes 1572872 | tf_op jit(solution)/shard_map/ppermute | solution.py:223
  9.1 1.7 %collective-permute-start = (bf16[512,256]{1,0:T(8,128)(2,1)S(1)}, bf16[512,256]{1,0:T(8,128)(2,1)S(1)}, u32[]{:S(2)}, u32[]{:S(2)}) collective-permute-start(bf16[512,256]{1,0:T(8,128)(2,1)S(1)} %get-tuple-element.13.refs_0_), channel_id=1, source_target_pairs={{0,8},{4,12},{8,16},{12,20},{16,24},{20,28},{24,32},{28,36},{32,40... | collective-permute-start | bytes 786440 | tf_op jit(solution)/shard_map/ppermute | solution.py:215
  10.8 4.0 %collective-permute-start.1 = (bf16[512,256]{1,0:T(8,128)(2,1)S(1)}, bf16[512,256]{1,0:T(8,128)(2,1)S(1)}, u32[]{:S(2)}, u32[]{:S(2)}) collective-permute-start(bf16[512,256]{1,0:T(8,128)(2,1)S(1)} %get-tuple-element.14.refs_1_), channel_id=1, source_target_pairs={{0,56},{4,60},{8,0},{12,4},{16,8},{20,12},{24,16},{28,20},{32,24},... | collective-permute-start | bytes 786440 | tf_op jit(solution)/shard_map/ppermute | solution.py:215
  14.9 2.7 %collective-permute-start.3 = (bf16[512,256]{1,0:T(8,128)(2,1)S(1)}, bf16[512,256]{1,0:T(8,128)(2,1)S(1)}, u32[]{:S(2)}, u32[]{:S(2)}) collective-permute-start(bf16[512,256]{1,0:T(8,128)(2,1)S(1)} %get-tuple-element.13.refs_0_), channel_id=1, source_target_pairs={{0,56},{4,60},{8,0},{12,4},{16,8},{20,12},{24,16},{28,20},{32,24},... | collective-permute-start | bytes 786440 | tf_op jit(solution)/shard_map/ppermute | solution.py:215
  17.6 3.3 %collective-permute-done.refs_2_ = bf16[512,256]{1,0:T(8,128)(2,1)S(1)} collective-permute-done((bf16[512,256]{1,0:T(8,128)(2,1)S(1)}, bf16[512,256]{1,0:T(8,128)(2,1)S(1)}, u32[]{:S(2)}, u32[]{:S(2)}) %collective-permute-start) | collective-permute-done | bytes 262176 | tf_op jit(solution)/shard_map/ppermute | solution.py:215
  20.9 5.6 %collective-permute-done.2.refs_4_ = bf16[512,256]{1,0:T(8,128)(2,1)S(1)} collective-permute-done((bf16[512,256]{1,0:T(8,128)(2,1)S(1)}, bf16[512,256]{1,0:T(8,128)(2,1)S(1)}, u32[]{:S(2)}, u32[]{:S(2)}) %collective-permute-start.2) | collective-permute-done | bytes 262176 | tf_op jit(solution)/shard_map/ppermute | solution.py:215
  27.9 4.1 %collective-permute-done.4.refs_6_ = bf16[512,256]{1,0:T(8,128)(2,1)S(1)} collective-permute-done((bf16[512,256]{1,0:T(8,128)(2,1)S(1)}, bf16[512,256]{1,0:T(8,128)(2,1)S(1)}, u32[]{:S(2)}, u32[]{:S(2)}) %collective-permute-start.4) | collective-permute-done | bytes 262176 | tf_op jit(solution)/shard_map/ppermute | solution.py:215
  33.5 2.9 %collective-permute-done.6.refs_8_ = bf16[512,256]{1,0:T(8,128)(2,1)S(1)} collective-permute-done((bf16[512,256]{1,0:T(8,128)(2,1)S(1)}, bf16[512,256]{1,0:T(8,128)(2,1)S(1)}, u32[]{:S(2)}, u32[]{:S(2)}) %collective-permute-start.6) | collective-permute-done | bytes 262176 | tf_op jit(solution)/shard_map/ppermute | solution.py:215
  36.4 2.4 %collective-permute-start.9 = (bf16[512,256]{1,0:T(8,128)(2,1)S(1)}, bf16[512,256]{1,0:T(8,128)(2,1)S(1)}, u32[]{:S(2)}, u32[]{:S(2)}) collective-permute-start(bf16[512,256]{1,0:T(8,128)(2,1)S(1)} %collective-permute-done.5.refs_7_), channel_id=1, source_target_pairs={{0,56},{4,60},{8,0},{12,4},{16,8},{20,12},{24,16},{28,20},{32,24},... | collective-permute-start | bytes 786440 | tf_op jit(solution)/shard_map/ppermute | solution.py:215
  39.4 2.6 %collective-permute-done.8.refs_10_ = bf16[512,256]{1,0:T(8,128)(2,1)S(1)} collective-permute-done((bf16[512,256]{1,0:T(8,128)(2,1)S(1)}, bf16[512,256]{1,0:T(8,128)(2,1)S(1)}, u32[]{:S(2)}, u32[]{:S(2)}) %collective-permute-start.8) | collective-permute-done | bytes 262176 | tf_op jit(solution)/shard_map/ppermute | solution.py:215
  42.0 2.2 %collective-permute-start.11 = (bf16[512,256]{1,0:T(8,128)(2,1)S(1)}, bf16[512,256]{1,0:T(8,128)(2,1)S(1)}, u32[]{:S(2)}, u32[]{:S(2)}) collective-permute-start(bf16[512,256]{1,0:T(8,128)(2,1)S(1)} %collective-permute-done.7.refs_9_), channel_id=1, source_target_pairs={{0,56},{4,60},{8,0},{12,4},{16,8},{20,12},{24,16},{28,20},{32,24},... | collective-permute-start | bytes 786440 | tf_op jit(solution)/shard_map/ppermute | solution.py:215
  44.3 3.4 %collective-permute-done.10.refs_12_ = bf16[512,256]{1,0:T(8,128)(2,1)S(1)} collective-permute-done((bf16[512,256]{1,0:T(8,128)(2,1)S(1)}, bf16[512,256]{1,0:T(8,128)(2,1)S(1)}, u32[]{:S(2)}, u32[]{:S(2)}) %collective-permute-start.10) | collective-permute-done | bytes 262176 | tf_op jit(solution)/shard_map/ppermute | solution.py:215
  47.6 2.2 %collective-permute-start.13 = (bf16[512,256]{1,0:T(8,128)(2,1)S(1)}, bf16[512,256]{1,0:T(8,128)(2,1)S(1)}, u32[]{:S(2)}, u32[]{:S(2)}) collective-permute-start(bf16[512,256]{1,0:T(8,128)(2,1)S(1)} %collective-permute-done.9.refs_11_), channel_id=1, source_target_pairs={{0,56},{4,60},{8,0},{12,4},{16,8},{20,12},{24,16},{28,20},{32,24},... | collective-permute-start | bytes 786440 | tf_op jit(solution)/shard_map/ppermute | solution.py:215
  49.9 2.8 %collective-permute-done.12.refs_14_ = bf16[512,256]{1,0:T(8,128)(2,1)S(1)} collective-permute-done((bf16[512,256]{1,0:T(8,128)(2,1)S(1)}, bf16[512,256]{1,0:T(8,128)(2,1)S(1)}, u32[]{:S(2)}, u32[]{:S(2)}) %collective-permute-start.12) | collective-permute-done | bytes 262176 | tf_op jit(solution)/shard_map/ppermute | solution.py:215
  52.7 1.9 %collective-permute-done.13.refs_15_ = bf16[512,256]{1,0:T(8,128)(2,1)S(1)} collective-permute-done((bf16[512,256]{1,0:T(8,128)(2,1)S(1)}, bf16[512,256]{1,0:T(8,128)(2,1)S(1)}, u32[]{:S(2)}, u32[]{:S(2)}) %collective-permute-start.13) | collective-permute-done | bytes 262176 | tf_op jit(solution)/shard_map/ppermute | solution.py:215
  55.6 3.9 %product1.1 = bf16[1024,512]{1,0:T(8,128)(2,1)S(1)} custom-call(bf16[512,256]{1,0:T(8,128)(2,1)S(1)} %get-tuple-element.13.refs_0_, bf16[512,256]{1,0:T(8,128)(2,1)S(1)} %get-tuple-element.14.refs_1_, bf16[512,256]{1,0:T(8,128)(2,1)S(1)} %collective-permute-done.refs_2_, bf16[512,256]{1,0:T(8,128)(2,1)S(1)} %collective-permute-done.1.refs_3_, ...), custom_call_target="tpu_custom_call" | custom-call | tf_op jit(solution)/shard_map/product1/pallas_call | solution.py:149
  59.5 3.5 %collective-permute-start.19 = (bf16[1024,512]{1,0:T(8,128)(2,1)S(1)}, bf16[1024,512]{1,0:T(8,128)(2,1)S(1)}, u32[]{:S(2)}, u32[]{:S(2)}) collective-permute-start(bf16[1024,512]{1,0:T(8,128)(2,1)S(1)} %product1.1), channel_id=1, source_target_pairs={{0,4},{4,0},{8,12},{12,8},{16,20},{20,16},{24,28},{28,24},{32,36},... | collective-permute-start | bytes 3145736 | tf_op jit(solution)/shard_map/ppermute | solution.py:223
  64.1 14.7 %collective-permute-done.17.refs_19_ = bf16[512,512]{1,0:T(8,128)(2,1)S(1)} collective-permute-done((bf16[512,512]{1,0:T(8,128)(2,1)S(1)}, bf16[512,512]{1,0:T(8,128)(2,1)S(1)}, u32[]{:S(2)}, u32[]{:S(2)}) %collective-permute-start.17) | collective-permute-done | bytes 524320 | tf_op jit(solution)/shard_map/ppermute | solution.py:219
  80.1 5.1 %product0.1.own_ref = f32[1024,512]{1,0:T(8,128)} custom-call(bf16[512,256]{1,0:T(8,128)(2,1)S(1)} %get-tuple-element.13.refs_0_, bf16[512,256]{1,0:T(8,128)(2,1)S(1)} %get-tuple-element.14.refs_1_, bf16[512,256]{1,0:T(8,128)(2,1)S(1)} %collective-permute-done.refs_2_, bf16[512,256]{1,0:T(8,128)(2,1)S(1)} %collective-permute-done.1.refs_3_, ...), custom_call_target="tpu_custom_call" | custom-call | tf_op jit(solution)/shard_map/product0/pallas_call | solution.py:149
  85.3 1.6 %copy-done.2 = f32[1024,512]{1,0:T(8,128)S(1)} copy-done((f32[1024,512]{1,0:T(8,128)S(1)}, f32[1024,512]{1,0:T(8,128)}, u32[]{:S(2)}) %copy-start.2) | copy-done | bytes 2097176
  88.6 2.4 %collective-permute-start.21 = (bf16[1024,128]{1,0:T(8,128)(2,1)S(1)}, bf16[1024,128]{1,0:T(8,128)(2,1)S(1)}, u32[]{:S(2)}, u32[]{:S(2)}) collective-permute-start(bf16[1024,128]{1,0:T(8,128)(2,1)S(1)} %get-tuple-element.19), channel_id=1, source_target_pairs={{0,2},{1,3},{2,0},{3,1},{4,6},{5,7},{6,4},{7,5},{8,10},{9,11},{10,... | collective-permute-start | bytes 786440 | tf_op jit(solution)/shard_map/ppermute | solution.py:219
  92.3 3.3 %collective-permute-done.20.p1 = bf16[1024,128]{1,0:T(8,128)(2,1)S(1)} collective-permute-done((bf16[1024,128]{1,0:T(8,128)(2,1)S(1)}, bf16[1024,128]{1,0:T(8,128)(2,1)S(1)}, u32[]{:S(2)}, u32[]{:S(2)}) %collective-permute-start.20) | collective-permute-done | bytes 262176 | tf_op jit(solution)/shard_map/ppermute | solution.py:219
  95.6 6.6 %collective-permute-done.21.p2 = bf16[1024,128]{1,0:T(8,128)(2,1)S(1)} collective-permute-done((bf16[1024,128]{1,0:T(8,128)(2,1)S(1)}, bf16[1024,128]{1,0:T(8,128)(2,1)S(1)}, u32[]{:S(2)}, u32[]{:S(2)}) %collective-permute-start.21) | collective-permute-done | bytes 262176 | tf_op jit(solution)/shard_map/ppermute | solution.py:219
  (47 shorter events, 15.3 us)
Async XLA Ops:
  2.8 4.9 %collective-permute-start.14 = (bf16[512,512]{1,0:T(8,128)(2,1)S(1)}, bf16[512,512]{1,0:T(8,128)(2,1)S(1)}, u32[]{:S(2)}, u32[]{:S(2)}) collective-permute-start(bf16[512,512]{1,0:T(8,128)(2,1)S(1)} %get-tuple-element.16), channel_id=1, source_target_pairs={{0,4},{4,0},{8,12},{12,8},{16,20},{20,16},{24,28},{28,24},{32,36},... | collective-permute-start | bytes 1572872 | tf_op jit(solution)/shard_map/ppermute | solution.py:223
  7.8 46.8 %copy-start = (bf16[2,512,512]{2,1,0:T(8,128)(2,1)}, bf16[2,512,512]{2,1,0:T(8,128)(2,1)S(1)}, u32[]{:S(2)}) copy-start(bf16[2,512,512]{2,1,0:T(8,128)(2,1)S(1)} %pad_maximum_fusion.refs_16_) | copy-start | bytes 3145732
  7.8 31.0 %collective-permute-start.16 = (bf16[2,512,512]{2,1,0:T(8,128)(2,1)S(1)}, bf16[2,512,512]{2,1,0:T(8,128)(2,1)S(1)}, u32[]{:S(2)}, u32[]{:S(2)}) collective-permute-start(bf16[2,512,512]{2,1,0:T(8,128)(2,1)S(1)} %pad_maximum_fusion.refs_16_), channel_id=1, source_target_pairs={{0,192},{64,0},{128,64},{192,128},{1,193},{65,1},{129,65},{193,129... | collective-permute-start | bytes 3145736 | tf_op jit(solution)/shard_map/ppermute | solution.py:219
  9.1 11.7 %collective-permute-start = (bf16[512,256]{1,0:T(8,128)(2,1)S(1)}, bf16[512,256]{1,0:T(8,128)(2,1)S(1)}, u32[]{:S(2)}, u32[]{:S(2)}) collective-permute-start(bf16[512,256]{1,0:T(8,128)(2,1)S(1)} %get-tuple-element.13.refs_0_), channel_id=1, source_target_pairs={{0,8},{4,12},{8,16},{12,20},{16,24},{20,28},{24,32},{28,36},{32,40... | collective-permute-start | bytes 786440 | tf_op jit(solution)/shard_map/ppermute | solution.py:215
  10.8 10.0 %collective-permute-start.1 = (bf16[512,256]{1,0:T(8,128)(2,1)S(1)}, bf16[512,256]{1,0:T(8,128)(2,1)S(1)}, u32[]{:S(2)}, u32[]{:S(2)}) collective-permute-start(bf16[512,256]{1,0:T(8,128)(2,1)S(1)} %get-tuple-element.14.refs_1_), channel_id=1, source_target_pairs={{0,56},{4,60},{8,0},{12,4},{16,8},{20,12},{24,16},{28,20},{32,24},... | collective-permute-start | bytes 786440 | tf_op jit(solution)/shard_map/ppermute | solution.py:215
  14.9 11.6 %collective-permute-start.2 = (bf16[512,256]{1,0:T(8,128)(2,1)S(1)}, bf16[512,256]{1,0:T(8,128)(2,1)S(1)}, u32[]{:S(2)}, u32[]{:S(2)}) collective-permute-start(bf16[512,256]{1,0:T(8,128)(2,1)S(1)} %get-tuple-element.14.refs_1_), channel_id=1, source_target_pairs={{0,8},{4,12},{8,16},{12,20},{16,24},{20,28},{24,32},{28,36},{32,40... | collective-permute-start | bytes 786440 | tf_op jit(solution)/shard_map/ppermute | solution.py:215
  14.9 12.7 %collective-permute-start.3 = (bf16[512,256]{1,0:T(8,128)(2,1)S(1)}, bf16[512,256]{1,0:T(8,128)(2,1)S(1)}, u32[]{:S(2)}, u32[]{:S(2)}) collective-permute-start(bf16[512,256]{1,0:T(8,128)(2,1)S(1)} %get-tuple-element.13.refs_0_), channel_id=1, source_target_pairs={{0,56},{4,60},{8,0},{12,4},{16,8},{20,12},{24,16},{28,20},{32,24},... | collective-permute-start | bytes 786440 | tf_op jit(solution)/shard_map/ppermute | solution.py:215
  20.8 11.2 %collective-permute-start.4 = (bf16[512,256]{1,0:T(8,128)(2,1)S(1)}, bf16[512,256]{1,0:T(8,128)(2,1)S(1)}, u32[]{:S(2)}, u32[]{:S(2)}) collective-permute-start(bf16[512,256]{1,0:T(8,128)(2,1)S(1)} %collective-permute-done.refs_2_), channel_id=1, source_target_pairs={{0,8},{4,12},{8,16},{12,20},{16,24},{20,28},{24,32},{28,36},{32,40... | collective-permute-start | bytes 786440 | tf_op jit(solution)/shard_map/ppermute | solution.py:215
  20.9 33.7 %collective-permute-start.15 = (bf16[2,512,512]{2,1,0:T(8,128)(2,1)S(1)}, bf16[2,512,512]{2,1,0:T(8,128)(2,1)S(1)}, u32[]{:S(2)}, u32[]{:S(2)}) collective-permute-start(bf16[2,512,512]{2,1,0:T(8,128)(2,1)S(1)} %pad_maximum_fusion.refs_16_), channel_id=1, source_target_pairs={{0,64},{64,128},{128,192},{192,0},{1,65},{65,129},{129,193},{193,1... | collective-permute-start | bytes 3145736 | tf_op jit(solution)/shard_map/ppermute | solution.py:219
  26.5 6.8 %collective-permute-start.5 = (bf16[512,256]{1,0:T(8,128)(2,1)S(1)}, bf16[512,256]{1,0:T(8,128)(2,1)S(1)}, u32[]{:S(2)}, u32[]{:S(2)}) collective-permute-start(bf16[512,256]{1,0:T(8,128)(2,1)S(1)} %collective-permute-done.1.refs_3_), channel_id=1, source_target_pairs={{0,56},{4,60},{8,0},{12,4},{16,8},{20,12},{24,16},{28,20},{32,24},... | collective-permute-start | bytes 786440 | tf_op jit(solution)/shard_map/ppermute | solution.py:215
  27.6 8.8 %collective-permute-start.6 = (bf16[512,256]{1,0:T(8,128)(2,1)S(1)}, bf16[512,256]{1,0:T(8,128)(2,1)S(1)}, u32[]{:S(2)}, u32[]{:S(2)}) collective-permute-start(bf16[512,256]{1,0:T(8,128)(2,1)S(1)} %collective-permute-done.2.refs_4_), channel_id=1, source_target_pairs={{0,8},{4,12},{8,16},{12,20},{16,24},{20,28},{24,32},{28,36},{32,40... | collective-permute-start | bytes 786440 | tf_op jit(solution)/shard_map/ppermute | solution.py:215
  32.1 6.8 %collective-permute-start.7 = (bf16[512,256]{1,0:T(8,128)(2,1)S(1)}, bf16[512,256]{1,0:T(8,128)(2,1)S(1)}, u32[]{:S(2)}, u32[]{:S(2)}) collective-permute-start(bf16[512,256]{1,0:T(8,128)(2,1)S(1)} %collective-permute-done.3.refs_5_), channel_id=1, source_target_pairs={{0,56},{4,60},{8,0},{12,4},{16,8},{20,12},{24,16},{28,20},{32,24},... | collective-permute-start | bytes 786440 | tf_op jit(solution)/shard_map/ppermute | solution.py:215
  33.2 8.8 %collective-permute-start.8 = (bf16[512,256]{1,0:T(8,128)(2,1)S(1)}, bf16[512,256]{1,0:T(8,128)(2,1)S(1)}, u32[]{:S(2)}, u32[]{:S(2)}) collective-permute-start(bf16[512,256]{1,0:T(8,128)(2,1)S(1)} %collective-permute-done.4.refs_6_), channel_id=1, source_target_pairs={{0,8},{4,12},{8,16},{12,20},{16,24},{20,28},{24,32},{28,36},{32,40... | collective-permute-start | bytes 786440 | tf_op jit(solution)/shard_map/ppermute | solution.py:215
  36.4 7.9 %collective-permute-start.9 = (bf16[512,256]{1,0:T(8,128)(2,1)S(1)}, bf16[512,256]{1,0:T(8,128)(2,1)S(1)}, u32[]{:S(2)}, u32[]{:S(2)}) collective-permute-start(bf16[512,256]{1,0:T(8,128)(2,1)S(1)} %collective-permute-done.5.refs_7_), channel_id=1, source_target_pairs={{0,56},{4,60},{8,0},{12,4},{16,8},{20,12},{24,16},{28,20},{32,24},... | collective-permute-start | bytes 786440 | tf_op jit(solution)/shard_map/ppermute | solution.py:215
  38.8 8.8 %collective-permute-start.10 = (bf16[512,256]{1,0:T(8,128)(2,1)S(1)}, bf16[512,256]{1,0:T(8,128)(2,1)S(1)}, u32[]{:S(2)}, u32[]{:S(2)}) collective-permute-start(bf16[512,256]{1,0:T(8,128)(2,1)S(1)} %collective-permute-done.6.refs_8_), channel_id=1, source_target_pairs={{0,8},{4,12},{8,16},{12,20},{16,24},{20,28},{24,32},{28,36},{32,40... | collective-permute-start | bytes 786440 | tf_op jit(solution)/shard_map/ppermute | solution.py:215
  38.9 15.7 %collective-permute-start.18 = (bf16[512,512]{1,0:T(8,128)(2,1)S(1)}, bf16[512,512]{1,0:T(8,128)(2,1)S(1)}, u32[]{:S(2)}, u32[]{:S(2)}) collective-permute-start(bf16[512,512]{1,0:T(8,128)(2,1)S(1)} %slice_bitcast_fusion), channel_id=1, source_target_pairs={{0,192},{64,0},{128,64},{192,128},{1,193},{65,1},{129,65},{193,129... | collective-permute-start | bytes 1572872 | tf_op jit(solution)/shard_map/ppermute | solution.py:219
  42.0 7.9 %collective-permute-start.11 = (bf16[512,256]{1,0:T(8,128)(2,1)S(1)}, bf16[512,256]{1,0:T(8,128)(2,1)S(1)}, u32[]{:S(2)}, u32[]{:S(2)}) collective-permute-start(bf16[512,256]{1,0:T(8,128)(2,1)S(1)} %collective-permute-done.7.refs_9_), channel_id=1, source_target_pairs={{0,56},{4,60},{8,0},{12,4},{16,8},{20,12},{24,16},{28,20},{32,24},... | collective-permute-start | bytes 786440 | tf_op jit(solution)/shard_map/ppermute | solution.py:215
  44.3 8.4 %collective-permute-start.12 = (bf16[512,256]{1,0:T(8,128)(2,1)S(1)}, bf16[512,256]{1,0:T(8,128)(2,1)S(1)}, u32[]{:S(2)}, u32[]{:S(2)}) collective-permute-start(bf16[512,256]{1,0:T(8,128)(2,1)S(1)} %collective-permute-done.8.refs_10_), channel_id=1, source_target_pairs={{0,8},{4,12},{8,16},{12,20},{16,24},{20,28},{24,32},{28,36},{32,40... | collective-permute-start | bytes 786440 | tf_op jit(solution)/shard_map/ppermute | solution.py:215
  47.6 6.9 %collective-permute-start.13 = (bf16[512,256]{1,0:T(8,128)(2,1)S(1)}, bf16[512,256]{1,0:T(8,128)(2,1)S(1)}, u32[]{:S(2)}, u32[]{:S(2)}) collective-permute-start(bf16[512,256]{1,0:T(8,128)(2,1)S(1)} %collective-permute-done.9.refs_11_), channel_id=1, source_target_pairs={{0,56},{4,60},{8,0},{12,4},{16,8},{20,12},{24,16},{28,20},{32,24},... | collective-permute-start | bytes 786440 | tf_op jit(solution)/shard_map/ppermute | solution.py:215
  59.5 25.8 %collective-permute-start.19 = (bf16[1024,512]{1,0:T(8,128)(2,1)S(1)}, bf16[1024,512]{1,0:T(8,128)(2,1)S(1)}, u32[]{:S(2)}, u32[]{:S(2)}) collective-permute-start(bf16[1024,512]{1,0:T(8,128)(2,1)S(1)} %product1.1), channel_id=1, source_target_pairs={{0,4},{4,0},{8,12},{12,8},{16,20},{20,16},{24,28},{28,24},{32,36},... | collective-permute-start | bytes 3145736 | tf_op jit(solution)/shard_map/ppermute | solution.py:223
  64.0 14.8 %collective-permute-start.17 = (bf16[512,512]{1,0:T(8,128)(2,1)S(1)}, bf16[512,512]{1,0:T(8,128)(2,1)S(1)}, u32[]{:S(2)}, u32[]{:S(2)}) collective-permute-start(bf16[512,512]{1,0:T(8,128)(2,1)S(1)} %slice_bitcast_fusion.1), channel_id=1, source_target_pairs={{0,64},{64,128},{128,192},{192,0},{1,65},{65,129},{129,193},{193,1... | collective-permute-start | bytes 1572872 | tf_op jit(solution)/shard_map/ppermute | solution.py:219
  87.2 8.3 %collective-permute-start.20 = (bf16[1024,128]{1,0:T(8,128)(2,1)S(1)}, bf16[1024,128]{1,0:T(8,128)(2,1)S(1)}, u32[]{:S(2)}, u32[]{:S(2)}) collective-permute-start(bf16[1024,128]{1,0:T(8,128)(2,1)S(1)} %get-tuple-element.18), channel_id=1, source_target_pairs={{0,1},{1,2},{2,3},{3,0},{4,5},{5,6},{6,7},{7,4},{8,9},{9,10},{10,1... | collective-permute-start | bytes 786440 | tf_op jit(solution)/shard_map/ppermute | solution.py:219
  88.6 13.6 %collective-permute-start.21 = (bf16[1024,128]{1,0:T(8,128)(2,1)S(1)}, bf16[1024,128]{1,0:T(8,128)(2,1)S(1)}, u32[]{:S(2)}, u32[]{:S(2)}) collective-permute-start(bf16[1024,128]{1,0:T(8,128)(2,1)S(1)} %get-tuple-element.19), channel_id=1, source_target_pairs={{0,2},{1,3},{2,0},{3,1},{4,6},{5,7},{6,4},{7,5},{8,10},{9,11},{10,... | collective-permute-start | bytes 786440 | tf_op jit(solution)/shard_map/ppermute | solution.py:219
  91.0 11.2 %collective-permute-start.22 = (bf16[1024,128]{1,0:T(8,128)(2,1)S(1)}, bf16[1024,128]{1,0:T(8,128)(2,1)S(1)}, u32[]{:S(2)}, u32[]{:S(2)}) collective-permute-start(bf16[1024,128]{1,0:T(8,128)(2,1)S(1)} %get-tuple-element.20), channel_id=1, source_target_pairs={{0,3},{1,0},{2,1},{3,2},{4,7},{5,4},{6,5},{7,6},{8,11},{9,8},{10,9... | collective-permute-start | bytes 786440 | tf_op jit(solution)/shard_map/ppermute | solution.py:219
  (6 other events, 26.5 us)

commit v2 on v1

v2 whole, which is shorter than its diff:
```python
import functools

import jax
import jax.numpy as jnp
from jax import lax
from jax.experimental import pallas as pl
from jax.experimental.pallas import tpu as pltpu
from jax.sharding import PartitionSpec as P

BLOCK = 32
F32 = jnp.float32
BF16 = jnp.bfloat16
ANY = pl.BlockSpec(memory_space=pl.ANY)
HBM = pl.BlockSpec(memory_space=pltpu.HBM)
VM = pl.BlockSpec(memory_space=pltpu.VMEM)


def vmem(mib):
    return pltpu.CompilerParams(vmem_limit_bytes=mib * 1024 * 1024)


def place():
    layer = lax.axis_index("layer")
    return layer // 2, layer % 2


def widen(mask, width):
    k = mask.shape[0]
    rep = lax.broadcasted_iota(jnp.int32, (k, width), 1) // (width // k)
    one = lax.broadcasted_iota(jnp.int32, (k, width), 0)
    spread = jnp.where(rep == one, 1.0, 0.0).astype(F32)
    flag = jnp.where(mask > 0, 1.0, 0.0).astype(F32)
    return lax.dot_general(flag, spread, (((0,), (0,)), ((), ())), preferred_element_type=F32)


def tall(flags):
    n, width = flags.shape
    return jnp.broadcast_to(flags.reshape(n, 1, width), (n, BLOCK, width)).reshape(
        n * BLOCK, width
    )


def left_kernel(x_ref, pat_ref, s_ref, t_ref, wide, buf, sem):
    a, b = place()
    rows, cols = buf.shape
    copy = pltpu.make_async_copy(
        x_ref.at[pl.ds(pl.multiple_of(a * rows, rows), rows),
                 pl.ds(pl.multiple_of(b * cols, cols), cols)],
        buf, sem)
    copy.start()
    wide[...] = widen(pat_ref[...], wide.shape[1])
    copy.wait()
    atoms = rows // BLOCK
    half = rows // 2
    flags = wide[pl.ds(pl.multiple_of(a * atoms, atoms), atoms),
                 pl.ds(pl.multiple_of(b * cols, cols), cols)]
    s_ref[...] = buf[:half, :] * tall(flags[: atoms // 2]).astype(BF16)
    t_ref[...] = buf[half:, :] * tall(flags[atoms // 2:]).astype(BF16)


def left_blocks(matrix, pattern):
    rows, cols = matrix.shape
    out = jax.ShapeDtypeStruct((rows // 4, cols // 2), BF16)
    return pl.pallas_call(
        left_kernel,
        out_shape=(out, out),
        in_specs=[HBM, VM],
        out_specs=(VM, VM),
        scratch_shapes=[
            pltpu.VMEM((rows // BLOCK, cols), F32),
            pltpu.VMEM((rows // 2, cols // 2), BF16),
            pltpu.SemaphoreType.DMA,
        ],
        compiler_params=vmem(6),
        name="left_blocks",
    )(matrix, pattern)


def right_kernel(x_ref, pat_ref, own_ref, send_ref, wide, buf, sems):
    _, b = place()
    h = lax.axis_index("col") % 2
    cols = wide.shape[1]
    slab = cols // 2
    atoms = slab // BLOCK
    copies = []
    for c in range(4):
        copies.append(pltpu.make_async_copy(
            x_ref.at[pl.ds(pl.multiple_of(c * cols + b * slab, slab), slab), :],
            buf.at[c], sems.at[c]))
        copies[-1].start()
    wide[...] = widen(pat_ref[...], cols)
    for c in range(4):
        copies[c].wait()
        start = pl.multiple_of(c * 2 * atoms + b * atoms, atoms)
        buf[c] = buf[c] * tall(wide[pl.ds(start, atoms), :]).astype(BF16)
    for i in range(2):
        own_ref[i * slab:(i + 1) * slab, :] = buf[2 * i + h]
        send_ref[i * slab:(i + 1) * slab, :] = buf[2 * i + 1 - h]


def right_blocks(matrix, pattern):
    rows, cols = matrix.shape
    out = jax.ShapeDtypeStruct((cols, cols), BF16)
    return pl.pallas_call(
        right_kernel,
        out_shape=(out, out),
        in_specs=[HBM, VM],
        out_specs=(VM, VM),
        scratch_shapes=[
            pltpu.VMEM((rows // BLOCK, cols), F32),
            pltpu.VMEM((4, cols // 2, cols), BF16),
            pltpu.SemaphoreType.DMA((4,)),
        ],
        compiler_params=vmem(10),
        name="right_blocks",
    )(matrix, pattern)


def gather_rows(rights, steps, right, sems):
    z = lax.axis_index("col") // 2
    r = lax.axis_index("row")
    up = 1 - 2 * (lax.axis_index("col") % 2)
    deep = rights[0].shape[1] // 2
    wide = rights[0].shape[2]
    slots = right.shape[1] // wide
    waits = []
    for i, step in enumerate(steps):
        source = lax.rem(z - step + 8, 8)
        away = lax.rem((r - source // 2) * up + 8, 4)
        low = pl.multiple_of(lax.rem(source, 2) * deep, deep)
        for j, ref in enumerate(rights):
            copies = [
                pltpu.make_async_copy(
                    ref.at[slot, pl.ds(low, deep), :],
                    right.at[pl.ds(i * deep, deep), pl.ds((slot if slots > 1 else 0) * wide, wide)],
                    sems.at[i, slot])
                for slot in range(2)
            ]

            @pl.when(away == j)
            def _():
                for copy in copies:
                    copy.start()
        waits.append(copies)
    return waits


def early_kernel(steps, *refs):
    n = len(steps[0])
    lefts = (refs[:n], refs[n:2 * n])
    rights = refs[2 * n:2 * n + 4]
    outs = refs[2 * n + 4:2 * n + 8]
    left, right, lsem, rsem = refs[2 * n + 8:]
    half, width = lefts[0][0].shape
    cols = right.shape[2] // 2
    waits = []
    for part in range(2):
        waits += gather_rows(rights, steps[part], right.at[part], rsem.at[part])
        for i in range(n):
            copy = pltpu.make_async_copy(
                lefts[part][i], left.at[part, :, pl.ds(i * width, width)], lsem.at[part, i])
            copy.start()
            waits.append([copy])
    for copies in waits:
        for copy in copies:
            copy.wait()
    for part in range(2):
        for slot in range(2):
            outs[2 * part + slot][...] = jnp.dot(
                left[part], right[part, :, slot * cols:(slot + 1) * cols],
                preferred_element_type=F32)


def early(lefts, steps, rights):
    half, width = lefts[0].shape
    cols = rights[0].shape[2]
    n = len(steps[0])
    out = jax.ShapeDtypeStruct((half, cols), F32)
    return pl.pallas_call(
        functools.partial(early_kernel, steps),
        out_shape=(out,) * 4,
        in_specs=[ANY] * (len(lefts) + 4),
        out_specs=(VM,) * 4,
        scratch_shapes=[
            pltpu.VMEM((2, half, n * width), BF16),
            pltpu.VMEM((2, n * width, 2 * cols), BF16),
            pltpu.SemaphoreType.DMA((2, n)),
            pltpu.SemaphoreType.DMA((2, n, 2)),
        ],
        compiler_params=vmem(20),
        name="early",
    )(*lefts, *rights)


def late_sum(slot, steps, acc_ref, lefts, rights, right, sems):
    z = lax.axis_index("col") // 2
    r = lax.axis_index("row")
    up = 1 - 2 * (lax.axis_index("col") % 2)
    deep = lefts[0].shape[1]
    waits = []
    for i, step in enumerate(steps):
        source = lax.rem(z - step + 8, 8)
        away = lax.rem((r - source // 2) * up + 8, 4)
        low = pl.multiple_of(lax.rem(source, 2) * deep, deep)
        for j, ref in enumerate(rights):
            copy = pltpu.make_async_copy(
                ref.at[slot, pl.ds(low, deep), :], right.at[pl.ds(i * deep, deep), :], sems.at[i])

            @pl.when(away == j)
            def _():
                copy.start()
        waits.append(copy)
    left = jnp.concatenate([ref[...] for ref in lefts], axis=1)
    for copy in waits:
        copy.wait()
    return acc_ref[...] + jnp.dot(left, right[...], preferred_element_type=F32)


def late_other_kernel(steps, acc_ref, *refs):
    n = len(steps)
    out_ref, right, sems = refs[n + 4:]
    out_ref[...] = late_sum(1, steps, acc_ref, refs[:n], refs[n:n + 4], right, sems).astype(BF16)


def late_other(acc, lefts, steps, rights):
    half, cols = acc.shape
    deep = lefts[0].shape[1]
    return pl.pallas_call(
        functools.partial(late_other_kernel, steps),
        out_shape=jax.ShapeDtypeStruct((half, cols), BF16),
        in_specs=[VM] * (1 + len(lefts)) + [ANY] * 4,
        out_specs=VM,
        scratch_shapes=[
            pltpu.VMEM((len(lefts) * deep, cols), BF16),
            pltpu.SemaphoreType.DMA((len(lefts),)),
        ],
        compiler_params=vmem(8),
        name="late_other",
    )(acc, *lefts, *rights)


def late_own_kernel(steps, acc_ref, other_ref, *refs):
    n = len(steps)
    outs = refs[n + 4:n + 8]
    right, whole, sems = refs[n + 8:]
    whole[...] = other_ref[...].astype(F32) + late_sum(
        0, steps, acc_ref, refs[:n], refs[n:n + 4], right, sems)
    layer = lax.axis_index("layer")
    width = outs[0].shape[1]
    for d, out in enumerate(outs):
        cols = pl.ds(pl.multiple_of(lax.rem(layer + d, 4) * width, width), width)
        out[...] = whole[:, cols].astype(out.dtype)


def late_own(acc, other, lefts, steps, rights):
    half, cols = acc.shape
    deep = lefts[0].shape[1]
    return pl.pallas_call(
        functools.partial(late_own_kernel, steps),
        out_shape=(jax.ShapeDtypeStruct((half, cols // 4), BF16),) * 4,
        in_specs=[VM] * (2 + len(lefts)) + [ANY] * 4,
        out_specs=(VM,) * 4,
        scratch_shapes=[
            pltpu.VMEM((len(lefts) * deep, cols), BF16),
            pltpu.VMEM((half, cols), F32),
            pltpu.SemaphoreType.DMA((len(lefts),)),
        ],
        compiler_params=vmem(8),
        name="late_own",
    )(acc, other, *lefts, *rights)


def total_kernel(*refs):
    pieces, (keep_ref, out_ref, parts, sems) = refs[:8], refs[8:]
    layer = lax.axis_index("layer")
    half = pieces[0].shape[0]
    copies = []
    for part in range(2):
        for d in range(4):
            copies.append(pltpu.make_async_copy(
                pieces[4 * part + d],
                parts.at[lax.rem(layer - d + 4, 4), pl.ds(part * half, half), :],
                sems.at[part, d]))
            copies[-1].start()
    flags = widen(keep_ref[...], out_ref.shape[1])
    for copy in copies:
        copy.wait()
    rows = 2 * half
    for a in range(2):
        both = parts[2 * a].astype(F32) + parts[2 * a + 1].astype(F32)
        kept = tall(flags[a * (rows // BLOCK):(a + 1) * (rows // BLOCK)]) > 0.5
        out_ref[a * rows:(a + 1) * rows, :] = jnp.where(kept, both, 0.0).astype(BF16)


def total(pieces, keep):
    half, width = pieces[0].shape
    return pl.pallas_call(
        total_kernel,
        out_shape=jax.ShapeDtypeStruct((4 * half, width), BF16),
        in_specs=[ANY] * 8 + [VM],
        out_specs=VM,
        scratch_shapes=[
            pltpu.VMEM((4, 2 * half, width), BF16),
            pltpu.SemaphoreType.DMA((2, 4)),
        ],
        compiler_params=vmem(8),
        name="total",
    )(*pieces, keep)


def along_z(x, d):
    return lax.ppermute(x, "col", [(c, (c // 2 + d) % 8 * 2 + c % 2) for c in range(16)])


def along(x, axis, d):
    return lax.ppermute(x, axis, [(i, (i + d) % 4) for i in range(4)])


def swap(x):
    return lax.ppermute(x, "col", [(c, c ^ 1) for c in range(16)])


def turn(x, d):
    pairs = []
    for r in range(4):
        for c in range(16):
            to = (r + (d if c % 2 == 0 else -d)) % 4
            pairs.append((r * 16 + c, to * 16 + c))
    return lax.ppermute(x, ("row", "col"), pairs)


def on_device(matrix, pattern, keep):
    pattern_t = pattern.T
    matrix = pltpu.with_memory_space_constraint(matrix, pltpu.HBM)
    s, t = left_blocks(matrix, pattern_t)
    s, t, matrix, pattern_t = lax.optimization_barrier((s, t, matrix, pattern_t))
    left = ({0: s}, {0: t})
    for step in (1, 2, 3, 4):
        for part in range(2):
            for way in (1, -1):
                if step < 4 or way == (1, -1)[part]:
                    at = way * step
                    left[part][at] = along_z(left[part][at - way], way)

    mine, theirs = right_blocks(matrix, pattern_t)
    both = jnp.stack([mine, swap(theirs)])
    below = turn(both, 1)
    above = turn(both, -1)
    far = turn(below, 1)
    rights = [both, below, far, above]

    order = ((0, 1, -1, 2, -2, 3), (0, -1, 1, -2, 2, -3))
    last = ((-3, 4), (3, -4))
    acc = early([left[p][i] for p in range(2) for i in order[p]], order, rights)
    pieces = []
    for p in range(2):
        blocks = [left[p][i] for i in last[p]]
        other = swap(late_other(acc[2 * p + 1], blocks, last[p], rights))
        mine = late_own(acc[2 * p], other, blocks, last[p], rights)
        pieces += [mine[0]] + [along(mine[d], "layer", d) for d in range(1, 4)]
    return total(pieces, keep.T)


def solution(mesh):
    in_specs = (P("row", "col"), P("row", "col"), P("row", ("col", "layer")))
    out_specs = P("row", ("col", "layer"))
    return jax.shard_map(
        on_device, mesh=mesh, in_specs=in_specs, out_specs=out_specs, check_vma=False
    )
```

time: 104 us -> 98.9 us (0.951)
  starting transfers between devices: 31.7 us -> 41.1 us
  waiting for transfers between devices: 52.8 us -> 43.8 us
  local copies, waits for them, and re-layouts: 7.36 us -> 0.7 us
  Pallas kernels: 11.3 us -> 12.7 us
    ppermute x7 -> x6, waiting for transfers between devices: 24.7 us -> 7.16 us  [along(): return lax.ppermute(x, axis, [(i, (i + d) % 4) for i in range(4)])]
    ppermute x0 -> x3, waiting for transfers between devices: none -> 14.5 us  [turn(): return lax.ppermute(x, ('row', 'col'), pairs)]
    ppermute x14, waiting for transfers between devices: 26.6 us -> 20.6 us  [along_z(): lax.ppermute(x, 'col', [(c, (c // 2 + d) % 8 * 2 + c % 2) for c in range(...]
    unnamed x16 -> x4, local copies, waits for them, and re-layouts: 6.25 us -> 0.7 us
    ppermute x14, starting transfers between devices: 18.3 us -> 23.1 us  [along_z(): lax.ppermute(x, 'col', [(c, (c // 2 + d) % 8 * 2 + c % 2) for c in range(...]
    ppermute x0 -> x3, starting transfers between devices: none -> 2.89 us  [turn(): return lax.ppermute(x, ('row', 'col'), pairs)]
    ppermute x7 -> x6, starting transfers between devices: 6.61 us -> 7.78 us  [along(): return lax.ppermute(x, axis, [(i, (i + d) % 4) for i in range(4)])]
    squeeze x2 -> x0, local copies, waits for them, and re-layouts: 1.11 us -> none  [on_device(): far = [along(below[0], 'row', 1), along(above[1], 'row', -1)]]
  transfers between devices with their start and end apart: 23 -> 26, of which waited for: 12 -> 11; matrix products, arithmetic and copies ran while one was open for 1% -> 0% of each run, Pallas kernels for 5% -> 8%
where the time goes in v2:
time: 98.9 us; the launch traced here: 98.7 us
  waiting for transfers between devices  43.8 us (44%)
  starting transfers between devices  41.1 us (42%)
  Pallas kernels  12.7 us (13%)
    ppermute x14, starting transfers between devices, along_z(): lax.ppermute(x, 'col', [(c, (c // 2 + d) % 8 * 2 + c % 2) for c in range(...  23.1 us
    ppermute x14, waiting for transfers between devices, along_z(): lax.ppermute(x, 'col', [(c, (c // 2 + d) % 8 * 2 + c % 2) for c in range(...  20.6 us
    ppermute x3, waiting for transfers between devices, turn(): return lax.ppermute(x, ('row', 'col'), pairs)  14.5 us
    ppermute x6, starting transfers between devices, along(): return lax.ppermute(x, axis, [(i, (i + d) % 4) for i in range(4)])  7.78 us
    ppermute x3, starting transfers between devices, swap(): return lax.ppermute(x, 'col', [(c, c ^ 1) for c in range(16)])  7.3 us
    ppermute x6, waiting for transfers between devices, along(): return lax.ppermute(x, axis, [(i, (i + d) % 4) for i in range(4)])  7.16 us
    pallas_call x1, Pallas kernels, early(): pl.pallas_call(functools.partial(early_kernel, steps), out_shape=(out,) *...  4.79 us
    ppermute x3, starting transfers between devices, turn(): return lax.ppermute(x, ('row', 'col'), pairs)  2.89 us
  transfers between devices with their start and end apart: 26, of which 11 were waited for; matrix products, arithmetic and copies ran while one was open for 0% of the time, Pallas kernels for 8%

profile of v2, /device:TPU:1, one launch (start us, length us, event | category | flops | bytes accessed | tf_op | source)
XLA Modules:
  0.0 98.7 jit_solution(16134349546763492259)
XLA Ops:
  3.2 3.3 %collective-permute-start.10 = (bf16[512,512]{1,0:T(8,128)(2,1)S(1)}, bf16[512,512]{1,0:T(8,128)(2,1)S(1)}, u32[]{:S(2)}, u32[]{:S(2)}) collective-permute-start(bf16[512,512]{1,0:T(8,128)(2,1)S(1)} %get-tuple-element.32), channel_id=1, source_target_pairs={{0,4},{4,0},{8,12},{12,8},{16,20},{20,16},{24,28},{28,24},{32,36},... | collective-permute-start | bytes 1572872 | tf_op jit(solution)/shard_map/ppermute | solution.py:320
  6.5 1.5 %collective-permute-done.10 = bf16[512,512]{1,0:T(8,128)(2,1)S(1)} collective-permute-done((bf16[512,512]{1,0:T(8,128)(2,1)S(1)}, bf16[512,512]{1,0:T(8,128)(2,1)S(1)}, u32[]{:S(2)}, u32[]{:S(2)}) %collective-permute-start.10) | collective-permute-done | bytes 524320 | tf_op jit(solution)/shard_map/ppermute | solution.py:320
  9.2 1.6 %collective-permute-start = (bf16[512,256]{1,0:T(8,128)(2,1)S(1)}, bf16[512,256]{1,0:T(8,128)(2,1)S(1)}, u32[]{:S(2)}, u32[]{:S(2)}) collective-permute-start(bf16[512,256]{1,0:T(8,128)(2,1)S(1)} %get-tuple-element.27.refs_0_), channel_id=1, source_target_pairs={{0,8},{4,12},{8,16},{12,20},{16,24},{20,28},{24,32},{28,36},{32,40... | collective-permute-start | bytes 786440 | tf_op jit(solution)/shard_map/ppermute | solution.py:312
  10.8 3.9 %collective-permute-start.1 = (bf16[512,256]{1,0:T(8,128)(2,1)S(1)}, bf16[512,256]{1,0:T(8,128)(2,1)S(1)}, u32[]{:S(2)}, u32[]{:S(2)}) collective-permute-start(bf16[512,256]{1,0:T(8,128)(2,1)S(1)} %get-tuple-element.27.refs_0_), channel_id=1, source_target_pairs={{0,56},{4,60},{8,0},{12,4},{16,8},{20,12},{24,16},{28,20},{32,24},... | collective-permute-start | bytes 786440 | tf_op jit(solution)/shard_map/ppermute | solution.py:312
  16.3 14.5 %collective-permute-done.11.refs_13_.refs_3_ = bf16[2,512,512]{2,1,0:T(8,128)(2,1)S(1)} collective-permute-done((bf16[2,512,512]{2,1,0:T(8,128)(2,1)S(1)}, bf16[2,512,512]{2,1,0:T(8,128)(2,1)S(1)}, u32[]{:S(2)}, u32[]{:S(2)}) %collective-permute-start.11) | collective-permute-done | bytes 1048608 | tf_op jit(solution)/shard_map/ppermute | solution.py:329
  30.7 1.8 %collective-permute-start.12 = (bf16[2,512,512]{2,1,0:T(8,128)(2,1)S(1)}, bf16[2,512,512]{2,1,0:T(8,128)(2,1)S(1)}, u32[]{:S(2)}, u32[]{:S(2)}) collective-permute-start(bf16[2,512,512]{2,1,0:T(8,128)(2,1)S(1)} %collective-permute-done.11.refs_13_.refs_3_), channel_id=1, source_target_pairs={{0,64},{4,196},{8,72},{12,204},{16,80},{20,212},{24,88},{28,220},{... | collective-permute-start | bytes 3145736 | tf_op jit(solution)/shard_map/ppermute | solution.py:329
  32.5 1.6 %collective-permute-start.6 = (bf16[512,256]{1,0:T(8,128)(2,1)S(1)}, bf16[512,256]{1,0:T(8,128)(2,1)S(1)}, u32[]{:S(2)}, u32[]{:S(2)}) collective-permute-start(bf16[512,256]{1,0:T(8,128)(2,1)S(1)} %get-tuple-element.28.refs_6_), channel_id=1, source_target_pairs={{0,8},{4,12},{8,16},{12,20},{16,24},{20,28},{24,32},{28,36},{32,40... | collective-permute-start | bytes 786440 | tf_op jit(solution)/shard_map/ppermute | solution.py:312
  34.2 1.6 %collective-permute-start.2 = (bf16[512,256]{1,0:T(8,128)(2,1)S(1)}, bf16[512,256]{1,0:T(8,128)(2,1)S(1)}, u32[]{:S(2)}, u32[]{:S(2)}) collective-permute-start(bf16[512,256]{1,0:T(8,128)(2,1)S(1)} %collective-permute-done.refs_1_), channel_id=1, source_target_pairs={{0,8},{4,12},{8,16},{12,20},{16,24},{20,28},{24,32},{28,36},{32,40... | collective-permute-start | bytes 786440 | tf_op jit(solution)/shard_map/ppermute | solution.py:312
  35.8 4.5 %collective-permute-start.7 = (bf16[512,256]{1,0:T(8,128)(2,1)S(1)}, bf16[512,256]{1,0:T(8,128)(2,1)S(1)}, u32[]{:S(2)}, u32[]{:S(2)}) collective-permute-start(bf16[512,256]{1,0:T(8,128)(2,1)S(1)} %collective-permute-done.5.refs_7_), channel_id=1, source_target_pairs={{0,56},{4,60},{8,0},{12,4},{16,8},{20,12},{24,16},{28,20},{32,24},... | collective-permute-start | bytes 786440 | tf_op jit(solution)/shard_map/ppermute | solution.py:312
  40.3 6.6 %collective-permute-done.6.refs_8_ = bf16[512,256]{1,0:T(8,128)(2,1)S(1)} collective-permute-done((bf16[512,256]{1,0:T(8,128)(2,1)S(1)}, bf16[512,256]{1,0:T(8,128)(2,1)S(1)}, u32[]{:S(2)}, u32[]{:S(2)}) %collective-permute-start.6) | collective-permute-done | bytes 262176 | tf_op jit(solution)/shard_map/ppermute | solution.py:312
  46.9 1.5 %collective-permute-start.3 = (bf16[512,256]{1,0:T(8,128)(2,1)S(1)}, bf16[512,256]{1,0:T(8,128)(2,1)S(1)}, u32[]{:S(2)}, u32[]{:S(2)}) collective-permute-start(bf16[512,256]{1,0:T(8,128)(2,1)S(1)} %collective-permute-done.1.refs_2_), channel_id=1, source_target_pairs={{0,56},{4,60},{8,0},{12,4},{16,8},{20,12},{24,16},{28,20},{32,24},... | collective-permute-start | bytes 786440 | tf_op jit(solution)/shard_map/ppermute | solution.py:312
  48.4 3.4 %collective-permute-done.2.refs_3_ = bf16[512,256]{1,0:T(8,128)(2,1)S(1)} collective-permute-done((bf16[512,256]{1,0:T(8,128)(2,1)S(1)}, bf16[512,256]{1,0:T(8,128)(2,1)S(1)}, u32[]{:S(2)}, u32[]{:S(2)}) %collective-permute-start.2) | collective-permute-done | bytes 262176 | tf_op jit(solution)/shard_map/ppermute | solution.py:312
  51.8 2.7 %collective-permute-start.9 = (bf16[512,256]{1,0:T(8,128)(2,1)S(1)}, bf16[512,256]{1,0:T(8,128)(2,1)S(1)}, u32[]{:S(2)}, u32[]{:S(2)}) collective-permute-start(bf16[512,256]{1,0:T(8,128)(2,1)S(1)} %collective-permute-done.7.refs_9_), channel_id=1, source_target_pairs={{0,56},{4,60},{8,0},{12,4},{16,8},{20,12},{24,16},{28,20},{32,24},... | collective-permute-start | bytes 786440 | tf_op jit(solution)/shard_map/ppermute | solution.py:312
  55.1 5.5 %collective-permute-done.8.refs_10_ = bf16[512,256]{1,0:T(8,128)(2,1)S(1)} collective-permute-done((bf16[512,256]{1,0:T(8,128)(2,1)S(1)}, bf16[512,256]{1,0:T(8,128)(2,1)S(1)}, u32[]{:S(2)}, u32[]{:S(2)}) %collective-permute-start.8) | collective-permute-done | bytes 262176 | tf_op jit(solution)/shard_map/ppermute | solution.py:312
  60.6 2.7 %collective-permute-start.21 = (bf16[512,256]{1,0:T(8,128)(2,1)S(1)}, bf16[512,256]{1,0:T(8,128)(2,1)S(1)}, u32[]{:S(2)}, u32[]{:S(2)}) collective-permute-start(bf16[512,256]{1,0:T(8,128)(2,1)S(1)} %collective-permute-done.9.refs_11_), channel_id=1, source_target_pairs={{0,56},{4,60},{8,0},{12,4},{16,8},{20,12},{24,16},{28,20},{32,24},... | collective-permute-start | bytes 786440 | tf_op jit(solution)/shard_map/ppermute | solution.py:312
  63.3 2.9 %collective-permute-done.4.refs_5_ = bf16[512,256]{1,0:T(8,128)(2,1)S(1)} collective-permute-done((bf16[512,256]{1,0:T(8,128)(2,1)S(1)}, bf16[512,256]{1,0:T(8,128)(2,1)S(1)}, u32[]{:S(2)}, u32[]{:S(2)}) %collective-permute-start.4) | collective-permute-done | bytes 262176 | tf_op jit(solution)/shard_map/ppermute | solution.py:312
  67.7 4.8 %early.1 = (f32[512,512]{1,0:T(8,128)S(1)}, f32[512,512]{1,0:T(8,128)S(1)}, f32[512,512]{1,0:T(8,128)S(1)}, f32[512,512]{1,0:T(8,128)S(1)}) custom-call(bf16[512,256]{1,0:T(8,128)(2,1)S(1)} %get-tuple-element.27.refs_0_, bf16[512,256]{1,0:T(8,128)(2,1)S(1)} %collective-permute-done.refs_1_, bf16[512,256]{1,0:T(8,128)(2,1)S(1)} %collective-permute-done.1.refs_2_, ...), custom_call_target="tpu_custom_call" | custom-call | tf_op jit(solution)/shard_map/early/pallas_call | solution.py:179
  73.2 2.5 %collective-permute-start.22 = (bf16[512,512]{1,0:T(8,128)(2,1)S(1)}, bf16[512,512]{1,0:T(8,128)(2,1)S(1)}, u32[]{:S(2)}, u32[]{:S(2)}) collective-permute-start(bf16[512,512]{1,0:T(8,128)(2,1)S(1)} %late_other.3), channel_id=1, source_target_pairs={{0,4},{4,0},{8,12},{12,8},{16,20},{20,16},{24,28},{28,24},{32,36},... | collective-permute-start | bytes 1572872 | tf_op jit(solution)/shard_map/ppermute | solution.py:320
  75.7 1.6 %collective-permute-done.15.refs_1_ = bf16[512,256]{1,0:T(8,128)(2,1)S(1)} collective-permute-done((bf16[512,256]{1,0:T(8,128)(2,1)S(1)}, bf16[512,256]{1,0:T(8,128)(2,1)S(1)}, u32[]{:S(2)}, u32[]{:S(2)}) %collective-permute-start.15) | collective-permute-done | bytes 262176 | tf_op jit(solution)/shard_map/ppermute | solution.py:312
  81.4 2.4 %collective-permute-start.24 = (bf16[512,128]{1,0:T(8,128)(2,1)S(1)}, bf16[512,128]{1,0:T(8,128)(2,1)S(1)}, u32[]{:S(2)}, u32[]{:S(2)}) collective-permute-start(bf16[512,128]{1,0:T(8,128)(2,1)S(1)} %get-tuple-element.43), channel_id=1, source_target_pairs={{0,2},{1,3},{2,0},{3,1},{4,6},{5,7},{6,4},{7,5},{8,10},{9,11},{10,... | collective-permute-start | bytes 393224 | tf_op jit(solution)/shard_map/ppermute | solution.py:316
  87.2 1.6 %collective-permute-start.19 = (bf16[512,128]{1,0:T(8,128)(2,1)S(1)}, bf16[512,128]{1,0:T(8,128)(2,1)S(1)}, u32[]{:S(2)}, u32[]{:S(2)}) collective-permute-start(bf16[512,128]{1,0:T(8,128)(2,1)S(1)} %get-tuple-element.38), channel_id=1, source_target_pairs={{0,3},{1,0},{2,1},{3,2},{4,7},{5,4},{6,5},{7,6},{8,11},{9,8},{10,9... | collective-permute-start | bytes 393224 | tf_op jit(solution)/shard_map/ppermute | solution.py:316
  90.3 2.7 %collective-permute-done.17.refs_1_ = bf16[512,128]{1,0:T(8,128)(2,1)S(1)} collective-permute-done((bf16[512,128]{1,0:T(8,128)(2,1)S(1)}, bf16[512,128]{1,0:T(8,128)(2,1)S(1)}, u32[]{:S(2)}, u32[]{:S(2)}) %collective-permute-start.17) | collective-permute-done | bytes 131104 | tf_op jit(solution)/shard_map/ppermute | solution.py:316
  93.0 2.9 %collective-permute-done.18.refs_2_ = bf16[512,128]{1,0:T(8,128)(2,1)S(1)} collective-permute-done((bf16[512,128]{1,0:T(8,128)(2,1)S(1)}, bf16[512,128]{1,0:T(8,128)(2,1)S(1)}, u32[]{:S(2)}, u32[]{:S(2)}) %collective-permute-start.18) | collective-permute-done | bytes 131104 | tf_op jit(solution)/shard_map/ppermute | solution.py:316
  95.9 2.6 %total.1 = bf16[2048,128]{1,0:T(8,128)(2,1)} custom-call(bf16[512,128]{1,0:T(8,128)(2,1)S(1)} %get-tuple-element.35.refs_0_, bf16[512,128]{1,0:T(8,128)(2,1)S(1)} %collective-permute-done.17.refs_1_, bf16[512,128]{1,0:T(8,128)(2,1)S(1)} %collective-permute-done.18.refs_2_, bf16[512,128]{1,0:T(8,128)(2,1)S(1)} %collective-permute-done.19.refs_3_, ...), custom_call_target="tpu_custom_call" | custom-call | tf_op jit(solution)/shard_map/total/pallas_call | solution.py:297
  (41 shorter events, 17.4 us)
Async XLA Ops:
  8.1 22.6 %collective-permute-start.11 = (bf16[2,512,512]{2,1,0:T(8,128)(2,1)S(1)}, bf16[2,512,512]{2,1,0:T(8,128)(2,1)S(1)}, u32[]{:S(2)}, u32[]{:S(2)}) collective-permute-start(bf16[2,512,512]{2,1,0:T(8,128)(2,1)S(1)} %pad_maximum_fusion.refs_12_.refs_2_), channel_id=1, source_target_pairs={{0,64},{4,196},{8,72},{12,204},{16,80},{20,212},{24,88},{28,220},{... | collective-permute-start | bytes 3145736 | tf_op jit(solution)/shard_map/ppermute | solution.py:329
  9.2 23.3 %collective-permute-start = (bf16[512,256]{1,0:T(8,128)(2,1)S(1)}, bf16[512,256]{1,0:T(8,128)(2,1)S(1)}, u32[]{:S(2)}, u32[]{:S(2)}) collective-permute-start(bf16[512,256]{1,0:T(8,128)(2,1)S(1)} %get-tuple-element.27.refs_0_), channel_id=1, source_target_pairs={{0,8},{4,12},{8,16},{12,20},{16,24},{20,28},{24,32},{28,36},{32,40... | collective-permute-start | bytes 786440 | tf_op jit(solution)/shard_map/ppermute | solution.py:312
  10.8 56.3 %collective-permute-start.13 = (bf16[2,512,512]{2,1,0:T(8,128)(2,1)S(1)}, bf16[2,512,512]{2,1,0:T(8,128)(2,1)S(1)}, u32[]{:S(2)}, u32[]{:S(2)}) collective-permute-start(bf16[2,512,512]{2,1,0:T(8,128)(2,1)S(1)} %pad_maximum_fusion.refs_12_.refs_2_), channel_id=1, source_target_pairs={{0,192},{4,68},{8,200},{12,76},{16,208},{20,84},{24,216},{28,92},{... | collective-permute-start | bytes 3145736 | tf_op jit(solution)/shard_map/ppermute | solution.py:329
  10.8 25.0 %collective-permute-start.1 = (bf16[512,256]{1,0:T(8,128)(2,1)S(1)}, bf16[512,256]{1,0:T(8,128)(2,1)S(1)}, u32[]{:S(2)}, u32[]{:S(2)}) collective-permute-start(bf16[512,256]{1,0:T(8,128)(2,1)S(1)} %get-tuple-element.27.refs_0_), channel_id=1, source_target_pairs={{0,56},{4,60},{8,0},{12,4},{16,8},{20,12},{24,16},{28,20},{32,24},... | collective-permute-start | bytes 786440 | tf_op jit(solution)/shard_map/ppermute | solution.py:312
  14.8 19.4 %collective-permute-start.5 = (bf16[512,256]{1,0:T(8,128)(2,1)S(1)}, bf16[512,256]{1,0:T(8,128)(2,1)S(1)}, u32[]{:S(2)}, u32[]{:S(2)}) collective-permute-start(bf16[512,256]{1,0:T(8,128)(2,1)S(1)} %get-tuple-element.28.refs_6_), channel_id=1, source_target_pairs={{0,56},{4,60},{8,0},{12,4},{16,8},{20,12},{24,16},{28,20},{32,24},... | collective-permute-start | bytes 786440 | tf_op jit(solution)/shard_map/ppermute | solution.py:312
  30.7 37.0 %collective-permute-start.12 = (bf16[2,512,512]{2,1,0:T(8,128)(2,1)S(1)}, bf16[2,512,512]{2,1,0:T(8,128)(2,1)S(1)}, u32[]{:S(2)}, u32[]{:S(2)}) collective-permute-start(bf16[2,512,512]{2,1,0:T(8,128)(2,1)S(1)} %collective-permute-done.11.refs_13_.refs_3_), channel_id=1, source_target_pairs={{0,64},{4,196},{8,72},{12,204},{16,80},{20,212},{24,88},{28,220},{... | collective-permute-start | bytes 3145736 | tf_op jit(solution)/shard_map/ppermute | solution.py:329
  32.5 14.3 %collective-permute-start.6 = (bf16[512,256]{1,0:T(8,128)(2,1)S(1)}, bf16[512,256]{1,0:T(8,128)(2,1)S(1)}, u32[]{:S(2)}, u32[]{:S(2)}) collective-permute-start(bf16[512,256]{1,0:T(8,128)(2,1)S(1)} %get-tuple-element.28.refs_6_), channel_id=1, source_target_pairs={{0,8},{4,12},{8,16},{12,20},{16,24},{20,28},{24,32},{28,36},{32,40... | collective-permute-start | bytes 786440 | tf_op jit(solution)/shard_map/ppermute | solution.py:312
  34.2 17.7 %collective-permute-start.2 = (bf16[512,256]{1,0:T(8,128)(2,1)S(1)}, bf16[512,256]{1,0:T(8,128)(2,1)S(1)}, u32[]{:S(2)}, u32[]{:S(2)}) collective-permute-start(bf16[512,256]{1,0:T(8,128)(2,1)S(1)} %collective-permute-done.refs_1_), channel_id=1, source_target_pairs={{0,8},{4,12},{8,16},{12,20},{16,24},{20,28},{24,32},{28,36},{32,40... | collective-permute-start | bytes 786440 | tf_op jit(solution)/shard_map/ppermute | solution.py:312
  35.8 16.0 %collective-permute-start.7 = (bf16[512,256]{1,0:T(8,128)(2,1)S(1)}, bf16[512,256]{1,0:T(8,128)(2,1)S(1)}, u32[]{:S(2)}, u32[]{:S(2)}) collective-permute-start(bf16[512,256]{1,0:T(8,128)(2,1)S(1)} %collective-permute-done.5.refs_7_), channel_id=1, source_target_pairs={{0,56},{4,60},{8,0},{12,4},{16,8},{20,12},{24,16},{28,20},{32,24},... | collective-permute-start | bytes 786440 | tf_op jit(solution)/shard_map/ppermute | solution.py:312
  46.9 8.2 %collective-permute-start.3 = (bf16[512,256]{1,0:T(8,128)(2,1)S(1)}, bf16[512,256]{1,0:T(8,128)(2,1)S(1)}, u32[]{:S(2)}, u32[]{:S(2)}) collective-permute-start(bf16[512,256]{1,0:T(8,128)(2,1)S(1)} %collective-permute-done.1.refs_2_), channel_id=1, source_target_pairs={{0,56},{4,60},{8,0},{12,4},{16,8},{20,12},{24,16},{28,20},{32,24},... | collective-permute-start | bytes 786440 | tf_op jit(solution)/shard_map/ppermute | solution.py:312
  51.8 8.8 %collective-permute-start.8 = (bf16[512,256]{1,0:T(8,128)(2,1)S(1)}, bf16[512,256]{1,0:T(8,128)(2,1)S(1)}, u32[]{:S(2)}, u32[]{:S(2)}) collective-permute-start(bf16[512,256]{1,0:T(8,128)(2,1)S(1)} %collective-permute-done.6.refs_8_), channel_id=1, source_target_pairs={{0,8},{4,12},{8,16},{12,20},{16,24},{20,28},{24,32},{28,36},{32,40... | collective-permute-start | bytes 786440 | tf_op jit(solution)/shard_map/ppermute | solution.py:312
  51.8 8.8 %collective-permute-start.9 = (bf16[512,256]{1,0:T(8,128)(2,1)S(1)}, bf16[512,256]{1,0:T(8,128)(2,1)S(1)}, u32[]{:S(2)}, u32[]{:S(2)}) collective-permute-start(bf16[512,256]{1,0:T(8,128)(2,1)S(1)} %collective-permute-done.7.refs_9_), channel_id=1, source_target_pairs={{0,56},{4,60},{8,0},{12,4},{16,8},{20,12},{24,16},{28,20},{32,24},... | collective-permute-start | bytes 786440 | tf_op jit(solution)/shard_map/ppermute | solution.py:312
  55.1 11.2 %collective-permute-start.4 = (bf16[512,256]{1,0:T(8,128)(2,1)S(1)}, bf16[512,256]{1,0:T(8,128)(2,1)S(1)}, u32[]{:S(2)}, u32[]{:S(2)}) collective-permute-start(bf16[512,256]{1,0:T(8,128)(2,1)S(1)} %collective-permute-done.2.refs_3_), channel_id=1, source_target_pairs={{0,8},{4,12},{8,16},{12,20},{16,24},{20,28},{24,32},{28,36},{32,40... | collective-permute-start | bytes 786440 | tf_op jit(solution)/shard_map/ppermute | solution.py:312
  60.6 11.9 %collective-permute-start.20 = (bf16[512,256]{1,0:T(8,128)(2,1)S(1)}, bf16[512,256]{1,0:T(8,128)(2,1)S(1)}, u32[]{:S(2)}, u32[]{:S(2)}) collective-permute-start(bf16[512,256]{1,0:T(8,128)(2,1)S(1)} %collective-permute-done.8.refs_10_), channel_id=1, source_target_pairs={{0,8},{4,12},{8,16},{12,20},{16,24},{20,28},{24,32},{28,36},{32,40... | collective-permute-start | bytes 786440 | tf_op jit(solution)/shard_map/ppermute | solution.py:312
  60.6 11.9 %collective-permute-start.21 = (bf16[512,256]{1,0:T(8,128)(2,1)S(1)}, bf16[512,256]{1,0:T(8,128)(2,1)S(1)}, u32[]{:S(2)}, u32[]{:S(2)}) collective-permute-start(bf16[512,256]{1,0:T(8,128)(2,1)S(1)} %collective-permute-done.9.refs_11_), channel_id=1, source_target_pairs={{0,56},{4,60},{8,0},{12,4},{16,8},{20,12},{24,16},{28,20},{32,24},... | collective-permute-start | bytes 786440 | tf_op jit(solution)/shard_map/ppermute | solution.py:312
  66.3 9.4 %collective-permute-start.14 = (bf16[512,256]{1,0:T(8,128)(2,1)S(1)}, bf16[512,256]{1,0:T(8,128)(2,1)S(1)}, u32[]{:S(2)}, u32[]{:S(2)}) collective-permute-start(bf16[512,256]{1,0:T(8,128)(2,1)S(1)} %collective-permute-done.3.refs_4_), channel_id=1, source_target_pairs={{0,56},{4,60},{8,0},{12,4},{16,8},{20,12},{24,16},{28,20},{32,24},... | collective-permute-start | bytes 786440 | tf_op jit(solution)/shard_map/ppermute | solution.py:312
  67.2 10.1 %collective-permute-start.15 = (bf16[512,256]{1,0:T(8,128)(2,1)S(1)}, bf16[512,256]{1,0:T(8,128)(2,1)S(1)}, u32[]{:S(2)}, u32[]{:S(2)}) collective-permute-start(bf16[512,256]{1,0:T(8,128)(2,1)S(1)} %collective-permute-done.4.refs_5_), channel_id=1, source_target_pairs={{0,8},{4,12},{8,16},{12,20},{16,24},{20,28},{24,32},{28,36},{32,40... | collective-permute-start | bytes 786440 | tf_op jit(solution)/shard_map/ppermute | solution.py:312
  77.8 7.2 %collective-permute-start.16 = (bf16[512,512]{1,0:T(8,128)(2,1)S(1)}, bf16[512,512]{1,0:T(8,128)(2,1)S(1)}, u32[]{:S(2)}, u32[]{:S(2)}) collective-permute-start(bf16[512,512]{1,0:T(8,128)(2,1)S(1)} %late_other.2), channel_id=1, source_target_pairs={{0,4},{4,0},{8,12},{12,8},{16,20},{20,16},{24,28},{28,24},{32,36},... | collective-permute-start | bytes 1572872 | tf_op jit(solution)/shard_map/ppermute | solution.py:320
  80.1 7.0 %collective-permute-start.23 = (bf16[512,128]{1,0:T(8,128)(2,1)S(1)}, bf16[512,128]{1,0:T(8,128)(2,1)S(1)}, u32[]{:S(2)}, u32[]{:S(2)}) collective-permute-start(bf16[512,128]{1,0:T(8,128)(2,1)S(1)} %get-tuple-element.42), channel_id=1, source_target_pairs={{0,1},{1,2},{2,3},{3,0},{4,5},{5,6},{6,7},{7,4},{8,9},{9,10},{10,1... | collective-permute-start | bytes 393224 | tf_op jit(solution)/shard_map/ppermute | solution.py:316
  81.4 8.9 %collective-permute-start.24 = (bf16[512,128]{1,0:T(8,128)(2,1)S(1)}, bf16[512,128]{1,0:T(8,128)(2,1)S(1)}, u32[]{:S(2)}, u32[]{:S(2)}) collective-permute-start(bf16[512,128]{1,0:T(8,128)(2,1)S(1)} %get-tuple-element.43), channel_id=1, source_target_pairs={{0,2},{1,3},{2,0},{3,1},{4,6},{5,7},{6,4},{7,5},{8,10},{9,11},{10,... | collective-permute-start | bytes 393224 | tf_op jit(solution)/shard_map/ppermute | solution.py:316
  83.9 6.5 %collective-permute-start.25 = (bf16[512,128]{1,0:T(8,128)(2,1)S(1)}, bf16[512,128]{1,0:T(8,128)(2,1)S(1)}, u32[]{:S(2)}, u32[]{:S(2)}) collective-permute-start(bf16[512,128]{1,0:T(8,128)(2,1)S(1)} %get-tuple-element.44), channel_id=1, source_target_pairs={{0,3},{1,0},{2,1},{3,2},{4,7},{5,4},{6,5},{7,6},{8,11},{9,8},{10,9... | collective-permute-start | bytes 393224 | tf_op jit(solution)/shard_map/ppermute | solution.py:316
  85.9 7.1 %collective-permute-start.17 = (bf16[512,128]{1,0:T(8,128)(2,1)S(1)}, bf16[512,128]{1,0:T(8,128)(2,1)S(1)}, u32[]{:S(2)}, u32[]{:S(2)}) collective-permute-start(bf16[512,128]{1,0:T(8,128)(2,1)S(1)} %get-tuple-element.36), channel_id=1, source_target_pairs={{0,1},{1,2},{2,3},{3,0},{4,5},{5,6},{6,7},{7,4},{8,9},{9,10},{10,1... | collective-permute-start | bytes 393224 | tf_op jit(solution)/shard_map/ppermute | solution.py:316
  86.3 9.7 %collective-permute-start.18 = (bf16[512,128]{1,0:T(8,128)(2,1)S(1)}, bf16[512,128]{1,0:T(8,128)(2,1)S(1)}, u32[]{:S(2)}, u32[]{:S(2)}) collective-permute-start(bf16[512,128]{1,0:T(8,128)(2,1)S(1)} %get-tuple-element.37), channel_id=1, source_target_pairs={{0,2},{1,3},{2,0},{3,1},{4,6},{5,7},{6,4},{7,5},{8,10},{9,11},{10,... | collective-permute-start | bytes 393224 | tf_op jit(solution)/shard_map/ppermute | solution.py:316
  87.2 8.8 %collective-permute-start.19 = (bf16[512,128]{1,0:T(8,128)(2,1)S(1)}, bf16[512,128]{1,0:T(8,128)(2,1)S(1)}, u32[]{:S(2)}, u32[]{:S(2)}) collective-permute-start(bf16[512,128]{1,0:T(8,128)(2,1)S(1)} %get-tuple-element.38), channel_id=1, source_target_pairs={{0,3},{1,0},{2,1},{3,2},{4,7},{5,4},{6,5},{7,6},{8,11},{9,8},{10,9... | collective-permute-start | bytes 393224 | tf_op jit(solution)/shard_map/ppermute | solution.py:316
  (4 other events, 22.6 us)

commit v3 on v2

--- a/solution.py
+++ b/solution.py
@@ -40,7 +40,7 @@
     )
 
 
-def left_kernel(x_ref, pat_ref, s_ref, t_ref, wide, buf, sem):
+def left_kernel(x_ref, pat_ref, out_ref, wide, buf, sem):
     a, b = place()
     rows, cols = buf.shape
     copy = pltpu.make_async_copy(
@@ -51,21 +51,18 @@
     wide[...] = widen(pat_ref[...], wide.shape[1])
     copy.wait()
     atoms = rows // BLOCK
-    half = rows // 2
     flags = wide[pl.ds(pl.multiple_of(a * atoms, atoms), atoms),
                  pl.ds(pl.multiple_of(b * cols, cols), cols)]
-    s_ref[...] = buf[:half, :] * tall(flags[: atoms // 2]).astype(BF16)
-    t_ref[...] = buf[half:, :] * tall(flags[atoms // 2:]).astype(BF16)
+    out_ref[...] = buf[...] * tall(flags).astype(BF16)
 
 
 def left_blocks(matrix, pattern):
     rows, cols = matrix.shape
-    out = jax.ShapeDtypeStruct((rows // 4, cols // 2), BF16)
     return pl.pallas_call(
         left_kernel,
-        out_shape=(out, out),
+        out_shape=jax.ShapeDtypeStruct((rows // 2, cols // 2), BF16),
         in_specs=[HBM, VM],
-        out_specs=(VM, VM),
+        out_specs=VM,
         scratch_shapes=[
             pltpu.VMEM((rows // BLOCK, cols), F32),
             pltpu.VMEM((rows // 2, cols // 2), BF16),
@@ -116,100 +113,81 @@
     )(matrix, pattern)
 
 
-def gather_rows(rights, steps, right, sems):
+def side():
+    return 1 - 2 * (lax.axis_index("col") % 2)
+
+
+def gather_rows(rights, steps, slots, right, sems):
     z = lax.axis_index("col") // 2
     r = lax.axis_index("row")
-    up = 1 - 2 * (lax.axis_index("col") % 2)
     deep = rights[0].shape[1] // 2
     wide = rights[0].shape[2]
-    slots = right.shape[1] // wide
     waits = []
     for i, step in enumerate(steps):
-        source = lax.rem(z - step + 8, 8)
-        away = lax.rem((r - source // 2) * up + 8, 4)
+        source = lax.rem(z - step * side() + 8, 8)
+        away = lax.rem((r - source // 2) * side() + 8, 4)
         low = pl.multiple_of(lax.rem(source, 2) * deep, deep)
         for j, ref in enumerate(rights):
             copies = [
                 pltpu.make_async_copy(
                     ref.at[slot, pl.ds(low, deep), :],
-                    right.at[pl.ds(i * deep, deep), pl.ds((slot if slots > 1 else 0) * wide, wide)],
-                    sems.at[i, slot])
-                for slot in range(2)
+                    right.at[pl.ds(i * deep, deep), pl.ds(k * wide, wide)],
+                    sems.at[i, k])
+                for k, slot in enumerate(slots)
             ]
 
             @pl.when(away == j)
             def _():
                 for copy in copies:
                     copy.start()
-        waits.append(copies)
+        waits += copies
     return waits
 
 
 def early_kernel(steps, *refs):
-    n = len(steps[0])
-    lefts = (refs[:n], refs[n:2 * n])
-    rights = refs[2 * n:2 * n + 4]
-    outs = refs[2 * n + 4:2 * n + 8]
-    left, right, lsem, rsem = refs[2 * n + 8:]
-    half, width = lefts[0][0].shape
-    cols = right.shape[2] // 2
-    waits = []
-    for part in range(2):
-        waits += gather_rows(rights, steps[part], right.at[part], rsem.at[part])
-        for i in range(n):
-            copy = pltpu.make_async_copy(
-                lefts[part][i], left.at[part, :, pl.ds(i * width, width)], lsem.at[part, i])
-            copy.start()
-            waits.append([copy])
-    for copies in waits:
-        for copy in copies:
-            copy.wait()
+    n = len(steps)
+    lefts, rights, outs = refs[:n], refs[n:n + 4], refs[n + 4:n + 8]
+    left, right, lsem, rsem = refs[n + 8:]
+    half, cols = outs[0].shape
+    width = lefts[0].shape[1]
+    waits = gather_rows(rights, steps, (0, 1), right, rsem)
+    for i in range(n):
+        waits.append(pltpu.make_async_copy(
+            lefts[i], left.at[:, pl.ds(i * width, width)], lsem.at[i]))
+        waits[-1].start()
+    for copy in waits:
+        copy.wait()
     for part in range(2):
         for slot in range(2):
             outs[2 * part + slot][...] = jnp.dot(
-                left[part], right[part, :, slot * cols:(slot + 1) * cols],
+                left[part * half:(part + 1) * half, :],
+                right[:, slot * cols:(slot + 1) * cols],
                 preferred_element_type=F32)
 
 
 def early(lefts, steps, rights):
-    half, width = lefts[0].shape
+    rows, width = lefts[0].shape
     cols = rights[0].shape[2]
-    n = len(steps[0])
-    out = jax.ShapeDtypeStruct((half, cols), F32)
+    n = len(steps)
+    out = jax.ShapeDtypeStruct((rows // 2, cols), F32)
     return pl.pallas_call(
         functools.partial(early_kernel, steps),
         out_shape=(out,) * 4,
-        in_specs=[ANY] * (len(lefts) + 4),
+        in_specs=[ANY] * (n + 4),
         out_specs=(VM,) * 4,
         scratch_shapes=[
-            pltpu.VMEM((2, half, n * width), BF16),
-            pltpu.VMEM((2, n * width, 2 * cols), BF16),
-            pltpu.SemaphoreType.DMA((2, n)),
-            pltpu.SemaphoreType.DMA((2, n, 2)),
-        ],
-        compiler_params=vmem(20),
+            pltpu.VMEM((rows, n * width), BF16),
+            pltpu.VMEM((n * width, 2 * cols), BF16),
+            pltpu.SemaphoreType.DMA((n,)),
+            pltpu.SemaphoreType.DMA((n, 2)),
+        ],
+        compiler_params=vmem(16),
         name="early",
     )(*lefts, *rights)
 
 
 def late_sum(slot, steps, acc_ref, lefts, rights, right, sems):
-    z = lax.axis_index("col") // 2
-    r = lax.axis_index("row")
-    up = 1 - 2 * (lax.axis_index("col") % 2)
-    deep = lefts[0].shape[1]
-    waits = []
-    for i, step in enumerate(steps):
-        source = lax.rem(z - step + 8, 8)
-        away = lax.rem((r - source // 2) * up + 8, 4)
-        low = pl.multiple_of(lax.rem(source, 2) * deep, deep)
-        for j, ref in enumerate(rights):
-            copy = pltpu.make_async_copy(
-                ref.at[slot, pl.ds(low, deep), :], right.at[pl.ds(i * deep, deep), :], sems.at[i])
-
-            @pl.when(away == j)
-            def _():
-                copy.start()
-        waits.append(copy)
+    waits = gather_rows(rights, steps, (slot,), right, sems)
     left = jnp.concatenate([ref[...] for ref in lefts], axis=1)
     for copy in waits:
         copy.wait()
@@ -232,7 +210,7 @@
         out_specs=VM,
         scratch_shapes=[
             pltpu.VMEM((len(lefts) * deep, cols), BF16),
-            pltpu.SemaphoreType.DMA((len(lefts),)),
+            pltpu.SemaphoreType.DMA((len(lefts), 1)),
         ],
         compiler_params=vmem(8),
         name="late_other",
@@ -263,7 +241,7 @@
         scratch_shapes=[
             pltpu.VMEM((len(lefts) * deep, cols), BF16),
             pltpu.VMEM((half, cols), F32),
-            pltpu.SemaphoreType.DMA((len(lefts),)),
+            pltpu.SemaphoreType.DMA((len(lefts), 1)),
         ],
         compiler_params=vmem(8),
         name="late_own",
@@ -308,8 +286,9 @@
     )(*pieces, keep)
 
 
-def along_z(x, d):
-    return lax.ppermute(x, "col", [(c, (c // 2 + d) % 8 * 2 + c % 2) for c in range(16)])
+def stream(x, d):
+    return lax.ppermute(
+        x, "col", [(c, (c // 2 + (d if c % 2 == 0 else -d)) % 8 * 2 + c % 2) for c in range(16)])
 
 
 def along(x, axis, d):
@@ -332,31 +311,32 @@
 def on_device(matrix, pattern, keep):
     pattern_t = pattern.T
     matrix = pltpu.with_memory_space_constraint(matrix, pltpu.HBM)
-    s, t = left_blocks(matrix, pattern_t)
-    s, t, matrix, pattern_t = lax.optimization_barrier((s, t, matrix, pattern_t))
-    left = ({0: s}, {0: t})
-    for step in (1, 2, 3, 4):
-        for part in range(2):
-            for way in (1, -1):
-                if step < 4 or way == (1, -1)[part]:
-                    at = way * step
-                    left[part][at] = along_z(left[part][at - way], way)
-
+    block = left_blocks(matrix, pattern_t)
+    block, matrix, pattern_t = lax.optimization_barrier((block, matrix, pattern_t))
     mine, theirs = right_blocks(matrix, pattern_t)
     both = jnp.stack([mine, swap(theirs)])
-    below = turn(both, 1)
-    above = turn(both, -1)
-    far = turn(below, 1)
-    rights = [both, below, far, above]
-
-    order = ((0, 1, -1, 2, -2, 3), (0, -1, 1, -2, 2, -3))
-    last = ((-3, 4), (3, -4))
-    acc = early([left[p][i] for p in range(2) for i in order[p]], order, rights)
+
+    up, down = stream(block, 1), stream(block, -1)
+    near = turn(both, 1)
+    blocks = {0: block, 1: up, -1: down}
+    up, down, both = lax.optimization_barrier((up, down, both))
+    up, down, other = stream(up, 1), stream(down, -1), turn(both, -1)
+    blocks.update({2: up, -2: down})
+    up, down, near = lax.optimization_barrier((up, down, near))
+    far = turn(near, 1)
+    up, down = stream(up, 1), stream(down, -1)
+    blocks.update({3: up, -3: down})
+    up, down, other, far = lax.optimization_barrier((up, down, other, far))
+    half = up.shape[0] // 2
+    ends = [stream(up[p * half:(p + 1) * half], 1) for p in range(2)]
+    rights = [both, near, far, other]
+
+    first, last = (0, 1, -1, 2, -2, 3, -3), (4,)
+    acc = early([blocks[i] for i in first], first, rights)
     pieces = []
     for p in range(2):
-        blocks = [left[p][i] for i in last[p]]
-        other = swap(late_other(acc[2 * p + 1], blocks, last[p], rights))
-        mine = late_own(acc[2 * p], other, blocks, last[p], rights)
+        other = swap(late_other(acc[2 * p + 1], [ends[p]], last, rights))
+        mine = late_own(acc[2 * p], other, [ends[p]], last, rights)
         pieces += [mine[0]] + [along(mine[d], "layer", d) for d in range(1, 4)]
     return total(pieces, keep.T)
 

time: 98.9 us -> 84.5 us (0.85)
  starting transfers between devices: 41.1 us -> 29.5 us
  waiting for transfers between devices: 43.8 us -> 41.5 us
    ppermute x3, waiting for transfers between devices: 14.5 us -> 0.01 us  [turn(): return lax.ppermute(x, ('row', 'col'), pairs)]
    ppermute x14 -> x8, starting transfers between devices: 23.1 us -> 9.33 us  [stream(): lax.ppermute(x, 'col', [(c, (c // 2 + (d if c % 2 == 0 else -d)) % 8 * 2...]
    ppermute x14 -> x8, waiting for transfers between devices: 20.6 us -> 34.1 us  [stream(): lax.ppermute(x, 'col', [(c, (c // 2 + (d if c % 2 == 0 else -d)) % 8 * 2...]
    ppermute x3, starting transfers between devices: 2.89 us -> 7.14 us  [turn(): return lax.ppermute(x, ('row', 'col'), pairs)]
    ppermute x3, starting transfers between devices: 7.3 us -> 5.25 us  [swap(): return lax.ppermute(x, 'col', [(c, c ^ 1) for c in range(16)])]
    ppermute x3, waiting for transfers between devices: 1.54 us -> 0.01 us  [swap(): return lax.ppermute(x, 'col', [(c, c ^ 1) for c in range(16)])]
  transfers between devices with their start and end apart: 26 -> 20, of which waited for: 11 -> 10; matrix products, arithmetic and copies ran while one was open for 0% -> 0% of each run, Pallas kernels for 8% -> 8%
where the time goes in v3:
time: 84.5 us; the launch traced here: 84.3 us
  waiting for transfers between devices  41.5 us (49%)
  starting transfers between devices  29.5 us (35%)
  Pallas kernels  12.2 us (14%)
    ppermute x8, waiting for transfers between devices, stream(): lax.ppermute(x, 'col', [(c, (c // 2 + (d if c % 2 == 0 else -d)) % 8 * 2...  34.1 us
    ppermute x8, starting transfers between devices, stream(): lax.ppermute(x, 'col', [(c, (c // 2 + (d if c % 2 == 0 else -d)) % 8 * 2...  9.33 us
    ppermute x6, starting transfers between devices, along(): return lax.ppermute(x, axis, [(i, (i + d) % 4) for i in range(4)])  7.79 us
    ppermute x6, waiting for transfers between devices, along(): return lax.ppermute(x, axis, [(i, (i + d) % 4) for i in range(4)])  7.37 us
    ppermute x3, starting transfers between devices, turn(): return lax.ppermute(x, ('row', 'col'), pairs)  7.14 us
    ppermute x3, starting transfers between devices, swap(): return lax.ppermute(x, 'col', [(c, c ^ 1) for c in range(16)])  5.25 us
    pallas_call x1, Pallas kernels, early(): pl.pallas_call(functools.partial(early_kernel, steps), out_shape=(out,) *...  5.08 us
    pallas_call x1, Pallas kernels, total(): pl.pallas_call(total_kernel, out_shape=jax.ShapeDtypeStruct((4 * half, wi...  2.61 us
  transfers between devices with their start and end apart: 20, of which 10 were waited for; matrix products, arithmetic and copies ran while one was open for 0% of the time, Pallas kernels for 8%

profile of v3, /device:TPU:1, one launch (start us, length us, event | category | flops | bytes accessed | tf_op | source)
XLA Modules:
  0.0 84.3 jit_solution(18274058467568990464)
XLA Ops:
  1.8 1.3 %right_blocks.1 = (bf16[512,512]{1,0:T(8,128)(2,1)S(1)}, bf16[512,512]{1,0:T(8,128)(2,1)S(1)}) custom-call(bf16[2048,512]{1,0:T(8,128)(2,1)} %x_ref.2, s32[16,64]{1,0:T(8,128)S(1)} %bitcast.6), custom_call_target="tpu_custom_call" | custom-call | tf_op jit(solution)/shard_map/right_blocks/pallas_call | solution.py:101
  3.2 3.3 %collective-permute-start.2 = (bf16[512,512]{1,0:T(8,128)(2,1)S(1)}, bf16[512,512]{1,0:T(8,128)(2,1)S(1)}, u32[]{:S(2)}, u32[]{:S(2)}) collective-permute-start(bf16[512,512]{1,0:T(8,128)(2,1)S(1)} %get-tuple-element.35), channel_id=1, source_target_pairs={{0,4},{4,0},{8,12},{12,8},{16,20},{20,16},{24,28},{28,24},{32,36},... | collective-permute-start | bytes 1572872 | tf_op jit(solution)/shard_map/ppermute | solution.py:299
  6.5 3.8 %collective-permute-start = (bf16[1024,256]{1,0:T(8,128)(2,1)S(1)}, bf16[1024,256]{1,0:T(8,128)(2,1)S(1)}, u32[]{:S(2)}, u32[]{:S(2)}) collective-permute-start(bf16[1024,256]{1,0:T(8,128)(2,1)S(1)} %left_blocks.1.refs_0_), channel_id=1, source_target_pairs={{0,8},{4,60},{8,16},{12,4},{16,24},{20,12},{24,32},{28,20},{32,40}... | collective-permute-start | bytes 1572872 | tf_op jit(solution)/shard_map/ppermute | solution.py:290
  10.5 2.8 %collective-permute-start.5 = (bf16[2,512,512]{2,1,0:T(8,128)(2,1)S(1)}, bf16[2,512,512]{2,1,0:T(8,128)(2,1)S(1)}, u32[]{:S(2)}, u32[]{:S(2)}) collective-permute-start(bf16[2,512,512]{2,1,0:T(8,128)(2,1)S(1)} %pad_maximum_fusion.refs_7_.refs_1_), channel_id=1, source_target_pairs={{0,64},{4,196},{8,72},{12,204},{16,80},{20,212},{24,88},{28,220},{... | collective-permute-start | bytes 3145736 | tf_op jit(solution)/shard_map/ppermute | solution.py:308
  13.3 8.2 %collective-permute-done.refs_1_ = bf16[1024,256]{1,0:T(8,128)(2,1)S(1)} collective-permute-done((bf16[1024,256]{1,0:T(8,128)(2,1)S(1)}, bf16[1024,256]{1,0:T(8,128)(2,1)S(1)}, u32[]{:S(2)}, u32[]{:S(2)}) %collective-permute-start) | collective-permute-done | bytes 524320 | tf_op jit(solution)/shard_map/ppermute | solution.py:290
  21.5 1.6 %collective-permute-done.1.refs_2_ = bf16[1024,256]{1,0:T(8,128)(2,1)S(1)} collective-permute-done((bf16[1024,256]{1,0:T(8,128)(2,1)S(1)}, bf16[1024,256]{1,0:T(8,128)(2,1)S(1)}, u32[]{:S(2)}, u32[]{:S(2)}) %collective-permute-start.1) | collective-permute-done | bytes 524320 | tf_op jit(solution)/shard_map/ppermute | solution.py:290
  23.1 1.8 %collective-permute-start.3 = (bf16[1024,256]{1,0:T(8,128)(2,1)S(1)}, bf16[1024,256]{1,0:T(8,128)(2,1)S(1)}, u32[]{:S(2)}, u32[]{:S(2)}) collective-permute-start(bf16[1024,256]{1,0:T(8,128)(2,1)S(1)} %collective-permute-done.refs_1_), channel_id=1, source_target_pairs={{0,8},{4,60},{8,16},{12,4},{16,24},{20,12},{24,32},{28,20},{32,40}... | collective-permute-start | bytes 1572872 | tf_op jit(solution)/shard_map/ppermute | solution.py:290
  24.9 1.3 %collective-permute-start.8 = (bf16[2,512,512]{2,1,0:T(8,128)(2,1)S(1)}, bf16[2,512,512]{2,1,0:T(8,128)(2,1)S(1)}, u32[]{:S(2)}, u32[]{:S(2)}) collective-permute-start(bf16[2,512,512]{2,1,0:T(8,128)(2,1)S(1)} %pad_maximum_fusion.refs_7_.refs_1_), channel_id=1, source_target_pairs={{0,192},{4,68},{8,200},{12,76},{16,208},{20,84},{24,216},{28,92},{... | collective-permute-start | bytes 3145736 | tf_op jit(solution)/shard_map/ppermute | solution.py:308
  26.2 10.7 %collective-permute-done.3.refs_3_ = bf16[1024,256]{1,0:T(8,128)(2,1)S(1)} collective-permute-done((bf16[1024,256]{1,0:T(8,128)(2,1)S(1)}, bf16[1024,256]{1,0:T(8,128)(2,1)S(1)}, u32[]{:S(2)}, u32[]{:S(2)}) %collective-permute-start.3) | collective-permute-done | bytes 524320 | tf_op jit(solution)/shard_map/ppermute | solution.py:290
  36.9 1.4 %collective-permute-done.4.refs_4_ = bf16[1024,256]{1,0:T(8,128)(2,1)S(1)} collective-permute-done((bf16[1024,256]{1,0:T(8,128)(2,1)S(1)}, bf16[1024,256]{1,0:T(8,128)(2,1)S(1)}, u32[]{:S(2)}, u32[]{:S(2)}) %collective-permute-start.4) | collective-permute-done | bytes 524320 | tf_op jit(solution)/shard_map/ppermute | solution.py:290
  38.3 3.0 %collective-permute-start.9 = (bf16[2,512,512]{2,1,0:T(8,128)(2,1)S(1)}, bf16[2,512,512]{2,1,0:T(8,128)(2,1)S(1)}, u32[]{:S(2)}, u32[]{:S(2)}) collective-permute-start(bf16[2,512,512]{2,1,0:T(8,128)(2,1)S(1)} %collective-permute-done.5.refs_8_.refs_2_), channel_id=1, source_target_pairs={{0,64},{4,196},{8,72},{12,204},{16,80},{20,212},{24,88},{28,220},{... | collective-permute-start | bytes 3145736 | tf_op jit(solution)/shard_map/ppermute | solution.py:308
  41.5 1.3 %collective-permute-start.7 = (bf16[1024,256]{1,0:T(8,128)(2,1)S(1)}, bf16[1024,256]{1,0:T(8,128)(2,1)S(1)}, u32[]{:S(2)}, u32[]{:S(2)}) collective-permute-start(bf16[1024,256]{1,0:T(8,128)(2,1)S(1)} %collective-permute-done.4.refs_4_), channel_id=1, source_target_pairs={{0,56},{4,12},{8,0},{12,20},{16,8},{20,28},{24,16},{28,36},{32,24}... | collective-permute-start | bytes 1572872 | tf_op jit(solution)/shard_map/ppermute | solution.py:290
  42.8 10.3 %collective-permute-done.6.refs_5_ = bf16[1024,256]{1,0:T(8,128)(2,1)S(1)} collective-permute-done((bf16[1024,256]{1,0:T(8,128)(2,1)S(1)}, bf16[1024,256]{1,0:T(8,128)(2,1)S(1)}, u32[]{:S(2)}, u32[]{:S(2)}) %collective-permute-start.6) | collective-permute-done | bytes 524320 | tf_op jit(solution)/shard_map/ppermute | solution.py:290
  53.1 1.4 %collective-permute-done.7.refs_6_ = bf16[1024,256]{1,0:T(8,128)(2,1)S(1)} collective-permute-done((bf16[1024,256]{1,0:T(8,128)(2,1)S(1)}, bf16[1024,256]{1,0:T(8,128)(2,1)S(1)}, u32[]{:S(2)}, u32[]{:S(2)}) %collective-permute-start.7) | collective-permute-done | bytes 524320 | tf_op jit(solution)/shard_map/ppermute | solution.py:290
  54.5 2.1 %collective-permute-start.15 = (bf16[512,256]{1,0:T(8,128)(2,1)S(1)}, bf16[512,256]{1,0:T(8,128)(2,1)S(1)}, u32[]{:S(2)}, u32[]{:S(2)}) collective-permute-start(bf16[512,256]{1,0:T(8,128)(2,1)S(1)} %get-tuple-element.57), channel_id=1, source_target_pairs={{0,8},{4,60},{8,16},{12,4},{16,24},{20,12},{24,32},{28,20},{32,40}... | collective-permute-start | bytes 786440 | tf_op jit(solution)/shard_map/ppermute | solution.py:290
  56.7 5.1 %early.1 = (f32[512,512]{1,0:T(8,128)S(1)}, f32[512,512]{1,0:T(8,128)S(1)}, f32[512,512]{1,0:T(8,128)S(1)}, f32[512,512]{1,0:T(8,128)S(1)}) custom-call(bf16[1024,256]{1,0:T(8,128)(2,1)S(1)} %left_blocks.1.refs_0_, bf16[1024,256]{1,0:T(8,128)(2,1)S(1)} %collective-permute-done.refs_1_, bf16[1024,256]{1,0:T(8,128)(2,1)S(1)} %collective-permute-done.1.refs_2_, ...), custom_call_target="tpu_custom_call" | custom-call | tf_op jit(solution)/shard_map/early/pallas_call | solution.py:173
  63.2 1.8 %collective-permute-start.11 = (bf16[512,512]{1,0:T(8,128)(2,1)S(1)}, bf16[512,512]{1,0:T(8,128)(2,1)S(1)}, u32[]{:S(2)}, u32[]{:S(2)}) collective-permute-start(bf16[512,512]{1,0:T(8,128)(2,1)S(1)} %late_other.2), channel_id=1, source_target_pairs={{0,4},{4,0},{8,12},{12,8},{16,20},{20,16},{24,28},{28,24},{32,36},... | collective-permute-start | bytes 1572872 | tf_op jit(solution)/shard_map/ppermute | solution.py:299
  65.7 1.3 %collective-permute-start.17 = (bf16[512,128]{1,0:T(8,128)(2,1)S(1)}, bf16[512,128]{1,0:T(8,128)(2,1)S(1)}, u32[]{:S(2)}, u32[]{:S(2)}) collective-permute-start(bf16[512,128]{1,0:T(8,128)(2,1)S(1)} %get-tuple-element.54), channel_id=1, source_target_pairs={{0,1},{1,2},{2,3},{3,0},{4,5},{5,6},{6,7},{7,4},{8,9},{9,10},{10,1... | collective-permute-start | bytes 393224 | tf_op jit(solution)/shard_map/ppermute | solution.py:295
  67.0 2.5 %collective-permute-start.18 = (bf16[512,128]{1,0:T(8,128)(2,1)S(1)}, bf16[512,128]{1,0:T(8,128)(2,1)S(1)}, u32[]{:S(2)}, u32[]{:S(2)}) collective-permute-start(bf16[512,128]{1,0:T(8,128)(2,1)S(1)} %get-tuple-element.55), channel_id=1, source_target_pairs={{0,2},{1,3},{2,0},{3,1},{4,6},{5,7},{6,4},{7,5},{8,10},{9,11},{10,... | collective-permute-start | bytes 393224 | tf_op jit(solution)/shard_map/ppermute | solution.py:295
  72.5 1.6 %collective-permute-start.14 = (bf16[512,128]{1,0:T(8,128)(2,1)S(1)}, bf16[512,128]{1,0:T(8,128)(2,1)S(1)}, u32[]{:S(2)}, u32[]{:S(2)}) collective-permute-start(bf16[512,128]{1,0:T(8,128)(2,1)S(1)} %get-tuple-element.50), channel_id=1, source_target_pairs={{0,3},{1,0},{2,1},{3,2},{4,7},{5,4},{6,5},{7,6},{8,11},{9,8},{10,9... | collective-permute-start | bytes 393224 | tf_op jit(solution)/shard_map/ppermute | solution.py:295
  74.2 1.8 %collective-permute-done.18.refs_6_ = bf16[512,128]{1,0:T(8,128)(2,1)S(1)} collective-permute-done((bf16[512,128]{1,0:T(8,128)(2,1)S(1)}, bf16[512,128]{1,0:T(8,128)(2,1)S(1)}, u32[]{:S(2)}, u32[]{:S(2)}) %collective-permute-start.18) | collective-permute-done | bytes 131104 | tf_op jit(solution)/shard_map/ppermute | solution.py:295
  75.9 2.9 %collective-permute-done.12.refs_1_ = bf16[512,128]{1,0:T(8,128)(2,1)S(1)} collective-permute-done((bf16[512,128]{1,0:T(8,128)(2,1)S(1)}, bf16[512,128]{1,0:T(8,128)(2,1)S(1)}, u32[]{:S(2)}, u32[]{:S(2)}) %collective-permute-start.12) | collective-permute-done | bytes 131104 | tf_op jit(solution)/shard_map/ppermute | solution.py:295
  78.9 2.7 %collective-permute-done.13.refs_2_ = bf16[512,128]{1,0:T(8,128)(2,1)S(1)} collective-permute-done((bf16[512,128]{1,0:T(8,128)(2,1)S(1)}, bf16[512,128]{1,0:T(8,128)(2,1)S(1)}, u32[]{:S(2)}, u32[]{:S(2)}) %collective-permute-start.13) | collective-permute-done | bytes 131104 | tf_op jit(solution)/shard_map/ppermute | solution.py:295
  81.5 2.6 %total.1 = bf16[2048,128]{1,0:T(8,128)(2,1)} custom-call(bf16[512,128]{1,0:T(8,128)(2,1)S(1)} %get-tuple-element.47.refs_0_, bf16[512,128]{1,0:T(8,128)(2,1)S(1)} %collective-permute-done.12.refs_1_, bf16[512,128]{1,0:T(8,128)(2,1)S(1)} %collective-permute-done.13.refs_2_, bf16[512,128]{1,0:T(8,128)(2,1)S(1)} %collective-permute-done.14.refs_3_, ...), custom_call_target="tpu_custom_call" | custom-call | tf_op jit(solution)/shard_map/total/pallas_call | solution.py:275
  (32 shorter events, 7.4 us)
Async XLA Ops:
  0.0 0.7 copy-start
  0.7 1.1 %copy-start.1 = (s32[64,16]{0,1:T(8,128)S(1)}, s32[64,16]{0,1:T(8,128)}, u32[]{:S(2)}) copy-start(s32[64,16]{0,1:T(8,128)} %param.4) | copy-start | bytes 12292
  3.2 7.2 %collective-permute-start.2 = (bf16[512,512]{1,0:T(8,128)(2,1)S(1)}, bf16[512,512]{1,0:T(8,128)(2,1)S(1)}, u32[]{:S(2)}, u32[]{:S(2)}) collective-permute-start(bf16[512,512]{1,0:T(8,128)(2,1)S(1)} %get-tuple-element.35), channel_id=1, source_target_pairs={{0,4},{4,0},{8,12},{12,8},{16,20},{20,16},{24,28},{28,24},{32,36},... | collective-permute-start | bytes 1572872 | tf_op jit(solution)/shard_map/ppermute | solution.py:299
  6.5 15.0 %collective-permute-start = (bf16[1024,256]{1,0:T(8,128)(2,1)S(1)}, bf16[1024,256]{1,0:T(8,128)(2,1)S(1)}, u32[]{:S(2)}, u32[]{:S(2)}) collective-permute-start(bf16[1024,256]{1,0:T(8,128)(2,1)S(1)} %left_blocks.1.refs_0_), channel_id=1, source_target_pairs={{0,8},{4,60},{8,16},{12,4},{16,24},{20,12},{24,32},{28,20},{32,40}... | collective-permute-start | bytes 1572872 | tf_op jit(solution)/shard_map/ppermute | solution.py:290
  10.4 12.8 %collective-permute-start.1 = (bf16[1024,256]{1,0:T(8,128)(2,1)S(1)}, bf16[1024,256]{1,0:T(8,128)(2,1)S(1)}, u32[]{:S(2)}, u32[]{:S(2)}) collective-permute-start(bf16[1024,256]{1,0:T(8,128)(2,1)S(1)} %left_blocks.1.refs_0_), channel_id=1, source_target_pairs={{0,56},{4,12},{8,0},{12,20},{16,8},{20,28},{24,16},{28,36},{32,24}... | collective-permute-start | bytes 1572872 | tf_op jit(solution)/shard_map/ppermute | solution.py:290
  10.5 27.8 %collective-permute-start.5 = (bf16[2,512,512]{2,1,0:T(8,128)(2,1)S(1)}, bf16[2,512,512]{2,1,0:T(8,128)(2,1)S(1)}, u32[]{:S(2)}, u32[]{:S(2)}) collective-permute-start(bf16[2,512,512]{2,1,0:T(8,128)(2,1)S(1)} %pad_maximum_fusion.refs_7_.refs_1_), channel_id=1, source_target_pairs={{0,64},{4,196},{8,72},{12,204},{16,80},{20,212},{24,88},{28,220},{... | collective-permute-start | bytes 3145736 | tf_op jit(solution)/shard_map/ppermute | solution.py:308
  23.1 13.8 %collective-permute-start.3 = (bf16[1024,256]{1,0:T(8,128)(2,1)S(1)}, bf16[1024,256]{1,0:T(8,128)(2,1)S(1)}, u32[]{:S(2)}, u32[]{:S(2)}) collective-permute-start(bf16[1024,256]{1,0:T(8,128)(2,1)S(1)} %collective-permute-done.refs_1_), channel_id=1, source_target_pairs={{0,8},{4,60},{8,16},{12,4},{16,24},{20,12},{24,32},{28,20},{32,40}... | collective-permute-start | bytes 1572872 | tf_op jit(solution)/shard_map/ppermute | solution.py:290
  24.9 13.3 %collective-permute-start.4 = (bf16[1024,256]{1,0:T(8,128)(2,1)S(1)}, bf16[1024,256]{1,0:T(8,128)(2,1)S(1)}, u32[]{:S(2)}, u32[]{:S(2)}) collective-permute-start(bf16[1024,256]{1,0:T(8,128)(2,1)S(1)} %collective-permute-done.1.refs_2_), channel_id=1, source_target_pairs={{0,56},{4,12},{8,0},{12,20},{16,8},{20,28},{24,16},{28,36},{32,24}... | collective-permute-start | bytes 1572872 | tf_op jit(solution)/shard_map/ppermute | solution.py:290
  24.9 17.8 %collective-permute-start.8 = (bf16[2,512,512]{2,1,0:T(8,128)(2,1)S(1)}, bf16[2,512,512]{2,1,0:T(8,128)(2,1)S(1)}, u32[]{:S(2)}, u32[]{:S(2)}) collective-permute-start(bf16[2,512,512]{2,1,0:T(8,128)(2,1)S(1)} %pad_maximum_fusion.refs_7_.refs_1_), channel_id=1, source_target_pairs={{0,192},{4,68},{8,200},{12,76},{16,208},{20,84},{24,216},{28,92},{... | collective-permute-start | bytes 3145736 | tf_op jit(solution)/shard_map/ppermute | solution.py:308
  38.3 16.2 %collective-permute-start.9 = (bf16[2,512,512]{2,1,0:T(8,128)(2,1)S(1)}, bf16[2,512,512]{2,1,0:T(8,128)(2,1)S(1)}, u32[]{:S(2)}, u32[]{:S(2)}) collective-permute-start(bf16[2,512,512]{2,1,0:T(8,128)(2,1)S(1)} %collective-permute-done.5.refs_8_.refs_2_), channel_id=1, source_target_pairs={{0,64},{4,196},{8,72},{12,204},{16,80},{20,212},{24,88},{28,220},{... | collective-permute-start | bytes 3145736 | tf_op jit(solution)/shard_map/ppermute | solution.py:308
  41.3 11.8 %collective-permute-start.6 = (bf16[1024,256]{1,0:T(8,128)(2,1)S(1)}, bf16[1024,256]{1,0:T(8,128)(2,1)S(1)}, u32[]{:S(2)}, u32[]{:S(2)}) collective-permute-start(bf16[1024,256]{1,0:T(8,128)(2,1)S(1)} %collective-permute-done.3.refs_3_), channel_id=1, source_target_pairs={{0,8},{4,60},{8,16},{12,4},{16,24},{20,12},{24,32},{28,20},{32,40}... | collective-permute-start | bytes 1572872 | tf_op jit(solution)/shard_map/ppermute | solution.py:290
  41.5 12.9 %collective-permute-start.7 = (bf16[1024,256]{1,0:T(8,128)(2,1)S(1)}, bf16[1024,256]{1,0:T(8,128)(2,1)S(1)}, u32[]{:S(2)}, u32[]{:S(2)}) collective-permute-start(bf16[1024,256]{1,0:T(8,128)(2,1)S(1)} %collective-permute-done.4.refs_4_), channel_id=1, source_target_pairs={{0,56},{4,12},{8,0},{12,20},{16,8},{20,28},{24,16},{28,36},{32,24}... | collective-permute-start | bytes 1572872 | tf_op jit(solution)/shard_map/ppermute | solution.py:290
  54.5 7.3 %collective-permute-start.15 = (bf16[512,256]{1,0:T(8,128)(2,1)S(1)}, bf16[512,256]{1,0:T(8,128)(2,1)S(1)}, u32[]{:S(2)}, u32[]{:S(2)}) collective-permute-start(bf16[512,256]{1,0:T(8,128)(2,1)S(1)} %get-tuple-element.57), channel_id=1, source_target_pairs={{0,8},{4,60},{8,16},{12,4},{16,24},{20,12},{24,32},{28,20},{32,40}... | collective-permute-start | bytes 786440 | tf_op jit(solution)/shard_map/ppermute | solution.py:290
  56.6 6.3 %collective-permute-start.10 = (bf16[512,256]{1,0:T(8,128)(2,1)S(1)}, bf16[512,256]{1,0:T(8,128)(2,1)S(1)}, u32[]{:S(2)}, u32[]{:S(2)}) collective-permute-start(bf16[512,256]{1,0:T(8,128)(2,1)S(1)} %get-tuple-element.58), channel_id=1, source_target_pairs={{0,8},{4,60},{8,16},{12,4},{16,24},{20,12},{24,32},{28,20},{32,40}... | collective-permute-start | bytes 786440 | tf_op jit(solution)/shard_map/ppermute | solution.py:290
  62.2 2.9 %collective-permute-start.16 = (bf16[512,512]{1,0:T(8,128)(2,1)S(1)}, bf16[512,512]{1,0:T(8,128)(2,1)S(1)}, u32[]{:S(2)}, u32[]{:S(2)}) collective-permute-start(bf16[512,512]{1,0:T(8,128)(2,1)S(1)} %late_other.3), channel_id=1, source_target_pairs={{0,4},{4,0},{8,12},{12,8},{16,20},{20,16},{24,28},{28,24},{32,36},... | collective-permute-start | bytes 1572872 | tf_op jit(solution)/shard_map/ppermute | solution.py:299
  63.2 7.4 %collective-permute-start.11 = (bf16[512,512]{1,0:T(8,128)(2,1)S(1)}, bf16[512,512]{1,0:T(8,128)(2,1)S(1)}, u32[]{:S(2)}, u32[]{:S(2)}) collective-permute-start(bf16[512,512]{1,0:T(8,128)(2,1)S(1)} %late_other.2), channel_id=1, source_target_pairs={{0,4},{4,0},{8,12},{12,8},{16,20},{20,16},{24,28},{28,24},{32,36},... | collective-permute-start | bytes 1572872 | tf_op jit(solution)/shard_map/ppermute | solution.py:299
  65.7 6.8 %collective-permute-start.17 = (bf16[512,128]{1,0:T(8,128)(2,1)S(1)}, bf16[512,128]{1,0:T(8,128)(2,1)S(1)}, u32[]{:S(2)}, u32[]{:S(2)}) collective-permute-start(bf16[512,128]{1,0:T(8,128)(2,1)S(1)} %get-tuple-element.54), channel_id=1, source_target_pairs={{0,1},{1,2},{2,3},{3,0},{4,5},{5,6},{6,7},{7,4},{8,9},{9,10},{10,1... | collective-permute-start | bytes 393224 | tf_op jit(solution)/shard_map/ppermute | solution.py:295
  67.0 8.9 %collective-permute-start.18 = (bf16[512,128]{1,0:T(8,128)(2,1)S(1)}, bf16[512,128]{1,0:T(8,128)(2,1)S(1)}, u32[]{:S(2)}, u32[]{:S(2)}) collective-permute-start(bf16[512,128]{1,0:T(8,128)(2,1)S(1)} %get-tuple-element.55), channel_id=1, source_target_pairs={{0,2},{1,3},{2,0},{3,1},{4,6},{5,7},{6,4},{7,5},{8,10},{9,11},{10,... | collective-permute-start | bytes 393224 | tf_op jit(solution)/shard_map/ppermute | solution.py:295
  69.5 6.5 %collective-permute-start.19 = (bf16[512,128]{1,0:T(8,128)(2,1)S(1)}, bf16[512,128]{1,0:T(8,128)(2,1)S(1)}, u32[]{:S(2)}, u32[]{:S(2)}) collective-permute-start(bf16[512,128]{1,0:T(8,128)(2,1)S(1)} %get-tuple-element.56), channel_id=1, source_target_pairs={{0,3},{1,0},{2,1},{3,2},{4,7},{5,4},{6,5},{7,6},{8,11},{9,8},{10,9... | collective-permute-start | bytes 393224 | tf_op jit(solution)/shard_map/ppermute | solution.py:295
  70.6 10.9 %copy-start.2 = (s32[64,4]{0,1:T(4,128)S(1)}, s32[64,4]{0,1:T(4,128)}, u32[]{:S(2)}) copy-start(s32[64,4]{0,1:T(4,128)} %param.5) | copy-start | bytes 3076
  71.3 7.6 %collective-permute-start.12 = (bf16[512,128]{1,0:T(8,128)(2,1)S(1)}, bf16[512,128]{1,0:T(8,128)(2,1)S(1)}, u32[]{:S(2)}, u32[]{:S(2)}) collective-permute-start(bf16[512,128]{1,0:T(8,128)(2,1)S(1)} %get-tuple-element.48), channel_id=1, source_target_pairs={{0,1},{1,2},{2,3},{3,0},{4,5},{5,6},{6,7},{7,4},{8,9},{9,10},{10,1... | collective-permute-start | bytes 393224 | tf_op jit(solution)/shard_map/ppermute | solution.py:295
  71.7 9.9 %collective-permute-start.13 = (bf16[512,128]{1,0:T(8,128)(2,1)S(1)}, bf16[512,128]{1,0:T(8,128)(2,1)S(1)}, u32[]{:S(2)}, u32[]{:S(2)}) collective-permute-start(bf16[512,128]{1,0:T(8,128)(2,1)S(1)} %get-tuple-element.49), channel_id=1, source_target_pairs={{0,2},{1,3},{2,0},{3,1},{4,6},{5,7},{6,4},{7,5},{8,10},{9,11},{10,... | collective-permute-start | bytes 393224 | tf_op jit(solution)/shard_map/ppermute | solution.py:295
  72.5 9.0 %collective-permute-start.14 = (bf16[512,128]{1,0:T(8,128)(2,1)S(1)}, bf16[512,128]{1,0:T(8,128)(2,1)S(1)}, u32[]{:S(2)}, u32[]{:S(2)}) collective-permute-start(bf16[512,128]{1,0:T(8,128)(2,1)S(1)} %get-tuple-element.50), channel_id=1, source_target_pairs={{0,3},{1,0},{2,1},{3,2},{4,7},{5,4},{6,5},{7,6},{8,11},{9,8},{10,9... | collective-permute-start | bytes 393224 | tf_op jit(solution)/shard_map/ppermute | solution.py:295

commit v4 on v0

v4 whole, which is shorter than its diff:
```python
import functools

import jax
import jax.numpy as jnp
from jax import lax
from jax.experimental import pallas as pl
from jax.experimental.pallas import tpu as pltpu
from jax.sharding import PartitionSpec as P

BLOCK = 32
F32 = jnp.float32
BF16 = jnp.bfloat16
ANY = pl.BlockSpec(memory_space=pl.ANY)
HBM = pl.BlockSpec(memory_space=pltpu.HBM)
VM = pl.BlockSpec(memory_space=pltpu.VMEM)


def vmem(mib):
    return pltpu.CompilerParams(vmem_limit_bytes=mib * 1024 * 1024)


def place():
    layer = lax.axis_index("layer")
    return layer // 2, layer % 2


def widen(mask, width):
    k = mask.shape[0]
    rep = lax.broadcasted_iota(jnp.int32, (k, width), 1) // (width // k)
    one = lax.broadcasted_iota(jnp.int32, (k, width), 0)
    spread = jnp.where(rep == one, 1.0, 0.0).astype(F32)
    flag = jnp.where(mask > 0, 1.0, 0.0).astype(F32)
    return lax.dot_general(flag, spread, (((0,), (0,)), ((), ())), preferred_element_type=F32)


def tall(flags):
    n, width = flags.shape
    return jnp.broadcast_to(flags.reshape(n, 1, width), (n, BLOCK, width)).reshape(
        n * BLOCK, width
    )


def prepare_kernel(x_ref, pat_ref, left_ref, own_ref, send_ref, pat, wide, buf, slabs, sems):
    a, b = place()
    h = lax.axis_index("col") % 2
    rows, cols = buf.shape
    copies = [
        pltpu.make_async_copy(pat_ref, pat, sems.at[0]),
        pltpu.make_async_copy(
            x_ref.at[pl.ds(pl.multiple_of(a * rows, rows), rows),
                     pl.ds(pl.multiple_of(b * cols, cols), cols)],
            buf, sems.at[1]),
    ]
    for c in range(4):
        copies.append(pltpu.make_async_copy(
            x_ref.at[pl.ds(pl.multiple_of((2 * c + b) * cols, cols), cols), :],
            slabs.at[c], sems.at[2 + c]))
    for copy in copies:
        copy.start()
    copies[0].wait()
    wide[...] = widen(pat[...], wide.shape[1])
    copies[1].wait()
    atoms = rows // BLOCK
    flags = wide[pl.ds(pl.multiple_of(a * atoms, atoms), atoms),
                 pl.ds(pl.multiple_of(b * cols, cols), cols)]
    left_ref[...] = buf[...] * tall(flags).astype(BF16)
    atoms = cols // BLOCK
    for copy in copies[2:]:
        copy.wait()
    for i in range(2):
        for ref, k in ((own_ref, 2 * i + h), (send_ref, 2 * i + 1 - h)):
            at = pl.ds(pl.multiple_of((2 * k + b) * atoms, atoms), atoms)
            ref[i * cols:(i + 1) * cols, :] = slabs[k] * tall(wide[at, :]).astype(BF16)


def prepare(matrix, pattern_t):
    rows, cols = matrix.shape
    right = jax.ShapeDtypeStruct((cols, cols), BF16)
    return pl.pallas_call(
        prepare_kernel,
        out_shape=(jax.ShapeDtypeStruct((rows // 2, cols // 2), BF16), right, right),
        in_specs=[HBM, HBM],
        out_specs=(VM,) * 3,
        scratch_shapes=[
            pltpu.VMEM(pattern_t.shape, jnp.int32),
            pltpu.VMEM((rows // BLOCK, cols), F32),
            pltpu.VMEM((rows // 2, cols // 2), BF16),
            pltpu.VMEM((4, cols // 2, cols), BF16),
            pltpu.SemaphoreType.DMA((6,)),
        ],
        compiler_params=vmem(12),
        name="prepare",
    )(matrix, pattern_t)


def side():
    return 1 - 2 * (lax.axis_index("col") % 2)


def meeting(step):
    source = lax.rem(lax.axis_index("col") // 2 - step * side() + 8, 8)
    away = lax.rem((lax.axis_index("row") - source // 2) * side() + 8, 4)
    return away, lax.rem(source, 2)


def early_kernel(steps, *refs):
    n = len(steps)
    lefts, (own, near, other), outs = refs[:n], refs[n:n + 3], refs[n + 3:n + 7]
    left, right, lsem, rsem = refs[n + 7:]
    half, cols = outs[0].shape
    width = lefts[0].shape[1]
    waits = []
    for i, step in enumerate(steps):
        away, low = meeting(step)
        low = pl.multiple_of(low * width, width)
        copy = pltpu.make_async_copy(lefts[i], left.at[:, pl.ds(i * width, width)], lsem.at[i])
        waits.append((copy, away != 2))
        pl.when(away != 2)(copy.start)

        @pl.when(away == 2)
        def _():
            left[:, i * width:(i + 1) * width] = jnp.zeros((2 * half, width), BF16)

        for ref, here in ((own, (away == 0) | (away == 2)), (near, away == 1), (other, away == 3)):
            for slot in range(2):
                copy = pltpu.make_async_copy(
                    ref.at[slot, pl.ds(low, width), :],
                    right.at[pl.ds(i * width, width), pl.ds(slot * cols, cols)],
                    rsem.at[i, slot])
                waits.append((copy, here))
                pl.when(here)(copy.start)
    for copy, here in waits:
        pl.when(here)(copy.wait)
    for part in range(2):
        for slot in range(2):
            outs[2 * part + slot][...] = jnp.dot(
                left[part * half:(part + 1) * half, :],
                right[:, slot * cols:(slot + 1) * cols],
                preferred_element_type=F32)


def early(lefts, steps, rights):
    rows, width = lefts[0].shape
    cols = rights[0].shape[2]
    n = len(steps)
    out = jax.ShapeDtypeStruct((rows // 2, cols), F32)
    return pl.pallas_call(
        functools.partial(early_kernel, steps),
        out_shape=(out,) * 4,
        in_specs=[ANY] * (n + 3),
        out_specs=(VM,) * 4,
        scratch_shapes=[
            pltpu.VMEM((rows, n * width), BF16),
            pltpu.VMEM((n * width, 2 * cols), BF16),
            pltpu.SemaphoreType.DMA((n,)),
            pltpu.SemaphoreType.DMA((n, 2)),
        ],
        compiler_params=vmem(16),
        name="early",
    )(*lefts, *rights)


def late_sum(part, slot, steps, acc_ref, ends, lefts, rights, left, right, lsem, rsem):
    half, width = acc_ref.shape[0], lefts[0].shape[1]
    z, r = lax.axis_index("col") // 2, lax.axis_index("row")
    rows = pl.ds(part * half, half)
    waits = []

    def copy(source, target, sem, here=None):
        one = pltpu.make_async_copy(source, target, sem)
        if here is None:
            one.start()
            waits.append(one.wait)
        else:
            pl.when(here)(one.start)
            waits.append(lambda: pl.when(here)(one.wait))

    for i, (end, step) in enumerate(zip(ends, (4, -3))):
        away, low = meeting(step)
        low = pl.multiple_of(low * width, width)
        at = pl.ds(i * width, width)
        copy(end.at[rows, :], left.at[:, at], lsem.at[i])
        for j, ref in enumerate(rights):
            copy(ref.at[slot, pl.ds(low, width), :], right.at[at, :], rsem.at[i], away == j)
    copy(rights[2].at[slot], right.at[pl.ds(2 * width, 2 * width), :], rsem.at[2])
    for q in range(2):
        source = 2 * lax.rem(r + 2, 4) + q
        step = lax.rem((z - source) * side() + 16, 8)
        at = pl.ds((2 + q) * width, width)
        for i, ref in enumerate(lefts):
            copy(ref.at[rows, :], left.at[:, at], lsem.at[2 + q], step == steps[i] % 8)

        @pl.when((step == 4) | (step == 5))
        def _():
            left[:, (2 + q) * width:(3 + q) * width] = jnp.zeros((half, width), BF16)

    for wait in waits:
        wait()
    return acc_ref[...] + jnp.dot(left[...], right[...], preferred_element_type=F32)


def late_scratch(half, width, cols):
    return [
        pltpu.VMEM((half, 4 * width), BF16),
        pltpu.VMEM((4 * width, cols), BF16),
        pltpu.SemaphoreType.DMA((4,)),
        pltpu.SemaphoreType.DMA((3,)),
    ]


def late_other_kernel(part, steps, acc_ref, *refs):
    ends, refs = refs[:2], refs[2:]
    n = len(steps)
    out_ref, *scratch = refs[n + 4:]
    out_ref[...] = late_sum(
        part, 1, steps, acc_ref, ends, refs[:n], refs[n:n + 4], *scratch).astype(BF16)


def late_other(part, acc, ends, lefts, steps, rights):
    half, cols = acc.shape
    return pl.pallas_call(
        functools.partial(late_other_kernel, part, steps),
        out_shape=jax.ShapeDtypeStruct((half, cols), BF16),
        in_specs=[VM] + [ANY] * (6 + len(lefts)),
        out_specs=VM,
        scratch_shapes=late_scratch(half, lefts[0].shape[1], cols),
        compiler_params=vmem(8),
        name="late_other",
    )(acc, *ends, *lefts, *rights)


def late_own_kernel(part, steps, acc_ref, other_ref, *refs):
    ends, refs = refs[:2], refs[2:]
    n = len(steps)
    outs, whole, scratch = refs[n + 4:n + 8], refs[n + 8], refs[n + 9:]
    whole[...] = other_ref[...].astype(F32) + late_sum(
        part, 0, steps, acc_ref, ends, refs[:n], refs[n:n + 4], *scratch)
    layer = lax.axis_index("layer")
    width = outs[0].shape[1]
    for d, out in enumerate(outs):
        cols = pl.ds(pl.multiple_of(lax.rem(layer + d, 4) * width, width), width)
        out[...] = whole[:, cols].astype(out.dtype)


def late_own(part, acc, other, ends, lefts, steps, rights):
    half, cols = acc.shape
    return pl.pallas_call(
        functools.partial(late_own_kernel, part, steps),
        out_shape=(jax.ShapeDtypeStruct((half, cols // 4), BF16),) * 4,
        in_specs=[VM] * 2 + [ANY] * (6 + len(lefts)),
        out_specs=(VM,) * 4,
        scratch_shapes=[pltpu.VMEM((half, cols), F32)] + late_scratch(half, lefts[0].shape[1], cols),
        compiler_params=vmem(8),
        name="late_own",
    )(acc, other, *ends, *lefts, *rights)


def total_kernel(part, p0, p1, p2, p3, keep_ref, *refs):
    out_ref, held, sems = refs[-3:]
    pieces = (p0, p1, p2, p3)
    layer = lax.axis_index("layer")
    half, width = p0.shape
    atoms = half // BLOCK
    flags = widen(keep_ref[...], width)
    for value in range(4):

        @pl.when(layer == value)
        def _():
            for a in range(2):
                two = [pieces[(value - 2 * a - b) % 4][...].astype(F32) for b in range(2)]
                at = (2 * a + part) * atoms
                kept = tall(flags[at:at + atoms]) > 0.5
                held[a] = jnp.where(kept, two[0] + two[1], 0.0).astype(BF16)

    copies = [
        pltpu.make_async_copy(
            held.at[a], out_ref.at[pl.ds((2 * a + part) * half, half), :], sems.at[a])
        for a in range(2)
    ]
    for copy in copies:
        copy.start()
    for copy in copies:
        copy.wait()


def total(part, pieces, keep_t, into=None):
    half, width = pieces[0].shape
    more = [] if into is None else [into]
    return pl.pallas_call(
        functools.partial(total_kernel, part),
        out_shape=jax.ShapeDtypeStruct((4 * half, width), BF16),
        in_specs=[VM] * 5 + [HBM] * len(more),
        out_specs=HBM,
        scratch_shapes=[pltpu.VMEM((2, half, width), BF16), pltpu.SemaphoreType.DMA((2,))],
        input_output_aliases={5: 0} if more else {},
        compiler_params=vmem(4),
        name="total",
    )(*pieces, keep_t, *more)


def stream(x, d):
    return lax.ppermute(
        x, "col", [(c, (c // 2 + (d if c % 2 == 0 else -d)) % 8 * 2 + c % 2) for c in range(16)])


def along(x, axis, d):
    return lax.ppermute(x, axis, [(i, (i + d) % 4) for i in range(4)])


def swap(x):
    return lax.ppermute(x, "col", [(c, c ^ 1) for c in range(16)])


def turn(x, d):
    pairs = []
    for r in range(4):
        for c in range(16):
            to = (r + (d if c % 2 == 0 else -d)) % 4
            pairs.append((r * 16 + c, to * 16 + c))
    return lax.ppermute(x, ("row", "col"), pairs)


def after(x, y):
    return lax.optimization_barrier((x, y))[0]


def on_device(matrix, pattern, keep):
    matrix = pltpu.with_memory_space_constraint(matrix, pltpu.HBM)
    pattern_t = pltpu.with_memory_space_constraint(pattern.T, pltpu.HBM)
    block, mine, theirs = prepare(matrix, pattern_t)
    theirs = swap(theirs)
    both = jnp.stack([mine, theirs])

    up1 = stream(block, 1)
    up2 = stream(up1, 1)
    up3 = stream(up2, 1)
    up4 = stream(up3, 1)
    down1 = stream(after(block, theirs), -1)
    down2 = stream(down1, -1)
    down3 = stream(down2, -1)
    near, other = turn(both, 1), turn(both, -1)
    far = turn(after(near, up2), 1)
    rights = [both, near, far, other]

    steps = (0, 1, -1, 2, -2, 3)
    lefts, ends = [block, up1, down1, up2, down2, up3], [up4, down3]
    acc = early(lefts, steps, [both, near, other])
    out, keep_t = None, keep.T
    for p in range(2):
        other = swap(late_other(p, acc[2 * p + 1], ends, lefts, steps, rights))
        mine = late_own(p, acc[2 * p], other, ends, lefts, steps, rights)
        moved = [mine[0]] + [along(mine[d], "layer", d) for d in range(1, 4)]
        out = total(p, moved, keep_t, out)
    return out


def solution(mesh):
    in_specs = (P("row", "col"), P("row", "col"), P("row", ("col", "layer")))
    out_specs = P("row", ("col", "layer"))
    return jax.shard_map(
        on_device, mesh=mesh, in_specs=in_specs, out_specs=out_specs, check_vma=False
    )
```

time: 186 us -> 80.6 us (0.43)
  the two profiles are of different devices: /device:TPU:1 before, /device:TPU:8 now
where the time goes in v4:
time: 80.6 us; the launch traced here: 80.5 us
  waiting for transfers between devices  39.5 us (49%)
  starting transfers between devices  27.8 us (34%)
  Pallas kernels  12.9 us (16%)
    ppermute x7, waiting for transfers between devices, stream(): lax.ppermute(x, 'col', [(c, (c // 2 + (d if c % 2 == 0 else -d)) % 8 * 2...  34.3 us
    ppermute x7, starting transfers between devices, stream(): lax.ppermute(x, 'col', [(c, (c // 2 + (d if c % 2 == 0 else -d)) % 8 * 2...  15.4 us
    ppermute x6, starting transfers between devices, along(): return lax.ppermute(x, axis, [(i, (i + d) % 4) for i in range(4)])  9.18 us
    ppermute x6, waiting for transfers between devices, along(): return lax.ppermute(x, axis, [(i, (i + d) % 4) for i in range(4)])  4.95 us
    pallas_call x1, Pallas kernels, early(): pl.pallas_call(functools.partial(early_kernel, steps), out_shape=(out,) *...  4.25 us
    pallas_call x2, Pallas kernels, late_own(): pl.pallas_call(functools.partial(late_own_kernel, part, steps), out_shape...  2.74 us
    ppermute x3, starting transfers between devices, turn(): return lax.ppermute(x, ('row', 'col'), pairs)  2.47 us
    pallas_call x2, Pallas kernels, late_other(): pl.pallas_call(functools.partial(late_other_kernel, part, steps), out_sha...  2.41 us
  transfers between devices with their start and end apart: 19, of which 9 were waited for; matrix products, arithmetic and copies ran while one was open for 0% of the time, Pallas kernels for 11%

profile of v4, /device:TPU:8, one launch (start us, length us, event | category | flops | bytes accessed | tf_op | source)
XLA Modules:
  0.0 80.5 jit_solution(14906618776040952722)
XLA Ops:
  0.0 1.5 %prepare.1 = (bf16[1024,256]{1,0:T(8,128)(2,1)S(1)}, bf16[512,512]{1,0:T(8,128)(2,1)S(1)}, bf16[512,512]{1,0:T(8,128)(2,1)S(1)}) custom-call(bf16[2048,512]{1,0:T(8,128)(2,1)} %x_ref.1, s32[16,64]{1,0:T(8,128)} %bitcast.8), custom_call_target="tpu_custom_call" | custom-call | tf_op jit(solution)/shard_map/prepare/pallas_call | solution.py:79
  1.6 2.0 %collective-permute-start = (bf16[1024,256]{1,0:T(8,128)(2,1)S(1)}, bf16[1024,256]{1,0:T(8,128)(2,1)S(1)}, u32[]{:S(2)}, u32[]{:S(2)}) collective-permute-start(bf16[1024,256]{1,0:T(8,128)(2,1)S(1)} %get-tuple-element.24.refs_0_.refs_2_), channel_id=1, source_target_pairs={{0,8},{4,60},{8,16},{12,4},{16,24},{20,12},{24,32},{28,20},{32,40}... | collective-permute-start | bytes 1572872 | tf_op jit(solution)/shard_map/ppermute | solution.py:302
  3.7 1.7 %collective-permute-start.6 = (bf16[2,512,512]{2,1,0:T(8,128)(2,1)S(1)}, bf16[2,512,512]{2,1,0:T(8,128)(2,1)S(1)}, u32[]{:S(2)}, u32[]{:S(2)}) collective-permute-start(bf16[2,512,512]{2,1,0:T(8,128)(2,1)S(1)} %pad_maximum_fusion.refs_6_.refs_8_), channel_id=1, source_target_pairs={{0,64},{4,196},{8,72},{12,204},{16,80},{20,212},{24,88},{28,220},{... | collective-permute-start | bytes 3145736 | tf_op jit(solution)/shard_map/ppermute | solution.py:320
  5.4 5.8 %collective-permute-start.2 = (bf16[1024,256]{1,0:T(8,128)(2,1)S(1)}, bf16[1024,256]{1,0:T(8,128)(2,1)S(1)}, u32[]{:S(2)}, u32[]{:S(2)}) collective-permute-start(bf16[1024,256]{1,0:T(8,128)(2,1)S(1)} %get-tuple-element.24.refs_0_.refs_2_), channel_id=1, source_target_pairs={{0,56},{4,12},{8,0},{12,20},{16,8},{20,28},{24,16},{28,36},{32,24}... | collective-permute-start | bytes 1572872 | tf_op jit(solution)/shard_map/ppermute | solution.py:302
  11.1 6.4 %collective-permute-done.refs_1_.refs_3_ = bf16[1024,256]{1,0:T(8,128)(2,1)S(1)} collective-permute-done((bf16[1024,256]{1,0:T(8,128)(2,1)S(1)}, bf16[1024,256]{1,0:T(8,128)(2,1)S(1)}, u32[]{:S(2)}, u32[]{:S(2)}) %collective-permute-start) | collective-permute-done | bytes 524320 | tf_op jit(solution)/shard_map/ppermute | solution.py:302
  17.5 2.0 %collective-permute-done.2.refs_2_.refs_4_ = bf16[1024,256]{1,0:T(8,128)(2,1)S(1)} collective-permute-done((bf16[1024,256]{1,0:T(8,128)(2,1)S(1)}, bf16[1024,256]{1,0:T(8,128)(2,1)S(1)}, u32[]{:S(2)}, u32[]{:S(2)}) %collective-permute-start.2) | collective-permute-done | bytes 524320 | tf_op jit(solution)/shard_map/ppermute | solution.py:302
  19.5 3.7 %collective-permute-start.4 = (bf16[1024,256]{1,0:T(8,128)(2,1)S(1)}, bf16[1024,256]{1,0:T(8,128)(2,1)S(1)}, u32[]{:S(2)}, u32[]{:S(2)}) collective-permute-start(bf16[1024,256]{1,0:T(8,128)(2,1)S(1)} %collective-permute-done.2.refs_2_.refs_4_), channel_id=1, source_target_pairs={{0,56},{4,12},{8,0},{12,20},{16,8},{20,28},{24,16},{28,36},{32,24}... | collective-permute-start | bytes 1572872 | tf_op jit(solution)/shard_map/ppermute | solution.py:302
  23.2 8.9 %collective-permute-done.3.refs_3_.refs_5_ = bf16[1024,256]{1,0:T(8,128)(2,1)S(1)} collective-permute-done((bf16[1024,256]{1,0:T(8,128)(2,1)S(1)}, bf16[1024,256]{1,0:T(8,128)(2,1)S(1)}, u32[]{:S(2)}, u32[]{:S(2)}) %collective-permute-start.3) | collective-permute-done | bytes 524320 | tf_op jit(solution)/shard_map/ppermute | solution.py:302
  32.9 3.9 %collective-permute-start.9 = (bf16[1024,256]{1,0:T(8,128)(2,1)S(1)}, bf16[1024,256]{1,0:T(8,128)(2,1)S(1)}, u32[]{:S(2)}, u32[]{:S(2)}) collective-permute-start(bf16[1024,256]{1,0:T(8,128)(2,1)S(1)} %collective-permute-done.4.refs_4_.refs_6_), channel_id=1, source_target_pairs={{0,56},{4,12},{8,0},{12,20},{16,8},{20,28},{24,16},{28,36},{32,24}... | collective-permute-start | bytes 1572872 | tf_op jit(solution)/shard_map/ppermute | solution.py:302
  36.9 10.9 %collective-permute-done.5.refs_5_.refs_7_ = bf16[1024,256]{1,0:T(8,128)(2,1)S(1)} collective-permute-done((bf16[1024,256]{1,0:T(8,128)(2,1)S(1)}, bf16[1024,256]{1,0:T(8,128)(2,1)S(1)}, u32[]{:S(2)}, u32[]{:S(2)}) %collective-permute-start.5) | collective-permute-done | bytes 524320 | tf_op jit(solution)/shard_map/ppermute | solution.py:302
  47.7 4.3 %early.1 = (f32[512,512]{1,0:T(8,128)S(1)}, f32[512,512]{1,0:T(8,128)S(1)}, f32[512,512]{1,0:T(8,128)S(1)}, f32[512,512]{1,0:T(8,128)S(1)}) custom-call(bf16[1024,256]{1,0:T(8,128)(2,1)S(1)} %get-tuple-element.24.refs_0_.refs_2_, bf16[1024,256]{1,0:T(8,128)(2,1)S(1)} %collective-permute-done.refs_1_.refs_3_, ...), custom_call_target="tpu_custom_call" | custom-call | tf_op jit(solution)/shard_map/early/pallas_call | solution.py:147
  52.0 6.1 %collective-permute-done.8.refs_0_ = bf16[1024,256]{1,0:T(8,128)(2,1)S(1)} collective-permute-done((bf16[1024,256]{1,0:T(8,128)(2,1)S(1)}, bf16[1024,256]{1,0:T(8,128)(2,1)S(1)}, u32[]{:S(2)}, u32[]{:S(2)}) %collective-permute-start.8) | collective-permute-done | bytes 524320 | tf_op jit(solution)/shard_map/ppermute | solution.py:302
  58.1 1.3 %late_other.3 = bf16[512,512]{1,0:T(8,128)(2,1)S(1)} custom-call(f32[512,512]{1,0:T(8,128)S(1)} %get-tuple-element.34.acc_ref, bf16[1024,256]{1,0:T(8,128)(2,1)S(1)} %collective-permute-done.8.refs_0_, bf16[1024,256]{1,0:T(8,128)(2,1)S(1)} %collective-permute-done.9.refs_1_, bf16[1024,256]{1,0:T(8,128)(2,1)S(1)} %get-tuple-element.24.refs_0_.refs_2_, ...), custom_call_target="tpu_custom_call" | custom-call | tf_op jit(solution)/shard_map/late_other/pallas_call | solution.py:221
  59.5 1.1 %late_other.2 = bf16[512,512]{1,0:T(8,128)(2,1)S(1)} custom-call(f32[512,512]{1,0:T(8,128)S(1)} %get-tuple-element.27.acc_ref, bf16[1024,256]{1,0:T(8,128)(2,1)S(1)} %collective-permute-done.8.refs_0_, bf16[1024,256]{1,0:T(8,128)(2,1)S(1)} %collective-permute-done.9.refs_1_, bf16[1024,256]{1,0:T(8,128)(2,1)S(1)} %get-tuple-element.24.refs_0_.refs_2_, ...), custom_call_target="tpu_custom_call" | custom-call | tf_op jit(solution)/shard_map/late_other/pallas_call | solution.py:221
  61.4 1.4 %late_own.3 = (bf16[512,128]{1,0:T(8,128)(2,1)S(1)}, bf16[512,128]{1,0:T(8,128)(2,1)S(1)}, bf16[512,128]{1,0:T(8,128)(2,1)S(1)}, bf16[512,128]{1,0:T(8,128)(2,1)S(1)}) custom-call(f32[512,512]{1,0:T(8,128)S(1)} %get-tuple-element.33.acc_ref, bf16[512,512]{1,0:T(8,128)(2,1)S(1)} %collective-permute-done.15.other_ref, ...), custom_call_target="tpu_custom_call" | custom-call | tf_op jit(solution)/shard_map/late_own/pallas_call | solution.py:247
  62.8 1.6 %collective-permute-start.16 = (bf16[512,128]{1,0:T(8,128)(2,1)S(1)}, bf16[512,128]{1,0:T(8,128)(2,1)S(1)}, u32[]{:S(2)}, u32[]{:S(2)}) collective-permute-start(bf16[512,128]{1,0:T(8,128)(2,1)S(1)} %get-tuple-element.36), channel_id=1, source_target_pairs={{0,1},{1,2},{2,3},{3,0},{4,5},{5,6},{6,7},{7,4},{8,9},{9,10},{10,1... | collective-permute-start | bytes 393224 | tf_op jit(solution)/shard_map/ppermute | solution.py:307
  64.4 2.7 %collective-permute-start.17 = (bf16[512,128]{1,0:T(8,128)(2,1)S(1)}, bf16[512,128]{1,0:T(8,128)(2,1)S(1)}, u32[]{:S(2)}, u32[]{:S(2)}) collective-permute-start(bf16[512,128]{1,0:T(8,128)(2,1)S(1)} %get-tuple-element.37), channel_id=1, source_target_pairs={{0,2},{1,3},{2,0},{3,1},{4,6},{5,7},{6,4},{7,5},{8,10},{9,11},{10,... | collective-permute-start | bytes 393224 | tf_op jit(solution)/shard_map/ppermute | solution.py:307
  67.1 1.4 %collective-permute-start.18 = (bf16[512,128]{1,0:T(8,128)(2,1)S(1)}, bf16[512,128]{1,0:T(8,128)(2,1)S(1)}, u32[]{:S(2)}, u32[]{:S(2)}) collective-permute-start(bf16[512,128]{1,0:T(8,128)(2,1)S(1)} %get-tuple-element.38), channel_id=1, source_target_pairs={{0,3},{1,0},{2,1},{3,2},{4,7},{5,4},{6,5},{7,6},{8,11},{9,8},{10,9... | collective-permute-start | bytes 393224 | tf_op jit(solution)/shard_map/ppermute | solution.py:307
  68.5 1.4 %late_own.2 = (bf16[512,128]{1,0:T(8,128)(2,1)S(1)}, bf16[512,128]{1,0:T(8,128)(2,1)S(1)}, bf16[512,128]{1,0:T(8,128)(2,1)S(1)}, bf16[512,128]{1,0:T(8,128)(2,1)S(1)}) custom-call(f32[512,512]{1,0:T(8,128)S(1)} %get-tuple-element.26.acc_ref, bf16[512,512]{1,0:T(8,128)(2,1)S(1)} %collective-permute-done.11.other_ref, ...), custom_call_target="tpu_custom_call" | custom-call | tf_op jit(solution)/shard_map/late_own/pallas_call | solution.py:247
  70.6 0.9 %collective-permute-start.13 = (bf16[512,128]{1,0:T(8,128)(2,1)S(1)}, bf16[512,128]{1,0:T(8,128)(2,1)S(1)}, u32[]{:S(2)}, u32[]{:S(2)}) collective-permute-start(bf16[512,128]{1,0:T(8,128)(2,1)S(1)} %get-tuple-element.31), channel_id=1, source_target_pairs={{0,2},{1,3},{2,0},{3,1},{4,6},{5,7},{6,4},{7,5},{8,10},{9,11},{10,... | collective-permute-start | bytes 393224 | tf_op jit(solution)/shard_map/ppermute | solution.py:307
  71.5 1.9 %collective-permute-start.14 = (bf16[512,128]{1,0:T(8,128)(2,1)S(1)}, bf16[512,128]{1,0:T(8,128)(2,1)S(1)}, u32[]{:S(2)}, u32[]{:S(2)}) collective-permute-start(bf16[512,128]{1,0:T(8,128)(2,1)S(1)} %get-tuple-element.32), channel_id=1, source_target_pairs={{0,3},{1,0},{2,1},{3,2},{4,7},{5,4},{6,5},{7,6},{8,11},{9,8},{10,9... | collective-permute-start | bytes 393224 | tf_op jit(solution)/shard_map/ppermute | solution.py:307
  74.2 1.0 %total.2.refs_0_ = bf16[2048,128]{1,0:T(8,128)(2,1)} custom-call(bf16[512,128]{1,0:T(8,128)(2,1)S(1)} %get-tuple-element.35.p0, bf16[512,128]{1,0:T(8,128)(2,1)S(1)} %collective-permute-done.16.p1, bf16[512,128]{1,0:T(8,128)(2,1)S(1)} %collective-permute-done.17.p2, bf16[512,128]{1,0:T(8,128)(2,1)S(1)} %collective-permute-done.18.p3, s32[4,64]{1,0:T(4,128)S(1)} %bitcast.5), custom_call_target="tpu_custom_call" | custom-call | tf_op jit(solution)/shard_map/total/pallas_call | solution.py:289
  75.2 4.0 %collective-permute-done.12.p1 = bf16[512,128]{1,0:T(8,128)(2,1)S(1)} collective-permute-done((bf16[512,128]{1,0:T(8,128)(2,1)S(1)}, bf16[512,128]{1,0:T(8,128)(2,1)S(1)}, u32[]{:S(2)}, u32[]{:S(2)}) %collective-permute-start.12) | collective-permute-done | bytes 131104 | tf_op jit(solution)/shard_map/ppermute | solution.py:307
  79.3 1.0 %total.3 = bf16[2048,128]{1,0:T(8,128)(2,1)} custom-call(bf16[512,128]{1,0:T(8,128)(2,1)S(1)} %get-tuple-element.29.p0, bf16[512,128]{1,0:T(8,128)(2,1)S(1)} %collective-permute-done.12.p1, bf16[512,128]{1,0:T(8,128)(2,1)S(1)} %collective-permute-done.13.p2, bf16[512,128]{1,0:T(8,128)(2,1)S(1)} %collective-permute-done.14.p3, ...), custom_call_target="tpu_custom_call", output_to_operand_aliasing={{}: (5, {})} | custom-call | tf_op jit(solution)/shard_map/total/pallas_call | solution.py:289
  (25 shorter events, 3.5 us)
Async XLA Ops:
  1.5 2.1 %collective-permute-start.1 = (bf16[512,512]{1,0:T(8,128)(2,1)S(1)}, bf16[512,512]{1,0:T(8,128)(2,1)S(1)}, u32[]{:S(2)}, u32[]{:S(2)}) collective-permute-start(bf16[512,512]{1,0:T(8,128)(2,1)S(1)} %get-tuple-element.23), channel_id=1, source_target_pairs={{0,4},{4,0},{8,12},{12,8},{16,20},{20,16},{24,28},{28,24},{32,36},... | collective-permute-start | bytes 1572872 | tf_op jit(solution)/shard_map/ppermute | solution.py:311
  1.6 15.9 %collective-permute-start = (bf16[1024,256]{1,0:T(8,128)(2,1)S(1)}, bf16[1024,256]{1,0:T(8,128)(2,1)S(1)}, u32[]{:S(2)}, u32[]{:S(2)}) collective-permute-start(bf16[1024,256]{1,0:T(8,128)(2,1)S(1)} %get-tuple-element.24.refs_0_.refs_2_), channel_id=1, source_target_pairs={{0,8},{4,60},{8,16},{12,4},{16,24},{20,12},{24,32},{28,20},{32,40}... | collective-permute-start | bytes 1572872 | tf_op jit(solution)/shard_map/ppermute | solution.py:302
  3.7 28.4 %collective-permute-start.6 = (bf16[2,512,512]{2,1,0:T(8,128)(2,1)S(1)}, bf16[2,512,512]{2,1,0:T(8,128)(2,1)S(1)}, u32[]{:S(2)}, u32[]{:S(2)}) collective-permute-start(bf16[2,512,512]{2,1,0:T(8,128)(2,1)S(1)} %pad_maximum_fusion.refs_6_.refs_8_), channel_id=1, source_target_pairs={{0,64},{4,196},{8,72},{12,204},{16,80},{20,212},{24,88},{28,220},{... | collective-permute-start | bytes 3145736 | tf_op jit(solution)/shard_map/ppermute | solution.py:320
  5.4 14.1 %collective-permute-start.2 = (bf16[1024,256]{1,0:T(8,128)(2,1)S(1)}, bf16[1024,256]{1,0:T(8,128)(2,1)S(1)}, u32[]{:S(2)}, u32[]{:S(2)}) collective-permute-start(bf16[1024,256]{1,0:T(8,128)(2,1)S(1)} %get-tuple-element.24.refs_0_.refs_2_), channel_id=1, source_target_pairs={{0,56},{4,12},{8,0},{12,20},{16,8},{20,28},{24,16},{28,36},{32,24}... | collective-permute-start | bytes 1572872 | tf_op jit(solution)/shard_map/ppermute | solution.py:302
  17.5 14.6 %collective-permute-start.3 = (bf16[1024,256]{1,0:T(8,128)(2,1)S(1)}, bf16[1024,256]{1,0:T(8,128)(2,1)S(1)}, u32[]{:S(2)}, u32[]{:S(2)}) collective-permute-start(bf16[1024,256]{1,0:T(8,128)(2,1)S(1)} %collective-permute-done.refs_1_.refs_3_), channel_id=1, source_target_pairs={{0,8},{4,60},{8,16},{12,4},{16,24},{20,12},{24,32},{28,20},{32,40}... | collective-permute-start | bytes 1572872 | tf_op jit(solution)/shard_map/ppermute | solution.py:302
  17.5 30.2 %collective-permute-start.7 = (bf16[2,512,512]{2,1,0:T(8,128)(2,1)S(1)}, bf16[2,512,512]{2,1,0:T(8,128)(2,1)S(1)}, u32[]{:S(2)}, u32[]{:S(2)}) collective-permute-start(bf16[2,512,512]{2,1,0:T(8,128)(2,1)S(1)} %pad_maximum_fusion.refs_6_.refs_8_), channel_id=1, source_target_pairs={{0,192},{4,68},{8,200},{12,76},{16,208},{20,84},{24,216},{28,92},{... | collective-permute-start | bytes 3145736 | tf_op jit(solution)/shard_map/ppermute | solution.py:320
  19.5 13.4 %collective-permute-start.4 = (bf16[1024,256]{1,0:T(8,128)(2,1)S(1)}, bf16[1024,256]{1,0:T(8,128)(2,1)S(1)}, u32[]{:S(2)}, u32[]{:S(2)}) collective-permute-start(bf16[1024,256]{1,0:T(8,128)(2,1)S(1)} %collective-permute-done.2.refs_2_.refs_4_), channel_id=1, source_target_pairs={{0,56},{4,12},{8,0},{12,20},{16,8},{20,28},{24,16},{28,36},{32,24}... | collective-permute-start | bytes 1572872 | tf_op jit(solution)/shard_map/ppermute | solution.py:302
  32.1 15.6 %collective-permute-start.5 = (bf16[1024,256]{1,0:T(8,128)(2,1)S(1)}, bf16[1024,256]{1,0:T(8,128)(2,1)S(1)}, u32[]{:S(2)}, u32[]{:S(2)}) collective-permute-start(bf16[1024,256]{1,0:T(8,128)(2,1)S(1)} %collective-permute-done.3.refs_3_.refs_5_), channel_id=1, source_target_pairs={{0,8},{4,60},{8,16},{12,4},{16,24},{20,12},{24,32},{28,20},{32,40}... | collective-permute-start | bytes 1572872 | tf_op jit(solution)/shard_map/ppermute | solution.py:302
  32.1 26.0 %collective-permute-start.10 = (bf16[2,512,512]{2,1,0:T(8,128)(2,1)S(1)}, bf16[2,512,512]{2,1,0:T(8,128)(2,1)S(1)}, u32[]{:S(2)}, u32[]{:S(2)}) collective-permute-start(bf16[2,512,512]{2,1,0:T(8,128)(2,1)S(1)} %collective-permute-done.6.refs_7_.refs_9_), channel_id=1, source_target_pairs={{0,64},{4,196},{8,72},{12,204},{16,80},{20,212},{24,88},{28,220},{... | collective-permute-start | bytes 3145736 | tf_op jit(solution)/shard_map/ppermute | solution.py:320
  32.9 19.1 %collective-permute-start.9 = (bf16[1024,256]{1,0:T(8,128)(2,1)S(1)}, bf16[1024,256]{1,0:T(8,128)(2,1)S(1)}, u32[]{:S(2)}, u32[]{:S(2)}) collective-permute-start(bf16[1024,256]{1,0:T(8,128)(2,1)S(1)} %collective-permute-done.4.refs_4_.refs_6_), channel_id=1, source_target_pairs={{0,56},{4,12},{8,0},{12,20},{16,8},{20,28},{24,16},{28,36},{32,24}... | collective-permute-start | bytes 1572872 | tf_op jit(solution)/shard_map/ppermute | solution.py:302
  47.7 10.4 %collective-permute-start.8 = (bf16[1024,256]{1,0:T(8,128)(2,1)S(1)}, bf16[1024,256]{1,0:T(8,128)(2,1)S(1)}, u32[]{:S(2)}, u32[]{:S(2)}) collective-permute-start(bf16[1024,256]{1,0:T(8,128)(2,1)S(1)} %collective-permute-done.5.refs_5_.refs_7_), channel_id=1, source_target_pairs={{0,8},{4,60},{8,16},{12,4},{16,24},{20,12},{24,32},{28,20},{32,40}... | collective-permute-start | bytes 1572872 | tf_op jit(solution)/shard_map/ppermute | solution.py:302
  59.4 2.0 %collective-permute-start.15 = (bf16[512,512]{1,0:T(8,128)(2,1)S(1)}, bf16[512,512]{1,0:T(8,128)(2,1)S(1)}, u32[]{:S(2)}, u32[]{:S(2)}) collective-permute-start(bf16[512,512]{1,0:T(8,128)(2,1)S(1)} %late_other.3), channel_id=1, source_target_pairs={{0,4},{4,0},{8,12},{12,8},{16,20},{20,16},{24,28},{28,24},{32,36},... | collective-permute-start | bytes 1572872 | tf_op jit(solution)/shard_map/ppermute | solution.py:311
  60.7 7.9 %collective-permute-start.11 = (bf16[512,512]{1,0:T(8,128)(2,1)S(1)}, bf16[512,512]{1,0:T(8,128)(2,1)S(1)}, u32[]{:S(2)}, u32[]{:S(2)}) collective-permute-start(bf16[512,512]{1,0:T(8,128)(2,1)S(1)} %late_other.2), channel_id=1, source_target_pairs={{0,4},{4,0},{8,12},{12,8},{16,20},{20,16},{24,28},{28,24},{32,36},... | collective-permute-start | bytes 1572872 | tf_op jit(solution)/shard_map/ppermute | solution.py:311
  62.8 8.7 %collective-permute-start.16 = (bf16[512,128]{1,0:T(8,128)(2,1)S(1)}, bf16[512,128]{1,0:T(8,128)(2,1)S(1)}, u32[]{:S(2)}, u32[]{:S(2)}) collective-permute-start(bf16[512,128]{1,0:T(8,128)(2,1)S(1)} %get-tuple-element.36), channel_id=1, source_target_pairs={{0,1},{1,2},{2,3},{3,0},{4,5},{5,6},{6,7},{7,4},{8,9},{9,10},{10,1... | collective-permute-start | bytes 393224 | tf_op jit(solution)/shard_map/ppermute | solution.py:307
  64.4 9.9 %collective-permute-start.17 = (bf16[512,128]{1,0:T(8,128)(2,1)S(1)}, bf16[512,128]{1,0:T(8,128)(2,1)S(1)}, u32[]{:S(2)}, u32[]{:S(2)}) collective-permute-start(bf16[512,128]{1,0:T(8,128)(2,1)S(1)} %get-tuple-element.37), channel_id=1, source_target_pairs={{0,2},{1,3},{2,0},{3,1},{4,6},{5,7},{6,4},{7,5},{8,10},{9,11},{10,... | collective-permute-start | bytes 393224 | tf_op jit(solution)/shard_map/ppermute | solution.py:307
  67.1 7.1 %collective-permute-start.18 = (bf16[512,128]{1,0:T(8,128)(2,1)S(1)}, bf16[512,128]{1,0:T(8,128)(2,1)S(1)}, u32[]{:S(2)}, u32[]{:S(2)}) collective-permute-start(bf16[512,128]{1,0:T(8,128)(2,1)S(1)} %get-tuple-element.38), channel_id=1, source_target_pairs={{0,3},{1,0},{2,1},{3,2},{4,7},{5,4},{6,5},{7,6},{8,11},{9,8},{10,9... | collective-permute-start | bytes 393224 | tf_op jit(solution)/shard_map/ppermute | solution.py:307
  68.5 5.7 %copy-start = (s32[64,4]{0,1:T(4,128)S(1)}, s32[64,4]{0,1:T(4,128)}, u32[]{:S(2)}) copy-start(s32[64,4]{0,1:T(4,128)} %param.5) | copy-start | bytes 3076
  69.9 9.4 %collective-permute-start.12 = (bf16[512,128]{1,0:T(8,128)(2,1)S(1)}, bf16[512,128]{1,0:T(8,128)(2,1)S(1)}, u32[]{:S(2)}, u32[]{:S(2)}) collective-permute-start(bf16[512,128]{1,0:T(8,128)(2,1)S(1)} %get-tuple-element.30), channel_id=1, source_target_pairs={{0,1},{1,2},{2,3},{3,0},{4,5},{5,6},{6,7},{7,4},{8,9},{9,10},{10,1... | collective-permute-start | bytes 393224 | tf_op jit(solution)/shard_map/ppermute | solution.py:307
  70.6 8.7 %collective-permute-start.13 = (bf16[512,128]{1,0:T(8,128)(2,1)S(1)}, bf16[512,128]{1,0:T(8,128)(2,1)S(1)}, u32[]{:S(2)}, u32[]{:S(2)}) collective-permute-start(bf16[512,128]{1,0:T(8,128)(2,1)S(1)} %get-tuple-element.31), channel_id=1, source_target_pairs={{0,2},{1,3},{2,0},{3,1},{4,6},{5,7},{6,4},{7,5},{8,10},{9,11},{10,... | collective-permute-start | bytes 393224 | tf_op jit(solution)/shard_map/ppermute | solution.py:307
  71.5 7.8 %collective-permute-start.14 = (bf16[512,128]{1,0:T(8,128)(2,1)S(1)}, bf16[512,128]{1,0:T(8,128)(2,1)S(1)}, u32[]{:S(2)}, u32[]{:S(2)}) collective-permute-start(bf16[512,128]{1,0:T(8,128)(2,1)S(1)} %get-tuple-element.32), channel_id=1, source_target_pairs={{0,3},{1,0},{2,1},{3,2},{4,7},{5,4},{6,5},{7,6},{8,11},{9,8},{10,9... | collective-permute-start | bytes 393224 | tf_op jit(solution)/shard_map/ppermute | solution.py:307

commit v5 on v4

v5 whole, which is shorter than its diff:
```python
import functools

import jax
import jax.numpy as jnp
from jax import lax
from jax.experimental import pallas as pl
from jax.experimental.pallas import tpu as pltpu
from jax.sharding import PartitionSpec as P

BLOCK = 32
F32 = jnp.float32
BF16 = jnp.bfloat16
ANY = pl.BlockSpec(memory_space=pl.ANY)
HBM = pl.BlockSpec(memory_space=pltpu.HBM)
VM = pl.BlockSpec(memory_space=pltpu.VMEM)


def vmem(mib):
    return pltpu.CompilerParams(vmem_limit_bytes=mib * 1024 * 1024)


def place():
    layer = lax.axis_index("layer")
    return layer // 2, layer % 2


def widen(mask, width):
    k = mask.shape[0]
    rep = lax.broadcasted_iota(jnp.int32, (k, width), 1) // (width // k)
    one = lax.broadcasted_iota(jnp.int32, (k, width), 0)
    spread = jnp.where(rep == one, 1.0, 0.0).astype(F32)
    flag = jnp.where(mask > 0, 1.0, 0.0).astype(F32)
    return lax.dot_general(flag, spread, (((0,), (0,)), ((), ())), preferred_element_type=F32)


def tall(flags):
    n, width = flags.shape
    return jnp.broadcast_to(flags.reshape(n, 1, width), (n, BLOCK, width)).reshape(
        n * BLOCK, width
    )


def prepare_kernel(x_ref, pat_ref, block_ref, top_ref, low_ref, own_ref, send_ref, pat, wide, buf, slabs, sems):
    a, b = place()
    h = lax.axis_index("col") % 2
    rows, cols = buf.shape
    copies = [
        pltpu.make_async_copy(pat_ref, pat, sems.at[0]),
        pltpu.make_async_copy(
            x_ref.at[pl.ds(pl.multiple_of(a * rows, rows), rows),
                     pl.ds(pl.multiple_of(b * cols, cols), cols)],
            buf, sems.at[1]),
    ]
    for c in range(4):
        copies.append(pltpu.make_async_copy(
            x_ref.at[pl.ds(pl.multiple_of((2 * c + b) * cols, cols), cols), :],
            slabs.at[c], sems.at[2 + c]))
    for copy in copies:
        copy.start()
    copies[0].wait()
    wide[...] = widen(pat[...], wide.shape[1])
    copies[1].wait()
    atoms = rows // BLOCK
    flags = wide[pl.ds(pl.multiple_of(a * atoms, atoms), atoms),
                 pl.ds(pl.multiple_of(b * cols, cols), cols)]
    half = rows // 2
    for part, ref in enumerate((top_ref, low_ref)):
        at = slice(part * half, (part + 1) * half)
        kept = buf[at, :] * tall(flags[part * atoms // 2:(part + 1) * atoms // 2]).astype(BF16)
        ref[...] = kept
        block_ref[at, :] = kept
    atoms = cols // BLOCK
    for copy in copies[2:]:
        copy.wait()
    for i in range(2):
        for ref, k in ((own_ref, 2 * i + h), (send_ref, 2 * i + 1 - h)):
            at = pl.ds(pl.multiple_of((2 * k + b) * atoms, atoms), atoms)
            ref[i * cols:(i + 1) * cols, :] = slabs[k] * tall(wide[at, :]).astype(BF16)


def prepare(matrix, pattern_t):
    rows, cols = matrix.shape
    block = jax.ShapeDtypeStruct((rows // 2, cols // 2), BF16)
    left = jax.ShapeDtypeStruct((rows // 4, cols // 2), BF16)
    right = jax.ShapeDtypeStruct((cols, cols), BF16)
    return pl.pallas_call(
        prepare_kernel,
        out_shape=(block, left, left, right, right),
        in_specs=[HBM, HBM],
        out_specs=(VM,) * 5,
        scratch_shapes=[
            pltpu.VMEM(pattern_t.shape, jnp.int32),
            pltpu.VMEM((rows // BLOCK, cols), F32),
            pltpu.VMEM((rows // 2, cols // 2), BF16),
            pltpu.VMEM((4, cols // 2, cols), BF16),
            pltpu.SemaphoreType.DMA((6,)),
        ],
        compiler_params=vmem(12),
        name="prepare",
    )(matrix, pattern_t)


def side():
    return 1 - 2 * (lax.axis_index("col") % 2)


def meeting(step):
    source = lax.rem(lax.axis_index("col") // 2 - step * side() + 8, 8)
    away = lax.rem((lax.axis_index("row") - source // 2) * side() + 8, 4)
    return away, lax.rem(source, 2)


def halves(refs):
    return [refs[i:i + 2] for i in range(0, len(refs), 2)]


def rows_of(ref, half, part):
    return ref if ref.shape[0] == half else ref.at[pl.ds(part * half, half), :]


def early_kernel(steps, *refs):
    n = len(steps)
    lefts, refs = halves(refs[:2 * n]), refs[2 * n:]
    (own, near, other), outs, (left, right, lsem, rsem) = refs[:3], refs[3:5], refs[5:]
    rows, cols = outs[0].shape
    half, width = lefts[0][0].shape
    waits = []
    for i, step in enumerate(steps):
        away, low = meeting(step)
        low = pl.multiple_of(low * width, width)
        for part in range(2):
            copy = pltpu.make_async_copy(
                rows_of(lefts[i][part], half, part),
                left.at[pl.ds(part * half, half), pl.ds(i * width, width)], lsem.at[i, part])
            waits.append((copy, away != 2))
            pl.when(away != 2)(copy.start)

        @pl.when(away == 2)
        def _():
            left[:, i * width:(i + 1) * width] = jnp.zeros((rows, width), BF16)

        for ref, here in ((own, (away == 0) | (away == 2)), (near, away == 1), (other, away == 3)):
            for slot in range(2):
                copy = pltpu.make_async_copy(
                    ref.at[slot, pl.ds(low, width), :],
                    right.at[pl.ds(i * width, width), pl.ds(slot * cols, cols)],
                    rsem.at[i, slot])
                waits.append((copy, here))
                pl.when(here)(copy.start)
    for copy, here in waits:
        pl.when(here)(copy.wait)
    for slot in range(2):
        outs[slot][...] = jnp.dot(
            left[...], right[:, slot * cols:(slot + 1) * cols], preferred_element_type=F32)


def early(lefts, steps, rights):
    rows, width = 2 * lefts[0].shape[0], lefts[0].shape[1]
    cols = rights[0].shape[2]
    n = len(steps)
    out = jax.ShapeDtypeStruct((rows, cols), F32)
    return pl.pallas_call(
        functools.partial(early_kernel, steps),
        out_shape=(out,) * 2,
        in_specs=[ANY] * (2 * n + 3),
        out_specs=(VM,) * 2,
        scratch_shapes=[
            pltpu.VMEM((rows, n * width), BF16),
            pltpu.VMEM((n * width, 2 * cols), BF16),
            pltpu.SemaphoreType.DMA((n, 2)),
            pltpu.SemaphoreType.DMA((n, 2)),
        ],
        compiler_params=vmem(16),
        name="early",
    )(*lefts, *rights)


def middle_kernel(steps, *refs):
    n = len(steps)
    own_ref, other_ref, *end = refs[:4]
    lefts, refs = halves(refs[4:4 + 2 * n]), refs[4 + 2 * n:]
    rights, refs = refs[:3], refs[3:]
    own_out, other_out, rows_out, left_out, right, lsem, rsem = refs
    rows, width = end[0].shape
    half = rows // 2
    cols = own_out.shape[1]
    z, r = lax.axis_index("col") // 2, lax.axis_index("row")
    waits = []

    def copy(source, target, sem, here):
        one = pltpu.make_async_copy(source, target, sem)
        pl.when(here)(one.start)
        waits.append(lambda: pl.when(here)(one.wait))

    for i, (step, ref) in enumerate(((-3, right), (4, rows_out))):
        away, low = meeting(step)
        low = pl.multiple_of(low * width, width)
        for j, source in zip((0, 1, 3), rights):
            for slot in range(2):
                copy(source.at[slot, pl.ds(low, width), :],
                     ref.at[:, pl.ds(slot * cols, cols)], rsem.at[i, slot], away == j)

        @pl.when(away == 2)
        def _():
            ref[...] = jnp.zeros_like(ref)

    for q in range(2):
        source = 2 * lax.rem(r + 2, 4) + q
        step = lax.rem((z - source) * side() + 16, 8)
        at = pl.ds(q * width, width)
        for i, ref in enumerate([*lefts, end]):
            for part in range(2):
                copy(rows_of(ref[part], half, part), left_out.at[pl.ds(part * half, half), at], lsem.at[q, part],
                     step == (*steps, -3)[i] % 8)

        @pl.when(step == 4)
        def _():
            left_out[:, q * width:(q + 1) * width] = jnp.zeros((rows, width), BF16)

    for wait in waits:
        wait()
    for slot, (ref, out) in enumerate(((own_ref, own_out), (other_ref, other_out))):
        for part in range(2):
            at = slice(part * half, (part + 1) * half)
            out[at, :] = ref[at, :] + jnp.dot(
                end[part][at, :], right[:, slot * cols:(slot + 1) * cols],
                preferred_element_type=F32)


def middle(acc, end, lefts, steps, rights):
    rows, width = end[0].shape
    cols = acc[0].shape[1]
    n = len(steps)
    out = jax.ShapeDtypeStruct((rows, cols), F32)
    return pl.pallas_call(
        functools.partial(middle_kernel, steps),
        out_shape=(
            out, out,
            jax.ShapeDtypeStruct((width, 2 * cols), BF16),
            jax.ShapeDtypeStruct((rows, 2 * width), BF16),
        ),
        in_specs=[VM] * 4 + [ANY] * (2 * n + 3),
        out_specs=(VM,) * 4,
        scratch_shapes=[
            pltpu.VMEM((width, 2 * cols), BF16),
            pltpu.SemaphoreType.DMA((2, 2)),
            pltpu.SemaphoreType.DMA((2, 2)),
        ],
        compiler_params=vmem(16),
        name="middle",
    )(*acc, *end, *lefts, *rights)


def columns(ref, ds, base, width):
    layer = lax.axis_index("layer")
    parts = [
        ref[:, pl.ds(pl.multiple_of(base + lax.rem(layer + d, 4) * width, width), width)]
        for d in ds
    ]
    return parts[0] if len(parts) == 1 else jnp.concatenate(parts, axis=1)


def piece(slot, ds, acc_ref, top_ref, low_ref, rows_ref, left_ref, far_ref):
    cols = acc_ref.shape[1]
    width = cols // 4
    away, low = meeting(4)
    deep = rows_ref.shape[0]
    here = pl.ds(pl.multiple_of(low * deep, deep), deep)
    rows = jnp.where(
        away == 2,
        columns(far_ref.at[slot, here, :], ds, 0, width),
        columns(rows_ref, ds, slot * cols, width))
    last = [jnp.dot(ref[...], rows, preferred_element_type=F32) for ref in (top_ref, low_ref)]
    return (
        columns(acc_ref, ds, 0, width)
        + jnp.concatenate(last, axis=0)
        + jnp.dot(left_ref[...], columns(far_ref.at[slot], ds, 0, width), preferred_element_type=F32)
    )


def others_kernel(ds, *refs):
    refs[-1][...] = piece(1, ds, *refs[:-1]).astype(BF16)


def others(ds, acc, late):
    rows, cols = acc.shape
    return pl.pallas_call(
        functools.partial(others_kernel, ds),
        out_shape=jax.ShapeDtypeStruct((rows, cols // 4 * len(ds)), BF16),
        in_specs=[VM] * 6,
        out_specs=VM,
        compiler_params=vmem(6),
        name="others",
    )(acc, *late)


def owns_kernel(ds, *refs):
    (got_ref, *refs), outs = refs[:7], refs[7:]
    width = outs[0].shape[1]
    sums = piece(0, ds, *refs) + got_ref[:, :width * len(ds)].astype(F32)
    for i, out in enumerate(outs):
        out[...] = sums[:, i * width:(i + 1) * width].astype(BF16)


def owns(ds, got, acc, late):
    rows, cols = acc.shape
    return pl.pallas_call(
        functools.partial(owns_kernel, ds),
        out_shape=(jax.ShapeDtypeStruct((rows, cols // 4), BF16),) * len(ds),
        in_specs=[VM] * 7,
        out_specs=(VM,) * len(ds),
        compiler_params=vmem(4),
        name="owns",
    )(got, acc, *late)


def total_kernel(p1, p2, p3, keep_ref, got_ref, *refs):
    *late, out_ref, part = refs
    layer = lax.axis_index("layer")
    rows, width = p1.shape
    atoms = rows // BLOCK
    got = got_ref[:, got_ref.shape[1] - width:].astype(F32)
    part[...] = (piece(0, (0,), *late) + got).astype(BF16)
    pieces = (part, p1, p2, p3)
    flags = widen(keep_ref[...], width)
    for value in range(4):

        @pl.when(layer == value)
        def _():
            for a in range(2):
                two = [pieces[(value - 2 * a - b) % 4][...].astype(F32) for b in range(2)]
                kept = tall(flags[a * atoms:(a + 1) * atoms]) > 0.5
                both = jnp.where(kept, two[0] + two[1], 0.0)
                out_ref[a * rows:(a + 1) * rows, :] = both.astype(BF16)


def total(moved, keep_t, got, acc, late):
    rows, width = moved[0].shape
    return pl.pallas_call(
        total_kernel,
        out_shape=jax.ShapeDtypeStruct((2 * rows, width), BF16),
        in_specs=[VM] * 11,
        out_specs=VM,
        scratch_shapes=[pltpu.VMEM((rows, width), BF16)],
        compiler_params=vmem(8),
        name="total",
    )(*moved, keep_t, got, acc, *late)


def stream(x, d):
    return lax.ppermute(
        x, "col", [(c, (c // 2 + (d if c % 2 == 0 else -d)) % 8 * 2 + c % 2) for c in range(16)])


def along(x, axis, d):
    return lax.ppermute(x, axis, [(i, (i + d) % 4) for i in range(4)])


def swap(x):
    return lax.ppermute(x, "col", [(c, c ^ 1) for c in range(16)])


def turn(x, d):
    pairs = []
    for r in range(4):
        for c in range(16):
            to = (r + (d if c % 2 == 0 else -d)) % 4
            pairs.append((r * 16 + c, to * 16 + c))
    return lax.ppermute(x, ("row", "col"), pairs)


def after(x, y):
    return lax.optimization_barrier((x, y))[0]


def on_device(matrix, pattern, keep):
    matrix = pltpu.with_memory_space_constraint(matrix, pltpu.HBM)
    pattern_t = pltpu.with_memory_space_constraint(pattern.T, pltpu.HBM)
    block, top, low, mine, theirs = prepare(matrix, pattern_t)
    theirs = swap(theirs)
    both = jnp.stack([mine, theirs])

    left = {0: (top, low)}
    down = block
    for step in range(1, 5):
        left[step] = tuple(stream(x, 1) for x in left[step - 1])
        if step < 4:
            down = stream(down, -1)
            left[-step] = (down, down)
    near, other = turn(both, 1), turn(both, -1)
    far = turn(after(near, (left[2], left[-2])), 1)

    steps = (0, 1, -1, 2, -2, 3)
    lefts, rights = [x for step in steps for x in left[step]], [both, near, other]
    acc = early(lefts, steps, rights)
    own, theirs, rows, meet = middle(acc, left[-3], lefts, steps, rights)
    late = [*left[4], rows, meet, far]
    sent = others((1, 3), theirs, late)
    got = swap(others((2, 0), after(theirs, sent), late))
    part1, part3 = owns((1, 3), swap(sent), own, late)
    (part2,) = owns((2,), got, own, late)
    moved = [along(part1, "layer", 1), along(part2, "layer", 2), along(part3, "layer", 3)]
    return total(moved, keep.T, got, own, late)


def solution(mesh):
    in_specs = (P("row", "col"), P("row", "col"), P("row", ("col", "layer")))
    out_specs = P("row", ("col", "layer"))
    return jax.shard_map(
        on_device, mesh=mesh, in_specs=in_specs, out_specs=out_specs, check_vma=False
    )
```

time: 80.6 us -> 77.4 us (0.960)
  the two profiles are of different devices: /device:TPU:8 before, /device:TPU:1 now
where the time goes in v5:
time: 77.4 us; the launch traced here: 77.3 us
  waiting for transfers between devices  33.1 us (43%)
  starting transfers between devices  32.7 us (42%)
  Pallas kernels  11.3 us (15%)
    ppermute x11, waiting for transfers between devices, stream(): lax.ppermute(x, 'col', [(c, (c // 2 + (d if c % 2 == 0 else -d)) % 8 * 2...  20.9 us
    ppermute x11, starting transfers between devices, stream(): lax.ppermute(x, 'col', [(c, (c // 2 + (d if c % 2 == 0 else -d)) % 8 * 2...  19.5 us
    ppermute x3, waiting for transfers between devices, along(): return lax.ppermute(x, axis, [(i, (i + d) % 4) for i in range(4)])  9.2 us
    ppermute x3, starting transfers between devices, along(): return lax.ppermute(x, axis, [(i, (i + d) % 4) for i in range(4)])  5.58 us
    ppermute x3, starting transfers between devices, swap(): return lax.ppermute(x, 'col', [(c, c ^ 1) for c in range(16)])  5.46 us
    pallas_call x1, Pallas kernels, early(): pl.pallas_call(functools.partial(early_kernel, steps), out_shape=(out,) *...  4.5 us
    ppermute x3, waiting for transfers between devices, swap(): return lax.ppermute(x, 'col', [(c, c ^ 1) for c in range(16)])  2.97 us
    ppermute x3, starting transfers between devices, turn(): return lax.ppermute(x, ('row', 'col'), pairs)  2.18 us
  transfers between devices with their start and end apart: 20, of which 10 were waited for; matrix products, arithmetic and copies ran while one was open for 0% of the time, Pallas kernels for 9%

profile of v5, /device:TPU:1, one launch (start us, length us, event | category | flops | bytes accessed | tf_op | source)
XLA Modules:
  0.0 77.3 jit_solution(9957346410034280368)
XLA Ops:
  0.0 1.5 %prepare.1 = (bf16[1024,256]{1,0:T(8,128)(2,1)S(1)}, bf16[512,256]{1,0:T(8,128)(2,1)S(1)}, bf16[512,256]{1,0:T(8,128)(2,1)S(1)}, bf16[512,512]{1,0:T(8,128)(2,1)S(1)}, bf16[512,512]{1,0:T(8,128)(2,1)S(1)}) custom-call(bf16[2048,512]{1,0:T(8,128)(2,1)} %x_ref.1, s32[16,64]{1,0:T(8,128)} %bitcast.7), custom_call_target="tpu_custom_call" | custom-call | tf_op jit(solution)/shard_map/prepare/pallas_call | solution.py:86
  1.5 3.3 %collective-permute-start.8 = (bf16[512,512]{1,0:T(8,128)(2,1)S(1)}, bf16[512,512]{1,0:T(8,128)(2,1)S(1)}, u32[]{:S(2)}, u32[]{:S(2)}) collective-permute-start(bf16[512,512]{1,0:T(8,128)(2,1)S(1)} %get-tuple-element.24), channel_id=1, source_target_pairs={{0,4},{4,0},{8,12},{12,8},{16,20},{20,16},{24,28},{28,24},{32,36},... | collective-permute-start | bytes 1572872 | tf_op jit(solution)/shard_map/ppermute | solution.py:360
  4.8 1.5 %collective-permute-done.8 = bf16[512,512]{1,0:T(8,128)(2,1)S(1)} collective-permute-done((bf16[512,512]{1,0:T(8,128)(2,1)S(1)}, bf16[512,512]{1,0:T(8,128)(2,1)S(1)}, u32[]{:S(2)}, u32[]{:S(2)}) %collective-permute-start.8) | collective-permute-done | bytes 524320 | tf_op jit(solution)/shard_map/ppermute | solution.py:360
  6.5 1.2 %collective-permute-start.9 = (bf16[2,512,512]{2,1,0:T(8,128)(2,1)S(1)}, bf16[2,512,512]{2,1,0:T(8,128)(2,1)S(1)}, u32[]{:S(2)}, u32[]{:S(2)}) collective-permute-start(bf16[2,512,512]{2,1,0:T(8,128)(2,1)S(1)} %pad_maximum_fusion.refs_12_.refs_16_), channel_id=1, source_target_pairs={{0,64},{4,196},{8,72},{12,204},{16,80},{20,212},{24,88},{28,220},{... | collective-permute-start | bytes 3145736 | tf_op jit(solution)/shard_map/ppermute | solution.py:369
  7.7 5.5 %collective-permute-start = (bf16[512,256]{1,0:T(8,128)(2,1)S(1)}, bf16[512,256]{1,0:T(8,128)(2,1)S(1)}, u32[]{:S(2)}, u32[]{:S(2)}) collective-permute-start(bf16[512,256]{1,0:T(8,128)(2,1)S(1)} %get-tuple-element.20.refs_0_.refs_4_), channel_id=1, source_target_pairs={{0,8},{4,60},{8,16},{12,4},{16,24},{20,12},{24,32},{28,20},{32,40}... | collective-permute-start | bytes 786440 | tf_op jit(solution)/shard_map/ppermute | solution.py:351
  13.9 2.0 %collective-permute-done.2.refs_4_.refs_5_.refs_8_.refs_9_ = bf16[1024,256]{1,0:T(8,128)(2,1)S(1)} collective-permute-done((bf16[1024,256]{1,0:T(8,128)(2,1)S(1)}, bf16[1024,256]{1,0:T(8,128)(2,1)S(1)}, u32[]{:S(2)}, u32[]{:S(2)}) %collective-permute-start.2) | collective-permute-done | bytes 524320 | tf_op jit(solution)/shard_map/ppermute | solution.py:351
  15.8 2.3 %collective-permute-done.refs_2_.refs_6_ = bf16[512,256]{1,0:T(8,128)(2,1)S(1)} collective-permute-done((bf16[512,256]{1,0:T(8,128)(2,1)S(1)}, bf16[512,256]{1,0:T(8,128)(2,1)S(1)}, u32[]{:S(2)}, u32[]{:S(2)}) %collective-permute-start) | collective-permute-done | bytes 262176 | tf_op jit(solution)/shard_map/ppermute | solution.py:351
  18.2 3.4 %collective-permute-start.3 = (bf16[512,256]{1,0:T(8,128)(2,1)S(1)}, bf16[512,256]{1,0:T(8,128)(2,1)S(1)}, u32[]{:S(2)}, u32[]{:S(2)}) collective-permute-start(bf16[512,256]{1,0:T(8,128)(2,1)S(1)} %collective-permute-done.refs_2_.refs_6_), channel_id=1, source_target_pairs={{0,8},{4,60},{8,16},{12,4},{16,24},{20,12},{24,32},{28,20},{32,40}... | collective-permute-start | bytes 786440 | tf_op jit(solution)/shard_map/ppermute | solution.py:351
  21.6 2.8 %collective-permute-start.4 = (bf16[512,256]{1,0:T(8,128)(2,1)S(1)}, bf16[512,256]{1,0:T(8,128)(2,1)S(1)}, u32[]{:S(2)}, u32[]{:S(2)}) collective-permute-start(bf16[512,256]{1,0:T(8,128)(2,1)S(1)} %collective-permute-done.1.refs_3_.refs_7_), channel_id=1, source_target_pairs={{0,8},{4,60},{8,16},{12,4},{16,24},{20,12},{24,32},{28,20},{32,40}... | collective-permute-start | bytes 786440 | tf_op jit(solution)/shard_map/ppermute | solution.py:351
  25.4 2.3 %collective-permute-done.3.refs_6_.refs_10_ = bf16[512,256]{1,0:T(8,128)(2,1)S(1)} collective-permute-done((bf16[512,256]{1,0:T(8,128)(2,1)S(1)}, bf16[512,256]{1,0:T(8,128)(2,1)S(1)}, u32[]{:S(2)}, u32[]{:S(2)}) %collective-permute-start.3) | collective-permute-done | bytes 262176 | tf_op jit(solution)/shard_map/ppermute | solution.py:351
  27.7 5.3 %collective-permute-done.4.refs_7_.refs_11_ = bf16[512,256]{1,0:T(8,128)(2,1)S(1)} collective-permute-done((bf16[512,256]{1,0:T(8,128)(2,1)S(1)}, bf16[512,256]{1,0:T(8,128)(2,1)S(1)}, u32[]{:S(2)}, u32[]{:S(2)}) %collective-permute-start.4) | collective-permute-done | bytes 262176 | tf_op jit(solution)/shard_map/ppermute | solution.py:351
  33.0 1.8 %collective-permute-start.11 = (bf16[1024,256]{1,0:T(8,128)(2,1)S(1)}, bf16[1024,256]{1,0:T(8,128)(2,1)S(1)}, u32[]{:S(2)}, u32[]{:S(2)}) collective-permute-start(bf16[1024,256]{1,0:T(8,128)(2,1)S(1)} %collective-permute-done.5.refs_8_.refs_9_.refs_12_.refs_13_), channel_id=1, source_target_pairs={{0,56},{4,12},{8,0},{12,20},{16,8},{20,28},{24,16},{28,36},{32,24}... | collective-permute-start | bytes 1572872 | tf_op jit(solution)/shard_map/ppermute | solution.py:351
  34.8 1.5 %collective-permute-start.6 = (bf16[512,256]{1,0:T(8,128)(2,1)S(1)}, bf16[512,256]{1,0:T(8,128)(2,1)S(1)}, u32[]{:S(2)}, u32[]{:S(2)}) collective-permute-start(bf16[512,256]{1,0:T(8,128)(2,1)S(1)} %collective-permute-done.3.refs_6_.refs_10_), channel_id=1, source_target_pairs={{0,8},{4,60},{8,16},{12,4},{16,24},{20,12},{24,32},{28,20},{32,40}... | collective-permute-start | bytes 786440 | tf_op jit(solution)/shard_map/ppermute | solution.py:351
  36.3 1.5 %collective-permute-start.7 = (bf16[512,256]{1,0:T(8,128)(2,1)S(1)}, bf16[512,256]{1,0:T(8,128)(2,1)S(1)}, u32[]{:S(2)}, u32[]{:S(2)}) collective-permute-start(bf16[512,256]{1,0:T(8,128)(2,1)S(1)} %collective-permute-done.4.refs_7_.refs_11_), channel_id=1, source_target_pairs={{0,8},{4,60},{8,16},{12,4},{16,24},{20,12},{24,32},{28,20},{32,40}... | collective-permute-start | bytes 786440 | tf_op jit(solution)/shard_map/ppermute | solution.py:351
  37.8 4.5 %collective-permute-done.6.refs_10_.refs_14_ = bf16[512,256]{1,0:T(8,128)(2,1)S(1)} collective-permute-done((bf16[512,256]{1,0:T(8,128)(2,1)S(1)}, bf16[512,256]{1,0:T(8,128)(2,1)S(1)}, u32[]{:S(2)}, u32[]{:S(2)}) %collective-permute-start.6) | collective-permute-done | bytes 262176 | tf_op jit(solution)/shard_map/ppermute | solution.py:351
  43.5 4.4 %collective-permute-done.7.refs_11_.refs_15_ = bf16[512,256]{1,0:T(8,128)(2,1)S(1)} collective-permute-done((bf16[512,256]{1,0:T(8,128)(2,1)S(1)}, bf16[512,256]{1,0:T(8,128)(2,1)S(1)}, u32[]{:S(2)}, u32[]{:S(2)}) %collective-permute-start.7) | collective-permute-done | bytes 262176 | tf_op jit(solution)/shard_map/ppermute | solution.py:351
  49.1 4.5 %early.1 = (f32[1024,512]{1,0:T(8,128)S(1)}, f32[1024,512]{1,0:T(8,128)S(1)}) custom-call(bf16[512,256]{1,0:T(8,128)(2,1)S(1)} %get-tuple-element.20.refs_0_.refs_4_, bf16[512,256]{1,0:T(8,128)(2,1)S(1)} %get-tuple-element.21.refs_1_.refs_5_, bf16[512,256]{1,0:T(8,128)(2,1)S(1)} %collective-permute-done.refs_2_.refs_6_, ...), custom_call_target="tpu_custom_call" | custom-call | tf_op jit(solution)/shard_map/early/pallas_call | solution.py:162
  56.1 2.0 %collective-permute-start.17 = (bf16[1024,256]{1,0:T(8,128)(2,1)S(1)}, bf16[1024,256]{1,0:T(8,128)(2,1)S(1)}, u32[]{:S(2)}, u32[]{:S(2)}) collective-permute-start(bf16[1024,256]{1,0:T(8,128)(2,1)S(1)} %others.3), channel_id=1, source_target_pairs={{0,4},{4,0},{8,12},{12,8},{16,20},{20,16},{24,28},{28,24},{32,36},... | collective-permute-start | bytes 1572872 | tf_op jit(solution)/shard_map/ppermute | solution.py:360
  58.2 1.4 %collective-permute-done.17.refs_0_.got_ref = bf16[1024,256]{1,0:T(8,128)(2,1)S(1)} collective-permute-done((bf16[1024,256]{1,0:T(8,128)(2,1)S(1)}, bf16[1024,256]{1,0:T(8,128)(2,1)S(1)}, u32[]{:S(2)}, u32[]{:S(2)}) %collective-permute-start.17) | collective-permute-done | bytes 524320 | tf_op jit(solution)/shard_map/ppermute | solution.py:360
  60.3 2.8 %collective-permute-start.18 = (bf16[1024,128]{1,0:T(8,128)(2,1)S(1)}, bf16[1024,128]{1,0:T(8,128)(2,1)S(1)}, u32[]{:S(2)}, u32[]{:S(2)}) collective-permute-start(bf16[1024,128]{1,0:T(8,128)(2,1)S(1)} %owns.3), channel_id=1, source_target_pairs={{0,2},{1,3},{2,0},{3,1},{4,6},{5,7},{6,4},{7,5},{8,10},{9,11},{10,... | collective-permute-start | bytes 786440 | tf_op jit(solution)/shard_map/ppermute | solution.py:356
  64.1 2.4 %collective-permute-start.19 = (bf16[1024,128]{1,0:T(8,128)(2,1)S(1)}, bf16[1024,128]{1,0:T(8,128)(2,1)S(1)}, u32[]{:S(2)}, u32[]{:S(2)}) collective-permute-start(bf16[1024,128]{1,0:T(8,128)(2,1)S(1)} %get-tuple-element.34), channel_id=1, source_target_pairs={{0,3},{1,0},{2,1},{3,2},{4,7},{5,4},{6,5},{7,6},{8,11},{9,8},{10,9... | collective-permute-start | bytes 786440 | tf_op jit(solution)/shard_map/ppermute | solution.py:356
  66.5 2.9 %collective-permute-done.18.p2 = bf16[1024,128]{1,0:T(8,128)(2,1)S(1)} collective-permute-done((bf16[1024,128]{1,0:T(8,128)(2,1)S(1)}, bf16[1024,128]{1,0:T(8,128)(2,1)S(1)}, u32[]{:S(2)}, u32[]{:S(2)}) %collective-permute-start.18) | collective-permute-done | bytes 262176 | tf_op jit(solution)/shard_map/ppermute | solution.py:356
  69.4 6.3 %collective-permute-done.16.p1 = bf16[1024,128]{1,0:T(8,128)(2,1)S(1)} collective-permute-done((bf16[1024,128]{1,0:T(8,128)(2,1)S(1)}, bf16[1024,128]{1,0:T(8,128)(2,1)S(1)}, u32[]{:S(2)}, u32[]{:S(2)}) %collective-permute-start.16) | collective-permute-done | bytes 262176 | tf_op jit(solution)/shard_map/ppermute | solution.py:356
  75.7 1.6 %total.1 = bf16[2048,128]{1,0:T(8,128)(2,1)} custom-call(bf16[1024,128]{1,0:T(8,128)(2,1)S(1)} %collective-permute-done.16.p1, bf16[1024,128]{1,0:T(8,128)(2,1)S(1)} %collective-permute-done.18.p2, bf16[1024,128]{1,0:T(8,128)(2,1)S(1)} %collective-permute-done.19.p3, s32[4,64]{1,0:T(4,128)S(1)} %bitcast.5, ...), custom_call_target="tpu_custom_call" | custom-call | tf_op jit(solution)/shard_map/total/pallas_call | solution.py:339
  (27 shorter events, 8.4 us)
Async XLA Ops:
  1.5 4.9 %collective-permute-start.8 = (bf16[512,512]{1,0:T(8,128)(2,1)S(1)}, bf16[512,512]{1,0:T(8,128)(2,1)S(1)}, u32[]{:S(2)}, u32[]{:S(2)}) collective-permute-start(bf16[512,512]{1,0:T(8,128)(2,1)S(1)} %get-tuple-element.24), channel_id=1, source_target_pairs={{0,4},{4,0},{8,12},{12,8},{16,20},{20,16},{24,28},{28,24},{32,36},... | collective-permute-start | bytes 1572872 | tf_op jit(solution)/shard_map/ppermute | solution.py:360
  4.8 11.0 %collective-permute-start.2 = (bf16[1024,256]{1,0:T(8,128)(2,1)S(1)}, bf16[1024,256]{1,0:T(8,128)(2,1)S(1)}, u32[]{:S(2)}, u32[]{:S(2)}) collective-permute-start(bf16[1024,256]{1,0:T(8,128)(2,1)S(1)} %get-tuple-element.22), channel_id=1, source_target_pairs={{0,56},{4,12},{8,0},{12,20},{16,8},{20,28},{24,16},{28,36},{32,24}... | collective-permute-start | bytes 1572872 | tf_op jit(solution)/shard_map/ppermute | solution.py:351
  6.5 26.5 %collective-permute-start.9 = (bf16[2,512,512]{2,1,0:T(8,128)(2,1)S(1)}, bf16[2,512,512]{2,1,0:T(8,128)(2,1)S(1)}, u32[]{:S(2)}, u32[]{:S(2)}) collective-permute-start(bf16[2,512,512]{2,1,0:T(8,128)(2,1)S(1)} %pad_maximum_fusion.refs_12_.refs_16_), channel_id=1, source_target_pairs={{0,64},{4,196},{8,72},{12,204},{16,80},{20,212},{24,88},{28,220},{... | collective-permute-start | bytes 3145736 | tf_op jit(solution)/shard_map/ppermute | solution.py:369
  7.7 10.5 %collective-permute-start = (bf16[512,256]{1,0:T(8,128)(2,1)S(1)}, bf16[512,256]{1,0:T(8,128)(2,1)S(1)}, u32[]{:S(2)}, u32[]{:S(2)}) collective-permute-start(bf16[512,256]{1,0:T(8,128)(2,1)S(1)} %get-tuple-element.20.refs_0_.refs_4_), channel_id=1, source_target_pairs={{0,8},{4,60},{8,16},{12,4},{16,24},{20,12},{24,32},{28,20},{32,40}... | collective-permute-start | bytes 786440 | tf_op jit(solution)/shard_map/ppermute | solution.py:351
  13.1 8.4 %collective-permute-start.1 = (bf16[512,256]{1,0:T(8,128)(2,1)S(1)}, bf16[512,256]{1,0:T(8,128)(2,1)S(1)}, u32[]{:S(2)}, u32[]{:S(2)}) collective-permute-start(bf16[512,256]{1,0:T(8,128)(2,1)S(1)} %get-tuple-element.21.refs_1_.refs_5_), channel_id=1, source_target_pairs={{0,8},{4,60},{8,16},{12,4},{16,24},{20,12},{24,32},{28,20},{32,40}... | collective-permute-start | bytes 786440 | tf_op jit(solution)/shard_map/ppermute | solution.py:351
  15.8 17.2 %collective-permute-start.5 = (bf16[1024,256]{1,0:T(8,128)(2,1)S(1)}, bf16[1024,256]{1,0:T(8,128)(2,1)S(1)}, u32[]{:S(2)}, u32[]{:S(2)}) collective-permute-start(bf16[1024,256]{1,0:T(8,128)(2,1)S(1)} %collective-permute-done.2.refs_4_.refs_5_.refs_8_.refs_9_), channel_id=1, source_target_pairs={{0,56},{4,12},{8,0},{12,20},{16,8},{20,28},{24,16},{28,36},{32,24}... | collective-permute-start | bytes 1572872 | tf_op jit(solution)/shard_map/ppermute | solution.py:351
  18.2 9.5 %collective-permute-start.3 = (bf16[512,256]{1,0:T(8,128)(2,1)S(1)}, bf16[512,256]{1,0:T(8,128)(2,1)S(1)}, u32[]{:S(2)}, u32[]{:S(2)}) collective-permute-start(bf16[512,256]{1,0:T(8,128)(2,1)S(1)} %collective-permute-done.refs_2_.refs_6_), channel_id=1, source_target_pairs={{0,8},{4,60},{8,16},{12,4},{16,24},{20,12},{24,32},{28,20},{32,40}... | collective-permute-start | bytes 786440 | tf_op jit(solution)/shard_map/ppermute | solution.py:351
  21.6 11.4 %collective-permute-start.4 = (bf16[512,256]{1,0:T(8,128)(2,1)S(1)}, bf16[512,256]{1,0:T(8,128)(2,1)S(1)}, u32[]{:S(2)}, u32[]{:S(2)}) collective-permute-start(bf16[512,256]{1,0:T(8,128)(2,1)S(1)} %collective-permute-done.1.refs_3_.refs_7_), channel_id=1, source_target_pairs={{0,8},{4,60},{8,16},{12,4},{16,24},{20,12},{24,32},{28,20},{32,40}... | collective-permute-start | bytes 786440 | tf_op jit(solution)/shard_map/ppermute | solution.py:351
  24.4 24.7 %collective-permute-start.10 = (bf16[2,512,512]{2,1,0:T(8,128)(2,1)S(1)}, bf16[2,512,512]{2,1,0:T(8,128)(2,1)S(1)}, u32[]{:S(2)}, u32[]{:S(2)}) collective-permute-start(bf16[2,512,512]{2,1,0:T(8,128)(2,1)S(1)} %pad_maximum_fusion.refs_12_.refs_16_), channel_id=1, source_target_pairs={{0,192},{4,68},{8,200},{12,76},{16,208},{20,84},{24,216},{28,92},{... | collective-permute-start | bytes 3145736 | tf_op jit(solution)/shard_map/ppermute | solution.py:369
  33.0 21.8 %collective-permute-start.14 = (bf16[2,512,512]{2,1,0:T(8,128)(2,1)S(1)}, bf16[2,512,512]{2,1,0:T(8,128)(2,1)S(1)}, u32[]{:S(2)}, u32[]{:S(2)}) collective-permute-start(bf16[2,512,512]{2,1,0:T(8,128)(2,1)S(1)} %collective-permute-done.9.refs_13_.refs_17_), channel_id=1, source_target_pairs={{0,64},{4,196},{8,72},{12,204},{16,80},{20,212},{24,88},{28,220},{... | collective-permute-start | bytes 3145736 | tf_op jit(solution)/shard_map/ppermute | solution.py:369
  33.0 20.6 %collective-permute-start.11 = (bf16[1024,256]{1,0:T(8,128)(2,1)S(1)}, bf16[1024,256]{1,0:T(8,128)(2,1)S(1)}, u32[]{:S(2)}, u32[]{:S(2)}) collective-permute-start(bf16[1024,256]{1,0:T(8,128)(2,1)S(1)} %collective-permute-done.5.refs_8_.refs_9_.refs_12_.refs_13_), channel_id=1, source_target_pairs={{0,56},{4,12},{8,0},{12,20},{16,8},{20,28},{24,16},{28,36},{32,24}... | collective-permute-start | bytes 1572872 | tf_op jit(solution)/shard_map/ppermute | solution.py:351
  34.8 7.5 %collective-permute-start.6 = (bf16[512,256]{1,0:T(8,128)(2,1)S(1)}, bf16[512,256]{1,0:T(8,128)(2,1)S(1)}, u32[]{:S(2)}, u32[]{:S(2)}) collective-permute-start(bf16[512,256]{1,0:T(8,128)(2,1)S(1)} %collective-permute-done.3.refs_6_.refs_10_), channel_id=1, source_target_pairs={{0,8},{4,60},{8,16},{12,4},{16,24},{20,12},{24,32},{28,20},{32,40}... | collective-permute-start | bytes 786440 | tf_op jit(solution)/shard_map/ppermute | solution.py:351
  36.3 11.6 %collective-permute-start.7 = (bf16[512,256]{1,0:T(8,128)(2,1)S(1)}, bf16[512,256]{1,0:T(8,128)(2,1)S(1)}, u32[]{:S(2)}, u32[]{:S(2)}) collective-permute-start(bf16[512,256]{1,0:T(8,128)(2,1)S(1)} %collective-permute-done.4.refs_7_.refs_11_), channel_id=1, source_target_pairs={{0,8},{4,60},{8,16},{12,4},{16,24},{20,12},{24,32},{28,20},{32,40}... | collective-permute-start | bytes 786440 | tf_op jit(solution)/shard_map/ppermute | solution.py:351
  42.3 12.5 %collective-permute-start.12 = (bf16[512,256]{1,0:T(8,128)(2,1)S(1)}, bf16[512,256]{1,0:T(8,128)(2,1)S(1)}, u32[]{:S(2)}, u32[]{:S(2)}) collective-permute-start(bf16[512,256]{1,0:T(8,128)(2,1)S(1)} %collective-permute-done.6.refs_10_.refs_14_), channel_id=1, source_target_pairs={{0,8},{4,60},{8,16},{12,4},{16,24},{20,12},{24,32},{28,20},{32,40}... | collective-permute-start | bytes 786440 | tf_op jit(solution)/shard_map/ppermute | solution.py:351
  47.9 6.9 %collective-permute-start.13 = (bf16[512,256]{1,0:T(8,128)(2,1)S(1)}, bf16[512,256]{1,0:T(8,128)(2,1)S(1)}, u32[]{:S(2)}, u32[]{:S(2)}) collective-permute-start(bf16[512,256]{1,0:T(8,128)(2,1)S(1)} %collective-permute-done.7.refs_11_.refs_15_), channel_id=1, source_target_pairs={{0,8},{4,60},{8,16},{12,4},{16,24},{20,12},{24,32},{28,20},{32,40}... | collective-permute-start | bytes 786440 | tf_op jit(solution)/shard_map/ppermute | solution.py:351
  56.1 3.6 %collective-permute-start.17 = (bf16[1024,256]{1,0:T(8,128)(2,1)S(1)}, bf16[1024,256]{1,0:T(8,128)(2,1)S(1)}, u32[]{:S(2)}, u32[]{:S(2)}) collective-permute-start(bf16[1024,256]{1,0:T(8,128)(2,1)S(1)} %others.3), channel_id=1, source_target_pairs={{0,4},{4,0},{8,12},{12,8},{16,20},{20,16},{24,28},{28,24},{32,36},... | collective-permute-start | bytes 1572872 | tf_op jit(solution)/shard_map/ppermute | solution.py:360
  58.1 5.0 %collective-permute-start.15 = (bf16[1024,256]{1,0:T(8,128)(2,1)S(1)}, bf16[1024,256]{1,0:T(8,128)(2,1)S(1)}, u32[]{:S(2)}, u32[]{:S(2)}) collective-permute-start(bf16[1024,256]{1,0:T(8,128)(2,1)S(1)} %others.2), channel_id=1, source_target_pairs={{0,4},{4,0},{8,12},{12,8},{16,20},{20,16},{24,28},{28,24},{32,36},... | collective-permute-start | bytes 1572872 | tf_op jit(solution)/shard_map/ppermute | solution.py:360
  60.2 15.5 %copy-start = (s32[64,4]{0,1:T(4,128)S(1)}, s32[64,4]{0,1:T(4,128)}, u32[]{:S(2)}) copy-start(s32[64,4]{0,1:T(4,128)} %param.5) | copy-start | bytes 3076
  60.3 9.1 %collective-permute-start.18 = (bf16[1024,128]{1,0:T(8,128)(2,1)S(1)}, bf16[1024,128]{1,0:T(8,128)(2,1)S(1)}, u32[]{:S(2)}, u32[]{:S(2)}) collective-permute-start(bf16[1024,128]{1,0:T(8,128)(2,1)S(1)} %owns.3), channel_id=1, source_target_pairs={{0,2},{1,3},{2,0},{3,1},{4,6},{5,7},{6,4},{7,5},{8,10},{9,11},{10,... | collective-permute-start | bytes 786440 | tf_op jit(solution)/shard_map/ppermute | solution.py:356
  63.7 12.0 %collective-permute-start.16 = (bf16[1024,128]{1,0:T(8,128)(2,1)S(1)}, bf16[1024,128]{1,0:T(8,128)(2,1)S(1)}, u32[]{:S(2)}, u32[]{:S(2)}) collective-permute-start(bf16[1024,128]{1,0:T(8,128)(2,1)S(1)} %get-tuple-element.32), channel_id=1, source_target_pairs={{0,1},{1,2},{2,3},{3,0},{4,5},{5,6},{6,7},{7,4},{8,9},{9,10},{10,1... | collective-permute-start | bytes 786440 | tf_op jit(solution)/shard_map/ppermute | solution.py:356
  64.1 11.6 %collective-permute-start.19 = (bf16[1024,128]{1,0:T(8,128)(2,1)S(1)}, bf16[1024,128]{1,0:T(8,128)(2,1)S(1)}, u32[]{:S(2)}, u32[]{:S(2)}) collective-permute-start(bf16[1024,128]{1,0:T(8,128)(2,1)S(1)} %get-tuple-element.34), channel_id=1, source_target_pairs={{0,3},{1,0},{2,1},{3,2},{4,7},{5,4},{6,5},{7,6},{8,11},{9,8},{10,9... | collective-permute-start | bytes 786440 | tf_op jit(solution)/shard_map/ppermute | solution.py:356

commit v6 on v5

--- a/solution.py
+++ b/solution.py
@@ -298,50 +298,59 @@
     (got_ref, *refs), outs = refs[:7], refs[7:]
     width = outs[0].shape[1]
     sums = piece(0, ds, *refs) + got_ref[:, :width * len(ds)].astype(F32)
+    half = outs[0].shape[0]
     for i, out in enumerate(outs):
-        out[...] = sums[:, i * width:(i + 1) * width].astype(BF16)
+        k, part = i % len(ds), i // len(ds)
+        out[...] = sums[part * half:(part + 1) * half, k * width:(k + 1) * width].astype(BF16)
 
 
 def owns(ds, got, acc, late):
     rows, cols = acc.shape
     return pl.pallas_call(
         functools.partial(owns_kernel, ds),
-        out_shape=(jax.ShapeDtypeStruct((rows, cols // 4), BF16),) * len(ds),
+        out_shape=(jax.ShapeDtypeStruct((rows // 2, cols // 4), BF16),) * (2 * len(ds)),
         in_specs=[VM] * 7,
-        out_specs=(VM,) * len(ds),
+        out_specs=(VM,) * (2 * len(ds)),
         compiler_params=vmem(4),
         name="owns",
     )(got, acc, *late)
 
 
-def total_kernel(p1, p2, p3, keep_ref, got_ref, *refs):
-    *late, out_ref, part = refs
+def total_kernel(*refs):
+    moved, (keep_ref, got_ref, *late, out_ref, part) = refs[:6], refs[6:]
     layer = lax.axis_index("layer")
-    rows, width = p1.shape
-    atoms = rows // BLOCK
+    rows, width = part.shape
+    half = rows // 2
+    atoms = half // BLOCK
     got = got_ref[:, got_ref.shape[1] - width:].astype(F32)
     part[...] = (piece(0, (0,), *late) + got).astype(BF16)
-    pieces = (part, p1, p2, p3)
     flags = widen(keep_ref[...], width)
+
+    def held(d, p):
+        ref = part.at[p * half:(p + 1) * half, :] if d == 0 else moved[2 * (d - 1) + p]
+        return ref[...].astype(F32)
+
     for value in range(4):
 
         @pl.when(layer == value)
         def _():
             for a in range(2):
-                two = [pieces[(value - 2 * a - b) % 4][...].astype(F32) for b in range(2)]
-                kept = tall(flags[a * atoms:(a + 1) * atoms]) > 0.5
-                both = jnp.where(kept, two[0] + two[1], 0.0)
-                out_ref[a * rows:(a + 1) * rows, :] = both.astype(BF16)
+                for p in range(2):
+                    two = [held((value - 2 * a - b) % 4, p) for b in range(2)]
+                    at = 2 * a + p
+                    kept = tall(flags[at * atoms:(at + 1) * atoms]) > 0.5
+                    out_ref[at * half:(at + 1) * half, :] = jnp.where(
+                        kept, two[0] + two[1], 0.0).astype(BF16)
 
 
 def total(moved, keep_t, got, acc, late):
-    rows, width = moved[0].shape
+    half, width = moved[0].shape
     return pl.pallas_call(
         total_kernel,
-        out_shape=jax.ShapeDtypeStruct((2 * rows, width), BF16),
-        in_specs=[VM] * 11,
+        out_shape=jax.ShapeDtypeStruct((4 * half, width), BF16),
+        in_specs=[VM] * 14,
         out_specs=VM,
-        scratch_shapes=[pltpu.VMEM((rows, width), BF16)],
+        scratch_shapes=[pltpu.VMEM((2 * half, width), BF16)],
         compiler_params=vmem(8),
         name="total",
     )(*moved, keep_t, got, acc, *late)
@@ -397,10 +406,12 @@
     late = [*left[4], rows, meet, far]
     sent = others((1, 3), theirs, late)
     got = swap(others((2, 0), after(theirs, sent), late))
-    part1, part3 = owns((1, 3), swap(sent), own, late)
-    (part2,) = owns((2,), got, own, late)
-    moved = [along(part1, "layer", 1), along(part2, "layer", 2), along(part3, "layer", 3)]
-    return total(moved, keep.T, got, own, late)
+    moved = {}
+    for ds, arrived in (((1, 3), swap(sent)), ((2,), got)):
+        for i, part in enumerate(owns(ds, arrived, own, late)):
+            d = ds[i % len(ds)]
+            moved[d, i // len(ds)] = along(part, "layer", d)
+    return total([moved[d, p] for d in (1, 2, 3) for p in range(2)], keep.T, got, own, late)
 
 
 def solution(mesh):

time: 77.4 us -> 77.4 us (level)
  waiting for transfers between devices: 33.1 us -> 30.5 us
  starting transfers between devices: 32.7 us -> 35.3 us
    ppermute x3 -> x6, waiting for transfers between devices: 9.2 us -> 6.62 us  [along(): return lax.ppermute(x, axis, [(i, (i + d) % 4) for i in range(4)])]
    ppermute x3 -> x6, starting transfers between devices: 5.58 us -> 8.12 us  [along(): return lax.ppermute(x, axis, [(i, (i + d) % 4) for i in range(4)])]
  transfers between devices with their start and end apart: 20 -> 23, of which waited for: 10 -> 11; matrix products, arithmetic and copies ran while one was open for 0% -> 0% of each run, Pallas kernels for 9% -> 9%
where the time goes in v6:
time: 77.4 us; the launch traced here: 77.3 us
  starting transfers between devices  35.3 us (46%)
  waiting for transfers between devices  30.5 us (39%)
  Pallas kernels  11.3 us (15%)
    ppermute x11, waiting for transfers between devices, stream(): lax.ppermute(x, 'col', [(c, (c // 2 + (d if c % 2 == 0 else -d)) % 8 * 2...  20.9 us
    ppermute x11, starting transfers between devices, stream(): lax.ppermute(x, 'col', [(c, (c // 2 + (d if c % 2 == 0 else -d)) % 8 * 2...  19.5 us
    ppermute x6, starting transfers between devices, along(): return lax.ppermute(x, axis, [(i, (i + d) % 4) for i in range(4)])  8.12 us
    ppermute x6, waiting for transfers between devices, along(): return lax.ppermute(x, axis, [(i, (i + d) % 4) for i in range(4)])  6.62 us
    ppermute x3, starting transfers between devices, swap(): return lax.ppermute(x, 'col', [(c, c ^ 1) for c in range(16)])  5.46 us
    pallas_call x1, Pallas kernels, early(): pl.pallas_call(functools.partial(early_kernel, steps), out_shape=(out,) *...  4.5 us
    ppermute x3, waiting for transfers between devices, swap(): return lax.ppermute(x, 'col', [(c, c ^ 1) for c in range(16)])  2.97 us
    ppermute x3, starting transfers between devices, turn(): return lax.ppermute(x, ('row', 'col'), pairs)  2.18 us
  transfers between devices with their start and end apart: 23, of which 11 were waited for; matrix products, arithmetic and copies ran while one was open for 0% of the time, Pallas kernels for 9%

profile of v6, /device:TPU:1, one launch (start us, length us, event | category | flops | bytes accessed | tf_op | source)
XLA Modules:
  0.0 77.3 jit_solution(16259366461422179200)
XLA Ops:
  0.0 1.5 %prepare.1 = (bf16[1024,256]{1,0:T(8,128)(2,1)S(1)}, bf16[512,256]{1,0:T(8,128)(2,1)S(1)}, bf16[512,256]{1,0:T(8,128)(2,1)S(1)}, bf16[512,512]{1,0:T(8,128)(2,1)S(1)}, bf16[512,512]{1,0:T(8,128)(2,1)S(1)}) custom-call(bf16[2048,512]{1,0:T(8,128)(2,1)} %x_ref.1, s32[16,64]{1,0:T(8,128)} %bitcast.7), custom_call_target="tpu_custom_call" | custom-call | tf_op jit(solution)/shard_map/prepare/pallas_call | solution.py:86
  1.5 3.3 %collective-permute-start.8 = (bf16[512,512]{1,0:T(8,128)(2,1)S(1)}, bf16[512,512]{1,0:T(8,128)(2,1)S(1)}, u32[]{:S(2)}, u32[]{:S(2)}) collective-permute-start(bf16[512,512]{1,0:T(8,128)(2,1)S(1)} %get-tuple-element.28), channel_id=1, source_target_pairs={{0,4},{4,0},{8,12},{12,8},{16,20},{20,16},{24,28},{28,24},{32,36},... | collective-permute-start | bytes 1572872 | tf_op jit(solution)/shard_map/ppermute | solution.py:369
  4.8 1.5 %collective-permute-done.8 = bf16[512,512]{1,0:T(8,128)(2,1)S(1)} collective-permute-done((bf16[512,512]{1,0:T(8,128)(2,1)S(1)}, bf16[512,512]{1,0:T(8,128)(2,1)S(1)}, u32[]{:S(2)}, u32[]{:S(2)}) %collective-permute-start.8) | collective-permute-done | bytes 524320 | tf_op jit(solution)/shard_map/ppermute | solution.py:369
  7.7 5.5 %collective-permute-start = (bf16[512,256]{1,0:T(8,128)(2,1)S(1)}, bf16[512,256]{1,0:T(8,128)(2,1)S(1)}, u32[]{:S(2)}, u32[]{:S(2)}) collective-permute-start(bf16[512,256]{1,0:T(8,128)(2,1)S(1)} %get-tuple-element.24.refs_0_.refs_4_), channel_id=1, source_target_pairs={{0,8},{4,60},{8,16},{12,4},{16,24},{20,12},{24,32},{28,20},{32,40}... | collective-permute-start | bytes 786440 | tf_op jit(solution)/shard_map/ppermute | solution.py:360
  13.9 2.0 %collective-permute-done.2.refs_4_.refs_5_.refs_8_.refs_9_ = bf16[1024,256]{1,0:T(8,128)(2,1)S(1)} collective-permute-done((bf16[1024,256]{1,0:T(8,128)(2,1)S(1)}, bf16[1024,256]{1,0:T(8,128)(2,1)S(1)}, u32[]{:S(2)}, u32[]{:S(2)}) %collective-permute-start.2) | collective-permute-done | bytes 524320 | tf_op jit(solution)/shard_map/ppermute | solution.py:360
  15.8 2.3 %collective-permute-done.refs_2_.refs_6_ = bf16[512,256]{1,0:T(8,128)(2,1)S(1)} collective-permute-done((bf16[512,256]{1,0:T(8,128)(2,1)S(1)}, bf16[512,256]{1,0:T(8,128)(2,1)S(1)}, u32[]{:S(2)}, u32[]{:S(2)}) %collective-permute-start) | collective-permute-done | bytes 262176 | tf_op jit(solution)/shard_map/ppermute | solution.py:360
  18.2 3.4 %collective-permute-start.3 = (bf16[512,256]{1,0:T(8,128)(2,1)S(1)}, bf16[512,256]{1,0:T(8,128)(2,1)S(1)}, u32[]{:S(2)}, u32[]{:S(2)}) collective-permute-start(bf16[512,256]{1,0:T(8,128)(2,1)S(1)} %collective-permute-done.refs_2_.refs_6_), channel_id=1, source_target_pairs={{0,8},{4,60},{8,16},{12,4},{16,24},{20,12},{24,32},{28,20},{32,40}... | collective-permute-start | bytes 786440 | tf_op jit(solution)/shard_map/ppermute | solution.py:360
  21.6 2.8 %collective-permute-start.4 = (bf16[512,256]{1,0:T(8,128)(2,1)S(1)}, bf16[512,256]{1,0:T(8,128)(2,1)S(1)}, u32[]{:S(2)}, u32[]{:S(2)}) collective-permute-start(bf16[512,256]{1,0:T(8,128)(2,1)S(1)} %collective-permute-done.1.refs_3_.refs_7_), channel_id=1, source_target_pairs={{0,8},{4,60},{8,16},{12,4},{16,24},{20,12},{24,32},{28,20},{32,40}... | collective-permute-start | bytes 786440 | tf_op jit(solution)/shard_map/ppermute | solution.py:360
  25.4 2.3 %collective-permute-done.3.refs_6_.refs_10_ = bf16[512,256]{1,0:T(8,128)(2,1)S(1)} collective-permute-done((bf16[512,256]{1,0:T(8,128)(2,1)S(1)}, bf16[512,256]{1,0:T(8,128)(2,1)S(1)}, u32[]{:S(2)}, u32[]{:S(2)}) %collective-permute-start.3) | collective-permute-done | bytes 262176 | tf_op jit(solution)/shard_map/ppermute | solution.py:360
  27.7 5.3 %collective-permute-done.4.refs_7_.refs_11_ = bf16[512,256]{1,0:T(8,128)(2,1)S(1)} collective-permute-done((bf16[512,256]{1,0:T(8,128)(2,1)S(1)}, bf16[512,256]{1,0:T(8,128)(2,1)S(1)}, u32[]{:S(2)}, u32[]{:S(2)}) %collective-permute-start.4) | collective-permute-done | bytes 262176 | tf_op jit(solution)/shard_map/ppermute | solution.py:360
  33.0 1.8 %collective-permute-start.11 = (bf16[1024,256]{1,0:T(8,128)(2,1)S(1)}, bf16[1024,256]{1,0:T(8,128)(2,1)S(1)}, u32[]{:S(2)}, u32[]{:S(2)}) collective-permute-start(bf16[1024,256]{1,0:T(8,128)(2,1)S(1)} %collective-permute-done.5.refs_8_.refs_9_.refs_12_.refs_13_), channel_id=1, source_target_pairs={{0,56},{4,12},{8,0},{12,20},{16,8},{20,28},{24,16},{28,36},{32,24}... | collective-permute-start | bytes 1572872 | tf_op jit(solution)/shard_map/ppermute | solution.py:360
  34.8 1.5 %collective-permute-start.6 = (bf16[512,256]{1,0:T(8,128)(2,1)S(1)}, bf16[512,256]{1,0:T(8,128)(2,1)S(1)}, u32[]{:S(2)}, u32[]{:S(2)}) collective-permute-start(bf16[512,256]{1,0:T(8,128)(2,1)S(1)} %collective-permute-done.3.refs_6_.refs_10_), channel_id=1, source_target_pairs={{0,8},{4,60},{8,16},{12,4},{16,24},{20,12},{24,32},{28,20},{32,40}... | collective-permute-start | bytes 786440 | tf_op jit(solution)/shard_map/ppermute | solution.py:360
  36.3 1.5 %collective-permute-start.7 = (bf16[512,256]{1,0:T(8,128)(2,1)S(1)}, bf16[512,256]{1,0:T(8,128)(2,1)S(1)}, u32[]{:S(2)}, u32[]{:S(2)}) collective-permute-start(bf16[512,256]{1,0:T(8,128)(2,1)S(1)} %collective-permute-done.4.refs_7_.refs_11_), channel_id=1, source_target_pairs={{0,8},{4,60},{8,16},{12,4},{16,24},{20,12},{24,32},{28,20},{32,40}... | collective-permute-start | bytes 786440 | tf_op jit(solution)/shard_map/ppermute | solution.py:360
  37.8 4.5 %collective-permute-done.6.refs_10_.refs_14_ = bf16[512,256]{1,0:T(8,128)(2,1)S(1)} collective-permute-done((bf16[512,256]{1,0:T(8,128)(2,1)S(1)}, bf16[512,256]{1,0:T(8,128)(2,1)S(1)}, u32[]{:S(2)}, u32[]{:S(2)}) %collective-permute-start.6) | collective-permute-done | bytes 262176 | tf_op jit(solution)/shard_map/ppermute | solution.py:360
  43.5 4.4 %collective-permute-done.7.refs_11_.refs_15_ = bf16[512,256]{1,0:T(8,128)(2,1)S(1)} collective-permute-done((bf16[512,256]{1,0:T(8,128)(2,1)S(1)}, bf16[512,256]{1,0:T(8,128)(2,1)S(1)}, u32[]{:S(2)}, u32[]{:S(2)}) %collective-permute-start.7) | collective-permute-done | bytes 262176 | tf_op jit(solution)/shard_map/ppermute | solution.py:360
  49.1 4.5 %early.1 = (f32[1024,512]{1,0:T(8,128)S(1)}, f32[1024,512]{1,0:T(8,128)S(1)}) custom-call(bf16[512,256]{1,0:T(8,128)(2,1)S(1)} %get-tuple-element.24.refs_0_.refs_4_, bf16[512,256]{1,0:T(8,128)(2,1)S(1)} %get-tuple-element.25.refs_1_.refs_5_, bf16[512,256]{1,0:T(8,128)(2,1)S(1)} %collective-permute-done.refs_2_.refs_6_, ...), custom_call_target="tpu_custom_call" | custom-call | tf_op jit(solution)/shard_map/early/pallas_call | solution.py:162
  56.1 2.0 %collective-permute-start.18 = (bf16[1024,256]{1,0:T(8,128)(2,1)S(1)}, bf16[1024,256]{1,0:T(8,128)(2,1)S(1)}, u32[]{:S(2)}, u32[]{:S(2)}) collective-permute-start(bf16[1024,256]{1,0:T(8,128)(2,1)S(1)} %others.3), channel_id=1, source_target_pairs={{0,4},{4,0},{8,12},{12,8},{16,20},{20,16},{24,28},{28,24},{32,36},... | collective-permute-start | bytes 1572872 | tf_op jit(solution)/shard_map/ppermute | solution.py:369
  58.2 1.4 %collective-permute-done.18.refs_0_.refs_7_ = bf16[1024,256]{1,0:T(8,128)(2,1)S(1)} collective-permute-done((bf16[1024,256]{1,0:T(8,128)(2,1)S(1)}, bf16[1024,256]{1,0:T(8,128)(2,1)S(1)}, u32[]{:S(2)}, u32[]{:S(2)}) %collective-permute-start.18) | collective-permute-done | bytes 524320 | tf_op jit(solution)/shard_map/ppermute | solution.py:369
  60.2 2.8 %collective-permute-start.19 = (bf16[512,128]{1,0:T(8,128)(2,1)S(1)}, bf16[512,128]{1,0:T(8,128)(2,1)S(1)}, u32[]{:S(2)}, u32[]{:S(2)}) collective-permute-start(bf16[512,128]{1,0:T(8,128)(2,1)S(1)} %get-tuple-element.39), channel_id=1, source_target_pairs={{0,2},{1,3},{2,0},{3,1},{4,6},{5,7},{6,4},{7,5},{8,10},{9,11},{10,... | collective-permute-start | bytes 393224 | tf_op jit(solution)/shard_map/ppermute | solution.py:365
  64.0 1.3 %collective-permute-start.16 = (bf16[512,128]{1,0:T(8,128)(2,1)S(1)}, bf16[512,128]{1,0:T(8,128)(2,1)S(1)}, u32[]{:S(2)}, u32[]{:S(2)}) collective-permute-start(bf16[512,128]{1,0:T(8,128)(2,1)S(1)} %get-tuple-element.36), channel_id=1, source_target_pairs={{0,1},{1,2},{2,3},{3,0},{4,5},{5,6},{6,7},{7,4},{8,9},{9,10},{10,1... | collective-permute-start | bytes 393224 | tf_op jit(solution)/shard_map/ppermute | solution.py:365
  66.4 1.4 %collective-permute-start.21 = (bf16[512,128]{1,0:T(8,128)(2,1)S(1)}, bf16[512,128]{1,0:T(8,128)(2,1)S(1)}, u32[]{:S(2)}, u32[]{:S(2)}) collective-permute-start(bf16[512,128]{1,0:T(8,128)(2,1)S(1)} %get-tuple-element.41), channel_id=1, source_target_pairs={{0,3},{1,0},{2,1},{3,2},{4,7},{5,4},{6,5},{7,6},{8,11},{9,8},{10,9... | collective-permute-start | bytes 393224 | tf_op jit(solution)/shard_map/ppermute | solution.py:365
  69.1 3.8 %collective-permute-done.16.refs_0_ = bf16[512,128]{1,0:T(8,128)(2,1)S(1)} collective-permute-done((bf16[512,128]{1,0:T(8,128)(2,1)S(1)}, bf16[512,128]{1,0:T(8,128)(2,1)S(1)}, u32[]{:S(2)}, u32[]{:S(2)}) %collective-permute-start.16) | collective-permute-done | bytes 131104 | tf_op jit(solution)/shard_map/ppermute | solution.py:365
  72.8 2.8 %collective-permute-done.17.refs_1_ = bf16[512,128]{1,0:T(8,128)(2,1)S(1)} collective-permute-done((bf16[512,128]{1,0:T(8,128)(2,1)S(1)}, bf16[512,128]{1,0:T(8,128)(2,1)S(1)}, u32[]{:S(2)}, u32[]{:S(2)}) %collective-permute-start.17) | collective-permute-done | bytes 131104 | tf_op jit(solution)/shard_map/ppermute | solution.py:365
  75.7 1.6 %total.1 = bf16[2048,128]{1,0:T(8,128)(2,1)} custom-call(bf16[512,128]{1,0:T(8,128)(2,1)S(1)} %collective-permute-done.16.refs_0_, bf16[512,128]{1,0:T(8,128)(2,1)S(1)} %collective-permute-done.17.refs_1_, bf16[512,128]{1,0:T(8,128)(2,1)S(1)} %collective-permute-done.19.refs_2_, bf16[512,128]{1,0:T(8,128)(2,1)S(1)} %collective-permute-done.20.refs_3_, ...), custom_call_target="tpu_custom_call" | custom-call | tf_op jit(solution)/shard_map/total/pallas_call | solution.py:348
  (33 shorter events, 11.8 us)
Async XLA Ops:
  1.5 4.9 %collective-permute-start.8 = (bf16[512,512]{1,0:T(8,128)(2,1)S(1)}, bf16[512,512]{1,0:T(8,128)(2,1)S(1)}, u32[]{:S(2)}, u32[]{:S(2)}) collective-permute-start(bf16[512,512]{1,0:T(8,128)(2,1)S(1)} %get-tuple-element.28), channel_id=1, source_target_pairs={{0,4},{4,0},{8,12},{12,8},{16,20},{20,16},{24,28},{28,24},{32,36},... | collective-permute-start | bytes 1572872 | tf_op jit(solution)/shard_map/ppermute | solution.py:369
  4.8 11.0 %collective-permute-start.2 = (bf16[1024,256]{1,0:T(8,128)(2,1)S(1)}, bf16[1024,256]{1,0:T(8,128)(2,1)S(1)}, u32[]{:S(2)}, u32[]{:S(2)}) collective-permute-start(bf16[1024,256]{1,0:T(8,128)(2,1)S(1)} %get-tuple-element.26), channel_id=1, source_target_pairs={{0,56},{4,12},{8,0},{12,20},{16,8},{20,28},{24,16},{28,36},{32,24}... | collective-permute-start | bytes 1572872 | tf_op jit(solution)/shard_map/ppermute | solution.py:360
  6.5 26.5 %collective-permute-start.9 = (bf16[2,512,512]{2,1,0:T(8,128)(2,1)S(1)}, bf16[2,512,512]{2,1,0:T(8,128)(2,1)S(1)}, u32[]{:S(2)}, u32[]{:S(2)}) collective-permute-start(bf16[2,512,512]{2,1,0:T(8,128)(2,1)S(1)} %pad_maximum_fusion.refs_12_.refs_16_), channel_id=1, source_target_pairs={{0,64},{4,196},{8,72},{12,204},{16,80},{20,212},{24,88},{28,220},{... | collective-permute-start | bytes 3145736 | tf_op jit(solution)/shard_map/ppermute | solution.py:378
  7.7 10.5 %collective-permute-start = (bf16[512,256]{1,0:T(8,128)(2,1)S(1)}, bf16[512,256]{1,0:T(8,128)(2,1)S(1)}, u32[]{:S(2)}, u32[]{:S(2)}) collective-permute-start(bf16[512,256]{1,0:T(8,128)(2,1)S(1)} %get-tuple-element.24.refs_0_.refs_4_), channel_id=1, source_target_pairs={{0,8},{4,60},{8,16},{12,4},{16,24},{20,12},{24,32},{28,20},{32,40}... | collective-permute-start | bytes 786440 | tf_op jit(solution)/shard_map/ppermute | solution.py:360
  13.1 8.4 %collective-permute-start.1 = (bf16[512,256]{1,0:T(8,128)(2,1)S(1)}, bf16[512,256]{1,0:T(8,128)(2,1)S(1)}, u32[]{:S(2)}, u32[]{:S(2)}) collective-permute-start(bf16[512,256]{1,0:T(8,128)(2,1)S(1)} %get-tuple-element.25.refs_1_.refs_5_), channel_id=1, source_target_pairs={{0,8},{4,60},{8,16},{12,4},{16,24},{20,12},{24,32},{28,20},{32,40}... | collective-permute-start | bytes 786440 | tf_op jit(solution)/shard_map/ppermute | solution.py:360
  15.8 17.2 %collective-permute-start.5 = (bf16[1024,256]{1,0:T(8,128)(2,1)S(1)}, bf16[1024,256]{1,0:T(8,128)(2,1)S(1)}, u32[]{:S(2)}, u32[]{:S(2)}) collective-permute-start(bf16[1024,256]{1,0:T(8,128)(2,1)S(1)} %collective-permute-done.2.refs_4_.refs_5_.refs_8_.refs_9_), channel_id=1, source_target_pairs={{0,56},{4,12},{8,0},{12,20},{16,8},{20,28},{24,16},{28,36},{32,24}... | collective-permute-start | bytes 1572872 | tf_op jit(solution)/shard_map/ppermute | solution.py:360
  18.2 9.5 %collective-permute-start.3 = (bf16[512,256]{1,0:T(8,128)(2,1)S(1)}, bf16[512,256]{1,0:T(8,128)(2,1)S(1)}, u32[]{:S(2)}, u32[]{:S(2)}) collective-permute-start(bf16[512,256]{1,0:T(8,128)(2,1)S(1)} %collective-permute-done.refs_2_.refs_6_), channel_id=1, source_target_pairs={{0,8},{4,60},{8,16},{12,4},{16,24},{20,12},{24,32},{28,20},{32,40}... | collective-permute-start | bytes 786440 | tf_op jit(solution)/shard_map/ppermute | solution.py:360
  21.6 11.4 %collective-permute-start.4 = (bf16[512,256]{1,0:T(8,128)(2,1)S(1)}, bf16[512,256]{1,0:T(8,128)(2,1)S(1)}, u32[]{:S(2)}, u32[]{:S(2)}) collective-permute-start(bf16[512,256]{1,0:T(8,128)(2,1)S(1)} %collective-permute-done.1.refs_3_.refs_7_), channel_id=1, source_target_pairs={{0,8},{4,60},{8,16},{12,4},{16,24},{20,12},{24,32},{28,20},{32,40}... | collective-permute-start | bytes 786440 | tf_op jit(solution)/shard_map/ppermute | solution.py:360
  24.4 24.7 %collective-permute-start.10 = (bf16[2,512,512]{2,1,0:T(8,128)(2,1)S(1)}, bf16[2,512,512]{2,1,0:T(8,128)(2,1)S(1)}, u32[]{:S(2)}, u32[]{:S(2)}) collective-permute-start(bf16[2,512,512]{2,1,0:T(8,128)(2,1)S(1)} %pad_maximum_fusion.refs_12_.refs_16_), channel_id=1, source_target_pairs={{0,192},{4,68},{8,200},{12,76},{16,208},{20,84},{24,216},{28,92},{... | collective-permute-start | bytes 3145736 | tf_op jit(solution)/shard_map/ppermute | solution.py:378
  33.0 21.8 %collective-permute-start.14 = (bf16[2,512,512]{2,1,0:T(8,128)(2,1)S(1)}, bf16[2,512,512]{2,1,0:T(8,128)(2,1)S(1)}, u32[]{:S(2)}, u32[]{:S(2)}) collective-permute-start(bf16[2,512,512]{2,1,0:T(8,128)(2,1)S(1)} %collective-permute-done.9.refs_13_.refs_17_), channel_id=1, source_target_pairs={{0,64},{4,196},{8,72},{12,204},{16,80},{20,212},{24,88},{28,220},{... | collective-permute-start | bytes 3145736 | tf_op jit(solution)/shard_map/ppermute | solution.py:378
  33.0 20.6 %collective-permute-start.11 = (bf16[1024,256]{1,0:T(8,128)(2,1)S(1)}, bf16[1024,256]{1,0:T(8,128)(2,1)S(1)}, u32[]{:S(2)}, u32[]{:S(2)}) collective-permute-start(bf16[1024,256]{1,0:T(8,128)(2,1)S(1)} %collective-permute-done.5.refs_8_.refs_9_.refs_12_.refs_13_), channel_id=1, source_target_pairs={{0,56},{4,12},{8,0},{12,20},{16,8},{20,28},{24,16},{28,36},{32,24}... | collective-permute-start | bytes 1572872 | tf_op jit(solution)/shard_map/ppermute | solution.py:360
  34.8 7.5 %collective-permute-start.6 = (bf16[512,256]{1,0:T(8,128)(2,1)S(1)}, bf16[512,256]{1,0:T(8,128)(2,1)S(1)}, u32[]{:S(2)}, u32[]{:S(2)}) collective-permute-start(bf16[512,256]{1,0:T(8,128)(2,1)S(1)} %collective-permute-done.3.refs_6_.refs_10_), channel_id=1, source_target_pairs={{0,8},{4,60},{8,16},{12,4},{16,24},{20,12},{24,32},{28,20},{32,40}... | collective-permute-start | bytes 786440 | tf_op jit(solution)/shard_map/ppermute | solution.py:360
  36.3 11.6 %collective-permute-start.7 = (bf16[512,256]{1,0:T(8,128)(2,1)S(1)}, bf16[512,256]{1,0:T(8,128)(2,1)S(1)}, u32[]{:S(2)}, u32[]{:S(2)}) collective-permute-start(bf16[512,256]{1,0:T(8,128)(2,1)S(1)} %collective-permute-done.4.refs_7_.refs_11_), channel_id=1, source_target_pairs={{0,8},{4,60},{8,16},{12,4},{16,24},{20,12},{24,32},{28,20},{32,40}... | collective-permute-start | bytes 786440 | tf_op jit(solution)/shard_map/ppermute | solution.py:360
  42.3 12.5 %collective-permute-start.12 = (bf16[512,256]{1,0:T(8,128)(2,1)S(1)}, bf16[512,256]{1,0:T(8,128)(2,1)S(1)}, u32[]{:S(2)}, u32[]{:S(2)}) collective-permute-start(bf16[512,256]{1,0:T(8,128)(2,1)S(1)} %collective-permute-done.6.refs_10_.refs_14_), channel_id=1, source_target_pairs={{0,8},{4,60},{8,16},{12,4},{16,24},{20,12},{24,32},{28,20},{32,40}... | collective-permute-start | bytes 786440 | tf_op jit(solution)/shard_map/ppermute | solution.py:360
  47.9 6.9 %collective-permute-start.13 = (bf16[512,256]{1,0:T(8,128)(2,1)S(1)}, bf16[512,256]{1,0:T(8,128)(2,1)S(1)}, u32[]{:S(2)}, u32[]{:S(2)}) collective-permute-start(bf16[512,256]{1,0:T(8,128)(2,1)S(1)} %collective-permute-done.7.refs_11_.refs_15_), channel_id=1, source_target_pairs={{0,8},{4,60},{8,16},{12,4},{16,24},{20,12},{24,32},{28,20},{32,40}... | collective-permute-start | bytes 786440 | tf_op jit(solution)/shard_map/ppermute | solution.py:360
  56.1 3.6 %collective-permute-start.18 = (bf16[1024,256]{1,0:T(8,128)(2,1)S(1)}, bf16[1024,256]{1,0:T(8,128)(2,1)S(1)}, u32[]{:S(2)}, u32[]{:S(2)}) collective-permute-start(bf16[1024,256]{1,0:T(8,128)(2,1)S(1)} %others.3), channel_id=1, source_target_pairs={{0,4},{4,0},{8,12},{12,8},{16,20},{20,16},{24,28},{28,24},{32,36},... | collective-permute-start | bytes 1572872 | tf_op jit(solution)/shard_map/ppermute | solution.py:369
  58.1 5.2 %collective-permute-start.15 = (bf16[1024,256]{1,0:T(8,128)(2,1)S(1)}, bf16[1024,256]{1,0:T(8,128)(2,1)S(1)}, u32[]{:S(2)}, u32[]{:S(2)}) collective-permute-start(bf16[1024,256]{1,0:T(8,128)(2,1)S(1)} %others.2), channel_id=1, source_target_pairs={{0,4},{4,0},{8,12},{12,8},{16,20},{20,16},{24,28},{28,24},{32,36},... | collective-permute-start | bytes 1572872 | tf_op jit(solution)/shard_map/ppermute | solution.py:369
  60.2 7.6 %collective-permute-start.19 = (bf16[512,128]{1,0:T(8,128)(2,1)S(1)}, bf16[512,128]{1,0:T(8,128)(2,1)S(1)}, u32[]{:S(2)}, u32[]{:S(2)}) collective-permute-start(bf16[512,128]{1,0:T(8,128)(2,1)S(1)} %get-tuple-element.39), channel_id=1, source_target_pairs={{0,2},{1,3},{2,0},{3,1},{4,6},{5,7},{6,4},{7,5},{8,10},{9,11},{10,... | collective-permute-start | bytes 393224 | tf_op jit(solution)/shard_map/ppermute | solution.py:365
  63.1 12.6 %copy-start = (s32[64,4]{0,1:T(4,128)S(1)}, s32[64,4]{0,1:T(4,128)}, u32[]{:S(2)}) copy-start(s32[64,4]{0,1:T(4,128)} %param.5) | copy-start | bytes 3076
  63.1 6.0 %collective-permute-start.20 = (bf16[512,128]{1,0:T(8,128)(2,1)S(1)}, bf16[512,128]{1,0:T(8,128)(2,1)S(1)}, u32[]{:S(2)}, u32[]{:S(2)}) collective-permute-start(bf16[512,128]{1,0:T(8,128)(2,1)S(1)} %get-tuple-element.40), channel_id=1, source_target_pairs={{0,2},{1,3},{2,0},{3,1},{4,6},{5,7},{6,4},{7,5},{8,10},{9,11},{10,... | collective-permute-start | bytes 393224 | tf_op jit(solution)/shard_map/ppermute | solution.py:365
  64.0 8.9 %collective-permute-start.16 = (bf16[512,128]{1,0:T(8,128)(2,1)S(1)}, bf16[512,128]{1,0:T(8,128)(2,1)S(1)}, u32[]{:S(2)}, u32[]{:S(2)}) collective-permute-start(bf16[512,128]{1,0:T(8,128)(2,1)S(1)} %get-tuple-element.36), channel_id=1, source_target_pairs={{0,1},{1,2},{2,3},{3,0},{4,5},{5,6},{6,7},{7,4},{8,9},{9,10},{10,1... | collective-permute-start | bytes 393224 | tf_op jit(solution)/shard_map/ppermute | solution.py:365
  65.2 10.4 %collective-permute-start.17 = (bf16[512,128]{1,0:T(8,128)(2,1)S(1)}, bf16[512,128]{1,0:T(8,128)(2,1)S(1)}, u32[]{:S(2)}, u32[]{:S(2)}) collective-permute-start(bf16[512,128]{1,0:T(8,128)(2,1)S(1)} %get-tuple-element.37), channel_id=1, source_target_pairs={{0,1},{1,2},{2,3},{3,0},{4,5},{5,6},{6,7},{7,4},{8,9},{9,10},{10,1... | collective-permute-start | bytes 393224 | tf_op jit(solution)/shard_map/ppermute | solution.py:365
  66.4 9.2 %collective-permute-start.21 = (bf16[512,128]{1,0:T(8,128)(2,1)S(1)}, bf16[512,128]{1,0:T(8,128)(2,1)S(1)}, u32[]{:S(2)}, u32[]{:S(2)}) collective-permute-start(bf16[512,128]{1,0:T(8,128)(2,1)S(1)} %get-tuple-element.41), channel_id=1, source_target_pairs={{0,3},{1,0},{2,1},{3,2},{4,7},{5,4},{6,5},{7,6},{8,11},{9,8},{10,9... | collective-permute-start | bytes 393224 | tf_op jit(solution)/shard_map/ppermute | solution.py:365
  67.9 7.8 %collective-permute-start.22 = (bf16[512,128]{1,0:T(8,128)(2,1)S(1)}, bf16[512,128]{1,0:T(8,128)(2,1)S(1)}, u32[]{:S(2)}, u32[]{:S(2)}) collective-permute-start(bf16[512,128]{1,0:T(8,128)(2,1)S(1)} %get-tuple-element.42), channel_id=1, source_target_pairs={{0,3},{1,0},{2,1},{3,2},{4,7},{5,4},{6,5},{7,6},{8,11},{9,8},{10,9... | collective-permute-start | bytes 393224 | tf_op jit(solution)/shard_map/ppermute | solution.py:365

commit v7 on v6

--- a/solution.py
+++ b/solution.py
@@ -294,20 +294,20 @@
     )(acc, *late)
 
 
-def owns_kernel(ds, *refs):
+def owns_kernel(ds, skip, *refs):
     (got_ref, *refs), outs = refs[:7], refs[7:]
     width = outs[0].shape[1]
-    sums = piece(0, ds, *refs) + got_ref[:, :width * len(ds)].astype(F32)
+    sums = piece(0, ds, *refs) + got_ref[:, skip * width:(skip + len(ds)) * width].astype(F32)
     half = outs[0].shape[0]
     for i, out in enumerate(outs):
         k, part = i % len(ds), i // len(ds)
         out[...] = sums[part * half:(part + 1) * half, k * width:(k + 1) * width].astype(BF16)
 
 
-def owns(ds, got, acc, late):
+def owns(ds, got, acc, late, skip=0):
     rows, cols = acc.shape
     return pl.pallas_call(
-        functools.partial(owns_kernel, ds),
+        functools.partial(owns_kernel, ds, skip),
         out_shape=(jax.ShapeDtypeStruct((rows // 2, cols // 4), BF16),) * (2 * len(ds)),
         in_specs=[VM] * 7,
         out_specs=(VM,) * (2 * len(ds)),
@@ -317,18 +317,14 @@
 
 
 def total_kernel(*refs):
-    moved, (keep_ref, got_ref, *late, out_ref, part) = refs[:6], refs[6:]
+    pieces, (keep_ref, out_ref) = refs[:8], refs[8:]
     layer = lax.axis_index("layer")
-    rows, width = part.shape
-    half = rows // 2
+    half, width = pieces[0].shape
     atoms = half // BLOCK
-    got = got_ref[:, got_ref.shape[1] - width:].astype(F32)
-    part[...] = (piece(0, (0,), *late) + got).astype(BF16)
     flags = widen(keep_ref[...], width)
 
     def held(d, p):
-        ref = part.at[p * half:(p + 1) * half, :] if d == 0 else moved[2 * (d - 1) + p]
-        return ref[...].astype(F32)
+        return pieces[2 * d + p][...].astype(F32)
 
     for value in range(4):
 
@@ -343,17 +339,16 @@
                         kept, two[0] + two[1], 0.0).astype(BF16)
 
 
-def total(moved, keep_t, got, acc, late):
-    half, width = moved[0].shape
+def total(pieces, keep_t):
+    half, width = pieces[0].shape
     return pl.pallas_call(
         total_kernel,
         out_shape=jax.ShapeDtypeStruct((4 * half, width), BF16),
-        in_specs=[VM] * 14,
+        in_specs=[VM] * 9,
         out_specs=VM,
-        scratch_shapes=[pltpu.VMEM((2 * half, width), BF16)],
         compiler_params=vmem(8),
         name="total",
-    )(*moved, keep_t, got, acc, *late)
+    )(*pieces, keep_t)
 
 
 def stream(x, d):
@@ -411,7 +406,8 @@
         for i, part in enumerate(owns(ds, arrived, own, late)):
             d = ds[i % len(ds)]
             moved[d, i // len(ds)] = along(part, "layer", d)
-    return total([moved[d, p] for d in (1, 2, 3) for p in range(2)], keep.T, got, own, late)
+    moved[0, 0], moved[0, 1] = owns((0,), got, own, late, 1)
+    return total([moved[d, p] for d in range(4) for p in range(2)], keep.T)
 
 
 def solution(mesh):

time: 77.4 us -> 77 us (level)
    pallas_call x2 -> x3, Pallas kernels: 1.24 us -> 1.82 us  [owns(): pl.pallas_call(functools.partial(owns_kernel, ds, skip), out_shape=(jax.S...]
  transfers between devices with their start and end apart: 23 -> 23, of which waited for: 11 -> 10; matrix products, arithmetic and copies ran while one was open for 0% -> 0% of each run, Pallas kernels for 9% -> 10%
where the time goes in v7:
time: 77 us; the launch traced here: 76.8 us
  starting transfers between devices  35.3 us (46%)
  waiting for transfers between devices  29.9 us (39%)
  Pallas kernels  11.4 us (15%)
    ppermute x11, waiting for transfers between devices, stream(): lax.ppermute(x, 'col', [(c, (c // 2 + (d if c % 2 == 0 else -d)) % 8 * 2...  20.9 us
    ppermute x11, starting transfers between devices, stream(): lax.ppermute(x, 'col', [(c, (c // 2 + (d if c % 2 == 0 else -d)) % 8 * 2...  19.5 us
    ppermute x6, starting transfers between devices, along(): return lax.ppermute(x, axis, [(i, (i + d) % 4) for i in range(4)])  8.12 us
    ppermute x6, waiting for transfers between devices, along(): return lax.ppermute(x, axis, [(i, (i + d) % 4) for i in range(4)])  6.03 us
    ppermute x3, starting transfers between devices, swap(): return lax.ppermute(x, 'col', [(c, c ^ 1) for c in range(16)])  5.46 us
    pallas_call x1, Pallas kernels, early(): pl.pallas_call(functools.partial(early_kernel, steps), out_shape=(out,) *...  4.5 us
    ppermute x3, waiting for transfers between devices, swap(): return lax.ppermute(x, 'col', [(c, c ^ 1) for c in range(16)])  2.97 us
    ppermute x3, starting transfers between devices, turn(): return lax.ppermute(x, ('row', 'col'), pairs)  2.18 us
  transfers between devices with their start and end apart: 23, of which 10 were waited for; matrix products, arithmetic and copies ran while one was open for 0% of the time, Pallas kernels for 10%

profile of v7, /device:TPU:1, one launch (start us, length us, event | category | flops | bytes accessed | tf_op | source)
XLA Modules:
  0.0 76.8 jit_solution(5366743000275552703)
XLA Ops:
  0.0 1.5 %prepare.1 = (bf16[1024,256]{1,0:T(8,128)(2,1)S(1)}, bf16[512,256]{1,0:T(8,128)(2,1)S(1)}, bf16[512,256]{1,0:T(8,128)(2,1)S(1)}, bf16[512,512]{1,0:T(8,128)(2,1)S(1)}, bf16[512,512]{1,0:T(8,128)(2,1)S(1)}) custom-call(bf16[2048,512]{1,0:T(8,128)(2,1)} %x_ref.1, s32[16,64]{1,0:T(8,128)} %bitcast.7), custom_call_target="tpu_custom_call" | custom-call | tf_op jit(solution)/shard_map/prepare/pallas_call | solution.py:86
  1.5 3.3 %collective-permute-start.8 = (bf16[512,512]{1,0:T(8,128)(2,1)S(1)}, bf16[512,512]{1,0:T(8,128)(2,1)S(1)}, u32[]{:S(2)}, u32[]{:S(2)}) collective-permute-start(bf16[512,512]{1,0:T(8,128)(2,1)S(1)} %get-tuple-element.30), channel_id=1, source_target_pairs={{0,4},{4,0},{8,12},{12,8},{16,20},{20,16},{24,28},{28,24},{32,36},... | collective-permute-start | bytes 1572872 | tf_op jit(solution)/shard_map/ppermute | solution.py:364
  4.8 1.5 %collective-permute-done.8 = bf16[512,512]{1,0:T(8,128)(2,1)S(1)} collective-permute-done((bf16[512,512]{1,0:T(8,128)(2,1)S(1)}, bf16[512,512]{1,0:T(8,128)(2,1)S(1)}, u32[]{:S(2)}, u32[]{:S(2)}) %collective-permute-start.8) | collective-permute-done | bytes 524320 | tf_op jit(solution)/shard_map/ppermute | solution.py:364
  7.7 5.5 %collective-permute-start = (bf16[512,256]{1,0:T(8,128)(2,1)S(1)}, bf16[512,256]{1,0:T(8,128)(2,1)S(1)}, u32[]{:S(2)}, u32[]{:S(2)}) collective-permute-start(bf16[512,256]{1,0:T(8,128)(2,1)S(1)} %get-tuple-element.26.refs_0_.refs_4_), channel_id=1, source_target_pairs={{0,8},{4,60},{8,16},{12,4},{16,24},{20,12},{24,32},{28,20},{32,40}... | collective-permute-start | bytes 786440 | tf_op jit(solution)/shard_map/ppermute | solution.py:355
  13.9 2.0 %collective-permute-done.2.refs_4_.refs_5_.refs_8_.refs_9_ = bf16[1024,256]{1,0:T(8,128)(2,1)S(1)} collective-permute-done((bf16[1024,256]{1,0:T(8,128)(2,1)S(1)}, bf16[1024,256]{1,0:T(8,128)(2,1)S(1)}, u32[]{:S(2)}, u32[]{:S(2)}) %collective-permute-start.2) | collective-permute-done | bytes 524320 | tf_op jit(solution)/shard_map/ppermute | solution.py:355
  15.8 2.3 %collective-permute-done.refs_2_.refs_6_ = bf16[512,256]{1,0:T(8,128)(2,1)S(1)} collective-permute-done((bf16[512,256]{1,0:T(8,128)(2,1)S(1)}, bf16[512,256]{1,0:T(8,128)(2,1)S(1)}, u32[]{:S(2)}, u32[]{:S(2)}) %collective-permute-start) | collective-permute-done | bytes 262176 | tf_op jit(solution)/shard_map/ppermute | solution.py:355
  18.2 3.4 %collective-permute-start.3 = (bf16[512,256]{1,0:T(8,128)(2,1)S(1)}, bf16[512,256]{1,0:T(8,128)(2,1)S(1)}, u32[]{:S(2)}, u32[]{:S(2)}) collective-permute-start(bf16[512,256]{1,0:T(8,128)(2,1)S(1)} %collective-permute-done.refs_2_.refs_6_), channel_id=1, source_target_pairs={{0,8},{4,60},{8,16},{12,4},{16,24},{20,12},{24,32},{28,20},{32,40}... | collective-permute-start | bytes 786440 | tf_op jit(solution)/shard_map/ppermute | solution.py:355
  21.6 2.8 %collective-permute-start.4 = (bf16[512,256]{1,0:T(8,128)(2,1)S(1)}, bf16[512,256]{1,0:T(8,128)(2,1)S(1)}, u32[]{:S(2)}, u32[]{:S(2)}) collective-permute-start(bf16[512,256]{1,0:T(8,128)(2,1)S(1)} %collective-permute-done.1.refs_3_.refs_7_), channel_id=1, source_target_pairs={{0,8},{4,60},{8,16},{12,4},{16,24},{20,12},{24,32},{28,20},{32,40}... | collective-permute-start | bytes 786440 | tf_op jit(solution)/shard_map/ppermute | solution.py:355
  25.4 2.3 %collective-permute-done.3.refs_6_.refs_10_ = bf16[512,256]{1,0:T(8,128)(2,1)S(1)} collective-permute-done((bf16[512,256]{1,0:T(8,128)(2,1)S(1)}, bf16[512,256]{1,0:T(8,128)(2,1)S(1)}, u32[]{:S(2)}, u32[]{:S(2)}) %collective-permute-start.3) | collective-permute-done | bytes 262176 | tf_op jit(solution)/shard_map/ppermute | solution.py:355
  27.7 5.3 %collective-permute-done.4.refs_7_.refs_11_ = bf16[512,256]{1,0:T(8,128)(2,1)S(1)} collective-permute-done((bf16[512,256]{1,0:T(8,128)(2,1)S(1)}, bf16[512,256]{1,0:T(8,128)(2,1)S(1)}, u32[]{:S(2)}, u32[]{:S(2)}) %collective-permute-start.4) | collective-permute-done | bytes 262176 | tf_op jit(solution)/shard_map/ppermute | solution.py:355
  33.0 1.8 %collective-permute-start.11 = (bf16[1024,256]{1,0:T(8,128)(2,1)S(1)}, bf16[1024,256]{1,0:T(8,128)(2,1)S(1)}, u32[]{:S(2)}, u32[]{:S(2)}) collective-permute-start(bf16[1024,256]{1,0:T(8,128)(2,1)S(1)} %collective-permute-done.5.refs_8_.refs_9_.refs_12_.refs_13_), channel_id=1, source_target_pairs={{0,56},{4,12},{8,0},{12,20},{16,8},{20,28},{24,16},{28,36},{32,24}... | collective-permute-start | bytes 1572872 | tf_op jit(solution)/shard_map/ppermute | solution.py:355
  34.8 1.5 %collective-permute-start.6 = (bf16[512,256]{1,0:T(8,128)(2,1)S(1)}, bf16[512,256]{1,0:T(8,128)(2,1)S(1)}, u32[]{:S(2)}, u32[]{:S(2)}) collective-permute-start(bf16[512,256]{1,0:T(8,128)(2,1)S(1)} %collective-permute-done.3.refs_6_.refs_10_), channel_id=1, source_target_pairs={{0,8},{4,60},{8,16},{12,4},{16,24},{20,12},{24,32},{28,20},{32,40}... | collective-permute-start | bytes 786440 | tf_op jit(solution)/shard_map/ppermute | solution.py:355
  36.3 1.5 %collective-permute-start.7 = (bf16[512,256]{1,0:T(8,128)(2,1)S(1)}, bf16[512,256]{1,0:T(8,128)(2,1)S(1)}, u32[]{:S(2)}, u32[]{:S(2)}) collective-permute-start(bf16[512,256]{1,0:T(8,128)(2,1)S(1)} %collective-permute-done.4.refs_7_.refs_11_), channel_id=1, source_target_pairs={{0,8},{4,60},{8,16},{12,4},{16,24},{20,12},{24,32},{28,20},{32,40}... | collective-permute-start | bytes 786440 | tf_op jit(solution)/shard_map/ppermute | solution.py:355
  37.8 4.5 %collective-permute-done.6.refs_10_.refs_14_ = bf16[512,256]{1,0:T(8,128)(2,1)S(1)} collective-permute-done((bf16[512,256]{1,0:T(8,128)(2,1)S(1)}, bf16[512,256]{1,0:T(8,128)(2,1)S(1)}, u32[]{:S(2)}, u32[]{:S(2)}) %collective-permute-start.6) | collective-permute-done | bytes 262176 | tf_op jit(solution)/shard_map/ppermute | solution.py:355
  43.5 4.4 %collective-permute-done.7.refs_11_.refs_15_ = bf16[512,256]{1,0:T(8,128)(2,1)S(1)} collective-permute-done((bf16[512,256]{1,0:T(8,128)(2,1)S(1)}, bf16[512,256]{1,0:T(8,128)(2,1)S(1)}, u32[]{:S(2)}, u32[]{:S(2)}) %collective-permute-start.7) | collective-permute-done | bytes 262176 | tf_op jit(solution)/shard_map/ppermute | solution.py:355
  49.1 4.5 %early.1 = (f32[1024,512]{1,0:T(8,128)S(1)}, f32[1024,512]{1,0:T(8,128)S(1)}) custom-call(bf16[512,256]{1,0:T(8,128)(2,1)S(1)} %get-tuple-element.26.refs_0_.refs_4_, bf16[512,256]{1,0:T(8,128)(2,1)S(1)} %get-tuple-element.27.refs_1_.refs_5_, bf16[512,256]{1,0:T(8,128)(2,1)S(1)} %collective-permute-done.refs_2_.refs_6_, ...), custom_call_target="tpu_custom_call" | custom-call | tf_op jit(solution)/shard_map/early/pallas_call | solution.py:162
  56.1 2.0 %collective-permute-start.15 = (bf16[1024,256]{1,0:T(8,128)(2,1)S(1)}, bf16[1024,256]{1,0:T(8,128)(2,1)S(1)}, u32[]{:S(2)}, u32[]{:S(2)}) collective-permute-start(bf16[1024,256]{1,0:T(8,128)(2,1)S(1)} %others.3), channel_id=1, source_target_pairs={{0,4},{4,0},{8,12},{12,8},{16,20},{20,16},{24,28},{28,24},{32,36},... | collective-permute-start | bytes 1572872 | tf_op jit(solution)/shard_map/ppermute | solution.py:364
  58.2 1.4 %collective-permute-done.15.refs_0_ = bf16[1024,256]{1,0:T(8,128)(2,1)S(1)} collective-permute-done((bf16[1024,256]{1,0:T(8,128)(2,1)S(1)}, bf16[1024,256]{1,0:T(8,128)(2,1)S(1)}, u32[]{:S(2)}, u32[]{:S(2)}) %collective-permute-start.15) | collective-permute-done | bytes 524320 | tf_op jit(solution)/shard_map/ppermute | solution.py:364
  60.2 2.8 %collective-permute-start.19 = (bf16[512,128]{1,0:T(8,128)(2,1)S(1)}, bf16[512,128]{1,0:T(8,128)(2,1)S(1)}, u32[]{:S(2)}, u32[]{:S(2)}) collective-permute-start(bf16[512,128]{1,0:T(8,128)(2,1)S(1)} %get-tuple-element.43), channel_id=1, source_target_pairs={{0,2},{1,3},{2,0},{3,1},{4,6},{5,7},{6,4},{7,5},{8,10},{9,11},{10,... | collective-permute-start | bytes 393224 | tf_op jit(solution)/shard_map/ppermute | solution.py:360
  64.0 1.2 %collective-permute-start.17 = (bf16[512,128]{1,0:T(8,128)(2,1)S(1)}, bf16[512,128]{1,0:T(8,128)(2,1)S(1)}, u32[]{:S(2)}, u32[]{:S(2)}) collective-permute-start(bf16[512,128]{1,0:T(8,128)(2,1)S(1)} %get-tuple-element.41), channel_id=1, source_target_pairs={{0,1},{1,2},{2,3},{3,0},{4,5},{5,6},{6,7},{7,4},{8,9},{9,10},{10,1... | collective-permute-start | bytes 393224 | tf_op jit(solution)/shard_map/ppermute | solution.py:360
  65.2 1.2 %collective-permute-start.18 = (bf16[512,128]{1,0:T(8,128)(2,1)S(1)}, bf16[512,128]{1,0:T(8,128)(2,1)S(1)}, u32[]{:S(2)}, u32[]{:S(2)}) collective-permute-start(bf16[512,128]{1,0:T(8,128)(2,1)S(1)} %get-tuple-element.42), channel_id=1, source_target_pairs={{0,1},{1,2},{2,3},{3,0},{4,5},{5,6},{6,7},{7,4},{8,9},{9,10},{10,1... | collective-permute-start | bytes 393224 | tf_op jit(solution)/shard_map/ppermute | solution.py:360
  66.4 1.4 %collective-permute-start.21 = (bf16[512,128]{1,0:T(8,128)(2,1)S(1)}, bf16[512,128]{1,0:T(8,128)(2,1)S(1)}, u32[]{:S(2)}, u32[]{:S(2)}) collective-permute-start(bf16[512,128]{1,0:T(8,128)(2,1)S(1)} %get-tuple-element.45), channel_id=1, source_target_pairs={{0,3},{1,0},{2,1},{3,2},{4,7},{5,4},{6,5},{7,6},{8,11},{9,8},{10,9... | collective-permute-start | bytes 393224 | tf_op jit(solution)/shard_map/ppermute | solution.py:360
  69.6 3.2 %collective-permute-done.17.refs_2_ = bf16[512,128]{1,0:T(8,128)(2,1)S(1)} collective-permute-done((bf16[512,128]{1,0:T(8,128)(2,1)S(1)}, bf16[512,128]{1,0:T(8,128)(2,1)S(1)}, u32[]{:S(2)}, u32[]{:S(2)}) %collective-permute-start.17) | collective-permute-done | bytes 131104 | tf_op jit(solution)/shard_map/ppermute | solution.py:360
  72.8 2.8 %collective-permute-done.18.refs_3_ = bf16[512,128]{1,0:T(8,128)(2,1)S(1)} collective-permute-done((bf16[512,128]{1,0:T(8,128)(2,1)S(1)}, bf16[512,128]{1,0:T(8,128)(2,1)S(1)}, u32[]{:S(2)}, u32[]{:S(2)}) %collective-permute-start.18) | collective-permute-done | bytes 131104 | tf_op jit(solution)/shard_map/ppermute | solution.py:360
  (34 shorter events, 12.3 us)
Async XLA Ops:
  1.5 4.9 %collective-permute-start.8 = (bf16[512,512]{1,0:T(8,128)(2,1)S(1)}, bf16[512,512]{1,0:T(8,128)(2,1)S(1)}, u32[]{:S(2)}, u32[]{:S(2)}) collective-permute-start(bf16[512,512]{1,0:T(8,128)(2,1)S(1)} %get-tuple-element.30), channel_id=1, source_target_pairs={{0,4},{4,0},{8,12},{12,8},{16,20},{20,16},{24,28},{28,24},{32,36},... | collective-permute-start | bytes 1572872 | tf_op jit(solution)/shard_map/ppermute | solution.py:364
  4.8 11.0 %collective-permute-start.2 = (bf16[1024,256]{1,0:T(8,128)(2,1)S(1)}, bf16[1024,256]{1,0:T(8,128)(2,1)S(1)}, u32[]{:S(2)}, u32[]{:S(2)}) collective-permute-start(bf16[1024,256]{1,0:T(8,128)(2,1)S(1)} %get-tuple-element.28), channel_id=1, source_target_pairs={{0,56},{4,12},{8,0},{12,20},{16,8},{20,28},{24,16},{28,36},{32,24}... | collective-permute-start | bytes 1572872 | tf_op jit(solution)/shard_map/ppermute | solution.py:355
  6.5 26.5 %collective-permute-start.9 = (bf16[2,512,512]{2,1,0:T(8,128)(2,1)S(1)}, bf16[2,512,512]{2,1,0:T(8,128)(2,1)S(1)}, u32[]{:S(2)}, u32[]{:S(2)}) collective-permute-start(bf16[2,512,512]{2,1,0:T(8,128)(2,1)S(1)} %pad_maximum_fusion.refs_12_.refs_16_), channel_id=1, source_target_pairs={{0,64},{4,196},{8,72},{12,204},{16,80},{20,212},{24,88},{28,220},{... | collective-permute-start | bytes 3145736 | tf_op jit(solution)/shard_map/ppermute | solution.py:373
  7.7 10.5 %collective-permute-start = (bf16[512,256]{1,0:T(8,128)(2,1)S(1)}, bf16[512,256]{1,0:T(8,128)(2,1)S(1)}, u32[]{:S(2)}, u32[]{:S(2)}) collective-permute-start(bf16[512,256]{1,0:T(8,128)(2,1)S(1)} %get-tuple-element.26.refs_0_.refs_4_), channel_id=1, source_target_pairs={{0,8},{4,60},{8,16},{12,4},{16,24},{20,12},{24,32},{28,20},{32,40}... | collective-permute-start | bytes 786440 | tf_op jit(solution)/shard_map/ppermute | solution.py:355
  13.1 8.4 %collective-permute-start.1 = (bf16[512,256]{1,0:T(8,128)(2,1)S(1)}, bf16[512,256]{1,0:T(8,128)(2,1)S(1)}, u32[]{:S(2)}, u32[]{:S(2)}) collective-permute-start(bf16[512,256]{1,0:T(8,128)(2,1)S(1)} %get-tuple-element.27.refs_1_.refs_5_), channel_id=1, source_target_pairs={{0,8},{4,60},{8,16},{12,4},{16,24},{20,12},{24,32},{28,20},{32,40}... | collective-permute-start | bytes 786440 | tf_op jit(solution)/shard_map/ppermute | solution.py:355
  15.8 17.2 %collective-permute-start.5 = (bf16[1024,256]{1,0:T(8,128)(2,1)S(1)}, bf16[1024,256]{1,0:T(8,128)(2,1)S(1)}, u32[]{:S(2)}, u32[]{:S(2)}) collective-permute-start(bf16[1024,256]{1,0:T(8,128)(2,1)S(1)} %collective-permute-done.2.refs_4_.refs_5_.refs_8_.refs_9_), channel_id=1, source_target_pairs={{0,56},{4,12},{8,0},{12,20},{16,8},{20,28},{24,16},{28,36},{32,24}... | collective-permute-start | bytes 1572872 | tf_op jit(solution)/shard_map/ppermute | solution.py:355
  18.2 9.5 %collective-permute-start.3 = (bf16[512,256]{1,0:T(8,128)(2,1)S(1)}, bf16[512,256]{1,0:T(8,128)(2,1)S(1)}, u32[]{:S(2)}, u32[]{:S(2)}) collective-permute-start(bf16[512,256]{1,0:T(8,128)(2,1)S(1)} %collective-permute-done.refs_2_.refs_6_), channel_id=1, source_target_pairs={{0,8},{4,60},{8,16},{12,4},{16,24},{20,12},{24,32},{28,20},{32,40}... | collective-permute-start | bytes 786440 | tf_op jit(solution)/shard_map/ppermute | solution.py:355
  21.6 11.4 %collective-permute-start.4 = (bf16[512,256]{1,0:T(8,128)(2,1)S(1)}, bf16[512,256]{1,0:T(8,128)(2,1)S(1)}, u32[]{:S(2)}, u32[]{:S(2)}) collective-permute-start(bf16[512,256]{1,0:T(8,128)(2,1)S(1)} %collective-permute-done.1.refs_3_.refs_7_), channel_id=1, source_target_pairs={{0,8},{4,60},{8,16},{12,4},{16,24},{20,12},{24,32},{28,20},{32,40}... | collective-permute-start | bytes 786440 | tf_op jit(solution)/shard_map/ppermute | solution.py:355
  24.4 24.7 %collective-permute-start.10 = (bf16[2,512,512]{2,1,0:T(8,128)(2,1)S(1)}, bf16[2,512,512]{2,1,0:T(8,128)(2,1)S(1)}, u32[]{:S(2)}, u32[]{:S(2)}) collective-permute-start(bf16[2,512,512]{2,1,0:T(8,128)(2,1)S(1)} %pad_maximum_fusion.refs_12_.refs_16_), channel_id=1, source_target_pairs={{0,192},{4,68},{8,200},{12,76},{16,208},{20,84},{24,216},{28,92},{... | collective-permute-start | bytes 3145736 | tf_op jit(solution)/shard_map/ppermute | solution.py:373
  33.0 21.8 %collective-permute-start.14 = (bf16[2,512,512]{2,1,0:T(8,128)(2,1)S(1)}, bf16[2,512,512]{2,1,0:T(8,128)(2,1)S(1)}, u32[]{:S(2)}, u32[]{:S(2)}) collective-permute-start(bf16[2,512,512]{2,1,0:T(8,128)(2,1)S(1)} %collective-permute-done.9.refs_13_.refs_17_), channel_id=1, source_target_pairs={{0,64},{4,196},{8,72},{12,204},{16,80},{20,212},{24,88},{28,220},{... | collective-permute-start | bytes 3145736 | tf_op jit(solution)/shard_map/ppermute | solution.py:373
  33.0 20.6 %collective-permute-start.11 = (bf16[1024,256]{1,0:T(8,128)(2,1)S(1)}, bf16[1024,256]{1,0:T(8,128)(2,1)S(1)}, u32[]{:S(2)}, u32[]{:S(2)}) collective-permute-start(bf16[1024,256]{1,0:T(8,128)(2,1)S(1)} %collective-permute-done.5.refs_8_.refs_9_.refs_12_.refs_13_), channel_id=1, source_target_pairs={{0,56},{4,12},{8,0},{12,20},{16,8},{20,28},{24,16},{28,36},{32,24}... | collective-permute-start | bytes 1572872 | tf_op jit(solution)/shard_map/ppermute | solution.py:355
  34.8 7.5 %collective-permute-start.6 = (bf16[512,256]{1,0:T(8,128)(2,1)S(1)}, bf16[512,256]{1,0:T(8,128)(2,1)S(1)}, u32[]{:S(2)}, u32[]{:S(2)}) collective-permute-start(bf16[512,256]{1,0:T(8,128)(2,1)S(1)} %collective-permute-done.3.refs_6_.refs_10_), channel_id=1, source_target_pairs={{0,8},{4,60},{8,16},{12,4},{16,24},{20,12},{24,32},{28,20},{32,40}... | collective-permute-start | bytes 786440 | tf_op jit(solution)/shard_map/ppermute | solution.py:355
  36.3 11.6 %collective-permute-start.7 = (bf16[512,256]{1,0:T(8,128)(2,1)S(1)}, bf16[512,256]{1,0:T(8,128)(2,1)S(1)}, u32[]{:S(2)}, u32[]{:S(2)}) collective-permute-start(bf16[512,256]{1,0:T(8,128)(2,1)S(1)} %collective-permute-done.4.refs_7_.refs_11_), channel_id=1, source_target_pairs={{0,8},{4,60},{8,16},{12,4},{16,24},{20,12},{24,32},{28,20},{32,40}... | collective-permute-start | bytes 786440 | tf_op jit(solution)/shard_map/ppermute | solution.py:355
  42.3 12.5 %collective-permute-start.12 = (bf16[512,256]{1,0:T(8,128)(2,1)S(1)}, bf16[512,256]{1,0:T(8,128)(2,1)S(1)}, u32[]{:S(2)}, u32[]{:S(2)}) collective-permute-start(bf16[512,256]{1,0:T(8,128)(2,1)S(1)} %collective-permute-done.6.refs_10_.refs_14_), channel_id=1, source_target_pairs={{0,8},{4,60},{8,16},{12,4},{16,24},{20,12},{24,32},{28,20},{32,40}... | collective-permute-start | bytes 786440 | tf_op jit(solution)/shard_map/ppermute | solution.py:355
  47.9 6.9 %collective-permute-start.13 = (bf16[512,256]{1,0:T(8,128)(2,1)S(1)}, bf16[512,256]{1,0:T(8,128)(2,1)S(1)}, u32[]{:S(2)}, u32[]{:S(2)}) collective-permute-start(bf16[512,256]{1,0:T(8,128)(2,1)S(1)} %collective-permute-done.7.refs_11_.refs_15_), channel_id=1, source_target_pairs={{0,8},{4,60},{8,16},{12,4},{16,24},{20,12},{24,32},{28,20},{32,40}... | collective-permute-start | bytes 786440 | tf_op jit(solution)/shard_map/ppermute | solution.py:355
  56.1 3.6 %collective-permute-start.15 = (bf16[1024,256]{1,0:T(8,128)(2,1)S(1)}, bf16[1024,256]{1,0:T(8,128)(2,1)S(1)}, u32[]{:S(2)}, u32[]{:S(2)}) collective-permute-start(bf16[1024,256]{1,0:T(8,128)(2,1)S(1)} %others.3), channel_id=1, source_target_pairs={{0,4},{4,0},{8,12},{12,8},{16,20},{20,16},{24,28},{28,24},{32,36},... | collective-permute-start | bytes 1572872 | tf_op jit(solution)/shard_map/ppermute | solution.py:364
  58.1 5.2 %collective-permute-start.16 = (bf16[1024,256]{1,0:T(8,128)(2,1)S(1)}, bf16[1024,256]{1,0:T(8,128)(2,1)S(1)}, u32[]{:S(2)}, u32[]{:S(2)}) collective-permute-start(bf16[1024,256]{1,0:T(8,128)(2,1)S(1)} %others.2), channel_id=1, source_target_pairs={{0,4},{4,0},{8,12},{12,8},{16,20},{20,16},{24,28},{28,24},{32,36},... | collective-permute-start | bytes 1572872 | tf_op jit(solution)/shard_map/ppermute | solution.py:364
  60.2 7.6 %collective-permute-start.19 = (bf16[512,128]{1,0:T(8,128)(2,1)S(1)}, bf16[512,128]{1,0:T(8,128)(2,1)S(1)}, u32[]{:S(2)}, u32[]{:S(2)}) collective-permute-start(bf16[512,128]{1,0:T(8,128)(2,1)S(1)} %get-tuple-element.43), channel_id=1, source_target_pairs={{0,2},{1,3},{2,0},{3,1},{4,6},{5,7},{6,4},{7,5},{8,10},{9,11},{10,... | collective-permute-start | bytes 393224 | tf_op jit(solution)/shard_map/ppermute | solution.py:360
  63.1 6.6 %collective-permute-start.20 = (bf16[512,128]{1,0:T(8,128)(2,1)S(1)}, bf16[512,128]{1,0:T(8,128)(2,1)S(1)}, u32[]{:S(2)}, u32[]{:S(2)}) collective-permute-start(bf16[512,128]{1,0:T(8,128)(2,1)S(1)} %get-tuple-element.44), channel_id=1, source_target_pairs={{0,2},{1,3},{2,0},{3,1},{4,6},{5,7},{6,4},{7,5},{8,10},{9,11},{10,... | collective-permute-start | bytes 393224 | tf_op jit(solution)/shard_map/ppermute | solution.py:360
  64.0 8.9 %collective-permute-start.17 = (bf16[512,128]{1,0:T(8,128)(2,1)S(1)}, bf16[512,128]{1,0:T(8,128)(2,1)S(1)}, u32[]{:S(2)}, u32[]{:S(2)}) collective-permute-start(bf16[512,128]{1,0:T(8,128)(2,1)S(1)} %get-tuple-element.41), channel_id=1, source_target_pairs={{0,1},{1,2},{2,3},{3,0},{4,5},{5,6},{6,7},{7,4},{8,9},{9,10},{10,1... | collective-permute-start | bytes 393224 | tf_op jit(solution)/shard_map/ppermute | solution.py:360
  65.2 10.4 %collective-permute-start.18 = (bf16[512,128]{1,0:T(8,128)(2,1)S(1)}, bf16[512,128]{1,0:T(8,128)(2,1)S(1)}, u32[]{:S(2)}, u32[]{:S(2)}) collective-permute-start(bf16[512,128]{1,0:T(8,128)(2,1)S(1)} %get-tuple-element.42), channel_id=1, source_target_pairs={{0,1},{1,2},{2,3},{3,0},{4,5},{5,6},{6,7},{7,4},{8,9},{9,10},{10,1... | collective-permute-start | bytes 393224 | tf_op jit(solution)/shard_map/ppermute | solution.py:360
  66.4 9.2 %collective-permute-start.21 = (bf16[512,128]{1,0:T(8,128)(2,1)S(1)}, bf16[512,128]{1,0:T(8,128)(2,1)S(1)}, u32[]{:S(2)}, u32[]{:S(2)}) collective-permute-start(bf16[512,128]{1,0:T(8,128)(2,1)S(1)} %get-tuple-element.45), channel_id=1, source_target_pairs={{0,3},{1,0},{2,1},{3,2},{4,7},{5,4},{6,5},{7,6},{8,11},{9,8},{10,9... | collective-permute-start | bytes 393224 | tf_op jit(solution)/shard_map/ppermute | solution.py:360
  67.9 7.8 %copy-start = (s32[64,4]{0,1:T(4,128)S(1)}, s32[64,4]{0,1:T(4,128)}, u32[]{:S(2)}) copy-start(s32[64,4]{0,1:T(4,128)} %param.5) | copy-start | bytes 3076
  67.9 7.8 %collective-permute-start.22 = (bf16[512,128]{1,0:T(8,128)(2,1)S(1)}, bf16[512,128]{1,0:T(8,128)(2,1)S(1)}, u32[]{:S(2)}, u32[]{:S(2)}) collective-permute-start(bf16[512,128]{1,0:T(8,128)(2,1)S(1)} %get-tuple-element.46), channel_id=1, source_target_pairs={{0,3},{1,0},{2,1},{3,2},{4,7},{5,4},{6,5},{7,6},{8,11},{9,8},{10,9... | collective-permute-start | bytes 393224 | tf_op jit(solution)/shard_map/ppermute | solution.py:360
